TPU v7x, 512 devices: a whole 4x8x8 slice. The times are simulated.
512 devices in a mesh: expert: 32 (over z_lo, y), dp: 8 (over x, core), half: 2 (over z_hi).
Axes of the slice: x: 4, y: 8, z: 8 (z_hi: 2, z_lo: 4; z = z_hi * 4 + z_lo), core: 2. Of those that a mesh axis runs over, the one named last changes fastest.
Arguments:
- patches: bfloat16 [65536, 1664], P(('expert', 'dp', 'half')), may hold values from -6 to 6
- upstream: bfloat16 [65536, 1664], P(('expert', 'dp', 'half')), may hold values from -6 to 6
- gates: bfloat16 [65536, 2], P(('expert', 'dp', 'half')), may hold values from 0.099609375 to 0.59765625
- expert_ids: int32 [65536, 2], P(('expert', 'dp', 'half')), may hold values from 0 to 31, as said below
- slot_ids: int32 [65536, 2], P(('expert', 'dp', 'half')), may hold values from -1 to 1, as said below
- in_weights: bfloat16 [32, 3328, 1664], P('expert', ('dp', 'half')), may hold values from -0.15625 to 0.15625
- out_weights: bfloat16 [32, 3328, 1664], P('expert', ('dp', 'half')), may hold values from -0.109375 to 0.109375
Outputs:
- patch_grad: bfloat16 [65536, 1664], P(('expert', 'dp', 'half'))
- gate_grad: float32 [65536, 2], P(('expert', 'dp', 'half'))
- in_weight_grad: bfloat16 [32, 3328, 1664], P('expert', ('dp', 'half'))
- out_weight_grad: bfloat16 [32, 3328, 1664], P('expert', ('dp', 'half'))
Inputs may be any that keep to these rules, and one draw needn't show every extreme that they name: `expert_ids`: the two experts of a patch differ; within the 128 patches of one device every expert is named 2 or more times. `slot_ids`: -1 marks a dropped assignment. Within the patches of one device, each expert's slots 0 to 1 are each held by exactly one assignment naming that expert.
All inputs are finite; a program needn't handle non-finite values.
Results may differ from a plain program's by a relative error of at most 0.024.
Values may be sent and summed in bfloat16 or wider, within the bound.
No kernel may reach another device: no remote copies, remote signals or barrier semaphores. Data moves between devices by JAX's collectives and lax.ppermute only.
A program may use at most 64 MiB of HBM per device.

v0:
```python
import jax
import jax.numpy as jnp
from jax import lax
from jax.sharding import PartitionSpec as P

CAP = 2


ROOT_TERM = 0.7978845608028654
CUBIC_TERM = 0.044715


def gelu_tanh(value):
    inner = ROOT_TERM * (value + CUBIC_TERM * value * value * value)
    return 0.5 * value * (1.0 + jnp.tanh(inner))


def gelu_slope(value):
    inner = ROOT_TERM * (value + CUBIC_TERM * value * value * value)
    tangent = jnp.tanh(inner)
    return 0.5 * (1.0 + tangent) + 0.5 * value * (1.0 - tangent * tangent) * ROOT_TERM * (
        1.0 + 3.0 * CUBIC_TERM * value * value
    )


def contract_rows(left, right):
    return lax.dot_general(
        left, right, (((0,), (0,)), ((), ())), preferred_element_type=jnp.float32
    )


def contract_width(left, right):
    return lax.dot_general(
        left, right, (((1,), (1,)), ((), ())), preferred_element_type=jnp.float32
    )


def local_backward(rows_in, rows_up, rows_gate, weight_in, weight_out, groups):
    count = rows_in.shape[0]
    span = weight_in.shape[0] // groups
    preact = contract_width(rows_in, weight_in)
    hidden_act = gelu_tanh(preact)
    hidden_bf = hidden_act.astype(jnp.bfloat16)
    back_proj = contract_width(rows_up, weight_out)
    gate_part = jnp.sum((hidden_act * back_proj).reshape(count, groups, span), axis=2).astype(
        jnp.bfloat16
    )
    scale = rows_gate.astype(jnp.float32)[:, None]
    preact_grad = (scale * back_proj * gelu_slope(preact)).astype(jnp.bfloat16)
    scaled_up = (scale * rows_up.astype(jnp.float32)).astype(jnp.bfloat16)
    grad_out = contract_rows(hidden_bf, scaled_up)
    grad_in = contract_rows(preact_grad, rows_in)
    input_parts = [
        jnp.dot(preact_grad, weight_in, preferred_element_type=jnp.float32).astype(jnp.bfloat16)
    ]
    return (gate_part, input_parts, grad_in, grad_out)


def local(patches, upstream, gates, expert_ids, slot_ids, in_weights, out_weights):
    experts_here = lax.axis_size("expert")
    width = experts_here * CAP
    feature = patches.shape[1]
    target = jnp.where(slot_ids >= 0, expert_ids * CAP + slot_ids, -1)
    match = target[:, :, None] == jnp.arange(width, dtype=jnp.int32)
    table = jnp.any(match, axis=1).astype(jnp.bfloat16)
    patch_slots = (
        contract_rows(table, patches).astype(jnp.bfloat16).reshape(experts_here, CAP, feature)
    )
    up_slots = (
        contract_rows(table, upstream).astype(jnp.bfloat16).reshape(experts_here, CAP, feature)
    )
    gate_slots = jnp.sum(jnp.where(match, gates.astype(jnp.float32)[:, :, None], 0.0), axis=(0, 1))
    gate_slots = gate_slots.astype(jnp.bfloat16).reshape(experts_here, CAP)
    arrived = (
        lax.all_to_all(patch_slots, "expert", split_axis=0, concat_axis=0, tiled=True),
        lax.all_to_all(up_slots, "expert", split_axis=0, concat_axis=0, tiled=True),
        lax.all_to_all(gate_slots, "expert", split_axis=0, concat_axis=0, tiled=True),
    )
    gathered = (
        lax.all_gather(arrived[0], ("dp", "half"), axis=0, tiled=True),
        lax.all_gather(arrived[1], ("dp", "half"), axis=0, tiled=True),
        lax.all_gather(arrived[2], ("dp", "half"), axis=0, tiled=True),
    )
    rows_in = gathered[0].reshape(-1, feature)
    rows_up = gathered[1].reshape(-1, feature)
    rows_gate = gathered[2].reshape(-1)
    gate_part, input_parts, grad_in, grad_out = local_backward(
        rows_in, rows_up, rows_gate, in_weights[0], out_weights[0], 1
    )
    summed = (
        lax.psum_scatter(
            input_parts[0].reshape(-1, CAP, feature),
            ("dp", "half"),
            scatter_dimension=0,
            tiled=True,
        ).astype(jnp.float32),
        lax.psum_scatter(
            gate_part.reshape(-1, CAP), ("dp", "half"), scatter_dimension=0, tiled=True
        ).astype(jnp.float32),
    )
    in_grad = grad_in.astype(jnp.bfloat16)
    out_grad = grad_out.astype(jnp.bfloat16)
    patch_back = summed[0].astype(jnp.bfloat16)
    gate_back = summed[1].astype(jnp.bfloat16)
    returned = (
        lax.all_to_all(patch_back, "expert", split_axis=0, concat_axis=0, tiled=True),
        lax.all_to_all(gate_back, "expert", split_axis=0, concat_axis=0, tiled=True),
    )
    patch_grad = jnp.dot(
        table, returned[0].reshape(width, feature), preferred_element_type=jnp.float32
    )
    gate_values = returned[1].reshape(width).astype(jnp.float32)
    gate_grad = jnp.sum(jnp.where(match, gate_values[None, None, :], 0.0), axis=2)
    return (patch_grad.astype(jnp.bfloat16), gate_grad, in_grad[None], out_grad[None])


def solution(mesh):
    in_specs = (
        P(("expert", "dp", "half"), None),
        P(("expert", "dp", "half"), None),
        P(("expert", "dp", "half"), None),
        P(("expert", "dp", "half"), None),
        P(("expert", "dp", "half"), None),
        P("expert", ("dp", "half"), None),
        P("expert", ("dp", "half"), None),
    )
    out_specs = (
        P(("expert", "dp", "half"), None),
        P(("expert", "dp", "half"), None),
        P("expert", ("dp", "half"), None),
        P("expert", ("dp", "half"), None),
    )
    return jax.shard_map(local, mesh=mesh, in_specs=in_specs, out_specs=out_specs, check_vma=False)
```

profile of v0, /device:TPU:6, one launch (start us, length us, event | category | flops | bytes accessed | tf_op | source)
XLA Modules:
  0.0 716.5 jit_solution(14628783991758616351)
XLA Ops:
  7.2 0.0 copy-start
  7.2 0.0 all-gather.6.cloned.1.call-start
  7.2 0.8 compare_select_fusion
  8.0 1.2 convolution_convert_fusion.3
  9.2 0.1 reshape.72
  9.3 24.6 %all_to_all.33 = bf16[32,2,1664]{2,1,0:T(2,128)(2,1)} all-to-all(bf16[32,2,1664]{2,1,0:T(2,128)(2,1)S(1)} %reshape.72), channel_id=1, replica_groups=mesh['expert'=32,'dp'=8,'half'=2] {'expert'}, dimensions={0} | all-to-all | bytes 425984 | tf_op jit(solution)/shard_map/all_to_all | solution.py:75
  33.9 0.0 all-gather.6.cloned.1.call-update
  33.9 0.0 all-gather.4.cloned.1.call-start
  33.9 1.2 convolution_convert_fusion.4
  35.2 0.1 reshape.70
  35.3 15.6 %all_to_all.34 = bf16[32,2,1664]{2,1,0:T(2,128)(2,1)} all-to-all(bf16[32,2,1664]{2,1,0:T(2,128)(2,1)S(1)} %reshape.70), channel_id=1, replica_groups=mesh['expert'=32,'dp'=8,'half'=2] {'expert'}, dimensions={0} | all-to-all | bytes 425984 | tf_op jit(solution)/shard_map/all_to_all | solution.py:76
  50.8 0.0 all-gather.4.cloned.1.call-update
  50.8 0.0 reduce-scatter.2.cloned.1.call-start
  50.9 58.9 %all-gather.6.cloned.1.call-done = bf16[512,2,1664]{2,1,0:T(2,128)(2,1)} async-done(((bf16[32,2,1664]{2,1,0:T(2,128)(2,1)}), bf16[512,2,1664]{2,1,0:T(2,128)(2,1)}) %all-gather.6.cloned.1.call-update) | async-done | bytes 3407888 | tf_op jit(solution)/shard_map/all_gather | solution.py:80
  109.8 8.1 %reshape.73 = bf16[1024,1664]{1,0:T(8,128)(2,1)} reshape(bf16[512,2,1664]{2,1,0:T(2,128)(2,1)} %all-gather.6.cloned.1.call-done) | data formatting | bytes 6815744 | tf_op jit(solution)/shard_map/reshape | solution.py:84
  117.9 3.2 fusion.13
  121.1 0.0 copy-start.2
  121.1 65.7 %all-gather.4.cloned.1.call-done = bf16[512,2,1664]{2,1,0:T(2,128)(2,1)} async-done(((bf16[32,2,1664]{2,1,0:T(2,128)(2,1)}), bf16[512,2,1664]{2,1,0:T(2,128)(2,1)}) %all-gather.4.cloned.1.call-update) | async-done | bytes 3407888 | tf_op jit(solution)/shard_map/all_gather | solution.py:81
  186.8 8.1 %reshape.71 = bf16[1024,1664]{1,0:T(8,128)(2,1)} reshape(bf16[512,2,1664]{2,1,0:T(2,128)(2,1)} %all-gather.4.cloned.1.call-done) | data formatting | bytes 6815744 | tf_op jit(solution)/shard_map/reshape | solution.py:85
  194.9 3.3 multiply_reduce_fusion
  198.2 0.9 convert_element_type.92
  199.1 0.0 reduce-scatter.2.cloned.1.call-update
  199.1 79.6 %reduce-scatter.2.cloned.1.call-done = bf16[32,2]{1,0:T(8,128)(2,1)} async-done(((bf16[512,2]{1,0:T(8,128)(2,1)}), bf16[32,2]{1,0:T(8,128)(2,1)}) %reduce-scatter.2.cloned.1.call-update) | async-done | bytes 144 | tf_op jit(solution)/shard_map/reduce_scatter | solution.py:97
  278.7 1.3 copy.30
  280.0 7.7 %all-to-all-start.4 = ((bf16[32,1,2]{2,1,0:T(2,128)(2,1)}), bf16[32,1,2]{2,1,0:T(2,128)(2,1)S(1)}, u32[]{:S(2)}, u32[]{:S(2)}) async-start(bf16[32,1,2]{2,1,0:T(2,128)(2,1)} %copy.30), calls=%async_computation.5 | async-start | bytes 32768 | tf_op jit(solution)/shard_map/all_to_all | solution.py:107
  287.7 0.0 all-reduce.3.cloned.1.call-start
  287.8 10.0 %all-to-all-done.4 = bf16[32,1,2]{2,1,0:T(2,128)(2,1)S(1)} async-done(((bf16[32,1,2]{2,1,0:T(2,128)(2,1)}), bf16[32,1,2]{2,1,0:T(2,128)(2,1)S(1)}, u32[]{:S(2)}, u32[]{:S(2)}) %all-to-all-start.4) | async-done | bytes 160 | tf_op jit(solution)/shard_map/all_to_all | solution.py:107
  297.7 0.1 convert_reduce_fusion.1
  297.8 0.1 reshape.77
  297.9 0.7 select_reduce_fusion
  298.6 0.1 convert_element_type.103
  298.7 13.1 %all_to_all.35 = bf16[32,1,2]{2,1,0:T(2,128)(2,1)S(1)} all-to-all(bf16[32,1,2]{2,1,0:T(2,128)(2,1)S(1)} %convert_element_type.103), channel_id=1, replica_groups=mesh['expert'=32,'dp'=8,'half'=2] {'expert'}, dimensions={0} | all-to-all | bytes 256 | tf_op jit(solution)/shard_map/all_to_all | solution.py:77
  311.8 42.9 %all-gather = bf16[512,1,2]{2,1,0:T(2,128)(2,1)S(1)} all-gather(bf16[32,1,2]{2,1,0:T(2,128)(2,1)S(1)} %all_to_all.35), channel_id=2, replica_groups=mesh['expert'=32,'dp'=8,'half'=2] {'dp','half'}, dimensions={0}, use_global_device_ids=true | all-gather | bytes 2176 | tf_op jit(solution)/shard_map/all_gather | solution.py:82
  354.6 0.8 convert_reduce_fusion
  355.4 0.2 reshape.76
  355.6 0.6 fusion.11
  356.2 3.0 convolution_convert_fusion
  359.2 7.9 %reshape.74 = bf16[512,2,1664]{2,1,0:T(2,128)(2,1)} reshape(bf16[1024,1664]{1,0:T(8,128)(2,1)} %convolution_convert_fusion) | data formatting | bytes 6815744 | tf_op jit(solution)/shard_map/reshape | solution.py:92
  367.0 0.0 all-reduce.3.cloned.1.call-update
  367.1 1.3 dynamic-slice
  369.0 319.6 %all-reduce.3.cloned.1.call-done = bf16[512,2,1664]{2,1,0:T(2,128)(2,1)} async-done(((bf16[512,2,1664]{2,1,0:T(2,128)(2,1)}), bf16[512,2,1664]{2,1,0:T(2,128)(2,1)}) %all-reduce.3.cloned.1.call-update) | async-done | bytes 3407888
  688.6 1.8 constant_dynamic-slice_fusion
  690.4 6.9 all-to-all-start.3
  697.3 3.9 fusion.4
  701.2 2.2 fusion.3
  703.4 5.4 all-to-all-done.3
  708.8 0.1 reshape.75
  708.9 1.1 convolution_convert_fusion.2
  (8 shorter events, 0.0 us)
Async XLA Ops:
  7.2 110.7 %copy-start = (bf16[1,208,1664]{2,1,0:T(8,128)(2,1)S(1)}, bf16[1,208,1664]{2,1,0:T(8,128)(2,1)}, u32[]{:S(2)}) copy-start(bf16[1,208,1664]{2,1,0:T(8,128)(2,1)} %param.12) | copy-start | bytes 2076676
  7.2 102.6 %all-gather.6.cloned.1.call-start = ((), (), s32[]{:S(2)}) async-start(), calls=%async_computation.7 | async-start | bytes 3620864 | tf_op jit(solution)/shard_map/all_gather | solution.py:80
  33.9 152.9 %all-gather.4.cloned.1.call-start = ((), (), s32[]{:S(2)}) async-start(), calls=%async_computation.6 | async-start | bytes 3620864 | tf_op jit(solution)/shard_map/all_gather | solution.py:81
  50.8 227.9 %reduce-scatter.2.cloned.1.call-start = ((), (), s32[]{:S(2)}) async-start(), calls=%async_computation.8 | async-start | bytes 139264 | tf_op jit(solution)/shard_map/reduce_scatter | solution.py:97
  121.1 73.8 %copy-start.2 = (bf16[1,208,1664]{2,1,0:T(8,128)(2,1)S(1)}, bf16[1,208,1664]{2,1,0:T(8,128)(2,1)}, u32[]{:S(2)}) copy-start(bf16[1,208,1664]{2,1,0:T(8,128)(2,1)} %param.13) | copy-start | bytes 2076676
  194.9 92.9 %copy-start.3 = (bf16[128,2]{0,1:T(2,128)(2,1)S(1)}, bf16[128,2]{0,1:T(2,128)(2,1)}, u32[]{:S(2)}) copy-start(bf16[128,2]{0,1:T(2,128)(2,1)} %param.9) | copy-start | bytes 1540
  280.0 17.7 %all-to-all-start.4 = ((bf16[32,1,2]{2,1,0:T(2,128)(2,1)}), bf16[32,1,2]{2,1,0:T(2,128)(2,1)S(1)}, u32[]{:S(2)}, u32[]{:S(2)}) async-start(bf16[32,1,2]{2,1,0:T(2,128)(2,1)} %copy.30), calls=%async_computation.5 | async-start | bytes 32768 | tf_op jit(solution)/shard_map/all_to_all | solution.py:107
  287.7 400.9 %all-reduce.3.cloned.1.call-start = ((), (), s32[]{:S(2)}) async-start(), calls=%async_computation.9 | async-start | bytes 6815744
  690.4 18.5 %all-to-all-start.3 = ((bf16[32,2,1664]{2,1,0:T(2,128)(2,1)}), bf16[32,2,1664]{2,1,0:T(2,128)(2,1)S(1)}, u32[]{:S(2)}, u32[]{:S(2)}) async-start(bf16[32,2,1664]{2,1,0:T(2,128)(2,1)} %constant_dynamic-slice_fusion), calls=%async_computation.3 | async-start | bytes 425984 | tf_op jit(solution)/shard_map/all_to_all | solution.py:106
  697.3 3.9 copy-start.1
Sparse Core Ops, SparseCore 0:
  34.0 75.7 all-gather.5
  113.1 73.6 all-gather.3
  199.2 79.4 reduce-scatter.1
  367.2 321.3 all-reduce.2
where the time goes:
time: 720 us; the launch traced here: 717 us
  waiting for transfers between devices  539 us (75%)
  blocking collectives  96.1 us (13%)
  local copies, waits for them, and re-layouts  30 us (4%)
  matrix products  19 us (3%)
  starting transfers between devices  14.8 us (2%)
  between operations  14.6 us (2%)
    unnamed x5, waiting for transfers between devices  320 us
    reduce_scatter x1, waiting for transfers between devices, local(): lax.psum_scatter(gate_part.reshape(-1, CAP), ('dp', 'half'), scatter_dime...  79.6 us
    all_gather x1, waiting for transfers between devices, local(): lax.all_gather(arrived[1], ('dp', 'half'), axis=0, tiled=True)  65.7 us
    all_gather x1, waiting for transfers between devices, local(): lax.all_gather(arrived[0], ('dp', 'half'), axis=0, tiled=True)  58.9 us
    all_gather x1, blocking collectives, local(): lax.all_gather(arrived[2], ('dp', 'half'), axis=0, tiled=True)  42.9 us
    all_to_all x1, blocking collectives, local(): lax.all_to_all(patch_slots, 'expert', split_axis=0, concat_axis=0, tiled=...  24.6 us
    all_to_all x1, blocking collectives, local(): lax.all_to_all(up_slots, 'expert', split_axis=0, concat_axis=0, tiled=True)  15.6 us
  transfers between devices with their start and end apart: 6, of which 6 were waited for; matrix products, arithmetic and copies ran while one was open for 3% of the time, Pallas kernels for 0%

commit v1 on v0

v1 whole, which is shorter than its diff:
```python
import jax
import jax.numpy as jnp
from jax import lax
from jax.experimental import pallas as pl
from jax.experimental.pallas import tpu as pltpu
from jax.sharding import Mesh, PartitionSpec as P

F32 = jnp.float32
BF16 = jnp.bfloat16
I32 = jnp.int32

CAP = 2
ROOT_TERM = 0.7978845608028654
CUBIC_TERM = 0.044715

T = 128
D = 1664
HS = 208
X = 4
SRC = 64
ROWS = SRC * CAP
SEND = SRC * 8
HALF_W = 896
QW = 512
GW = D + 128
VMEM_LIMIT = 56 * 1024 * 1024


def params():
    return pltpu.CompilerParams(vmem_limit_bytes=VMEM_LIMIT)


def dot(left, right):
    return jnp.dot(left, right, preferred_element_type=F32)


def dot_rows(left, right):
    return lax.dot_general(left, right, (((0,), (0,)), ((), ())), preferred_element_type=F32)


def dot_width(left, right):
    return lax.dot_general(left, right, (((1,), (1,)), ((), ())), preferred_element_type=F32)


def slot_match(ids, slots):
    target = jnp.where(slots >= 0, ids * CAP + slots, -1)
    row = lax.broadcasted_iota(I32, (T, SEND), 1)
    slot = (row >> 4) * CAP + (row & 1)
    return target[:, 0:1] == slot, target[:, 1:2] == slot, row


def pack_rows_kernel(patches, upstream, gates, ids, slots, out):
    m0, m1, row = slot_match(ids[...], slots[...])
    g = gates[...].astype(F32)
    hit = jnp.where(m0 | m1, 1.0, 0.0)
    gate = jnp.where(m0, g[:, 0:1], 0.0) + jnp.where(m1, g[:, 1:2], 0.0)
    is_up = (row & 2) != 0
    right = (row & 4) != 0
    p_sel = jnp.where(is_up, 0.0, hit)
    u_sel = jnp.where(is_up, gate, 0.0)
    p_l = jnp.where(right, 0.0, p_sel).astype(BF16)
    p_r = jnp.where(right, p_sel, 0.0).astype(BF16)
    u_l = jnp.where(right, 0.0, u_sel).astype(BF16)
    u_r = jnp.where(right, u_sel, 0.0).astype(BF16)
    rest = D - HALF_W
    out[:, :rest] = (
        dot_rows(p_l, patches[:, :rest])
        + dot_rows(u_l, upstream[:, :rest])
        + dot_rows(p_r, patches[:, HALF_W:])
        + dot_rows(u_r, upstream[:, HALF_W:])
    ).astype(BF16)
    out[:, rest:] = (
        dot_rows(p_l, patches[:, rest:HALF_W]) + dot_rows(u_l, upstream[:, rest:HALF_W])
    ).astype(BF16)


def unpack_rows_kernel(got, out):
    part = 256
    o = lax.broadcasted_iota(I32, (128, part), 0)
    c = lax.broadcasted_iota(I32, (128, part), 1)
    want = ((o & 63) >> 1) * 8 + (o >> 6) * 2 + (o & 1)
    for g in range(SEND // part):
        block = got[pl.ds(g * part, part), :]
        for h in range(2):
            sel = jnp.where(c == want + 4 * h, 1.0, 0.0).astype(BF16)
            wide = HALF_W if h == 0 else D - HALF_W
            rows = dot(sel, block[:, :wide]).astype(BF16)
            out[pl.ds(g * 64, 64), pl.ds(h * HALF_W, wide)] = rows[:64]
            out[pl.ds(ROWS + g * 64, 64), pl.ds(h * HALF_W, wide)] = rows[64:]


def gelu_and_slope(value):
    square = value * value
    tangent = jnp.tanh(ROOT_TERM * value * (1.0 + CUBIC_TERM * square))
    up = 0.5 * (1.0 + tangent)
    slope = up + 0.5 * value * (1.0 - tangent * tangent) * ROOT_TERM * (1.0 + 3.0 * CUBIC_TERM * square)
    return value * up, slope


def load_rows(sources, p_all, u_all, sems):
    copies = []
    for b, source in enumerate(sources):
        for k, place in enumerate((p_all, u_all)):
            copy = pltpu.make_async_copy(
                source.at[pl.ds(k * ROWS, ROWS), :], place.at[pl.ds(b * ROWS, ROWS), :], sems.at[k, b]
            )
            copy.start()
            copies.append(copy)
    for copy in copies:
        copy.wait()


def expert_kernel(r0, r1, r2, r3, wi0, wi1, wo0, wo1, i0, i1, i2, i3, pg_out, hid_out, p_all, u_all, sems):
    load_rows((r0, r1, r2, r3), p_all, u_all, sems)
    gate = jnp.zeros((X * ROWS, 1), F32)
    grads = []
    for c, (wi, wo) in enumerate(((wi0, wo0), (wi1, wo1))):
        pre = dot_width(p_all[...], wi[...])
        back = dot_width(u_all[...], wo[...])
        hid, slope = gelu_and_slope(pre)
        gate += jnp.sum(hid * back, axis=1, keepdims=True)
        pg = (back * slope).astype(BF16)
        pg_out[c] = pg
        hid_out[c] = hid.astype(BF16)
        grads.append(pg)
    lane = lax.broadcasted_iota(I32, (ROWS, 128), 1)
    for b, out in enumerate((i0, i1, i2, i3)):
        rows = slice(b * ROWS, (b + 1) * ROWS)
        out[:, :D] = (dot(grads[0][rows], wi0[...]) + dot(grads[1][rows], wi1[...])).astype(BF16)
        out[:, D:] = jnp.where(lane == 0, gate[rows], 0.0).astype(BF16)


def weight_kernel(r0, r1, r2, r3, pg, hid, own_in, own_out, other, p_all, u_all, sems):
    load_rows((r0, r1, r2, r3), p_all, u_all, sems)
    own_in[...] = dot_rows(pg[0], p_all[...])
    own_out[...] = dot_rows(hid[0], u_all[...])
    other[pl.ds(0, HS), :] = dot_rows(pg[1], p_all[...]).astype(BF16)
    other[pl.ds(HS, HS), :] = dot_rows(hid[1], u_all[...]).astype(BF16)


def weight_sum_kernel(own_in, own_out, got, grad_in, grad_out):
    grad_in[...] = (own_in[...] + got[pl.ds(0, HS), :].astype(F32)).astype(BF16)
    grad_out[...] = (own_out[...] + got[pl.ds(HS, HS), :].astype(F32)).astype(BF16)


def pack_back_kernel(i0, i1, i2, i3, out):
    total = (
        (i0[...].astype(F32) + i1[...].astype(F32)) + (i2[...].astype(F32) + i3[...].astype(F32))
    ).astype(BF16)
    row = lax.broadcasted_iota(I32, (SEND, ROWS), 0)
    col = lax.broadcasted_iota(I32, (SEND, ROWS), 1)
    want = (row >> 3) * 2 + (row & 1)
    quarter = (row >> 1) & 3
    sels = [jnp.where((col == want) & (quarter == q), 1.0, 0.0).astype(BF16) for q in range(4)]
    last = GW - 3 * QW
    narrow = sum(dot(sels[q], total[:, q * QW : q * QW + last]) for q in range(4))
    wide = sum(dot(sels[q], total[:, q * QW + last : (q + 1) * QW]) for q in range(3))
    out[:, :last] = narrow.astype(BF16)
    out[:, last:] = wide.astype(BF16)


def unpack_back_kernel(got, gates, ids, slots, patch_grad, gate_grad):
    m0, m1, row = slot_match(ids[...], slots[...])
    quarter = (row >> 1) & 3
    hit = jnp.where(m0 | m1, 1.0, 0.0)
    for q in range(4):
        wide = QW if q < 3 else D - 3 * QW
        sel = jnp.where(quarter == q, hit, 0.0).astype(BF16)
        patch_grad[:, pl.ds(q * QW, wide)] = dot(sel, got[:, :wide]).astype(BF16)
    gate_block = got[:, D - 3 * QW : GW - 3 * QW]
    g = gates[...].astype(F32)
    for k, m in enumerate((m0, m1)):
        sel = jnp.where((quarter == 3) & m, 1.0, 0.0).astype(BF16)
        gate_grad[:, k : k + 1] = dot(sel, gate_block)[:, 0:1] / g[:, k : k + 1]


def shape(dims, kind=BF16):
    return jax.ShapeDtypeStruct(dims, kind)


ANY = pl.BlockSpec(memory_space=pl.ANY)
VM = pl.BlockSpec(memory_space=pltpu.VMEM)


def call(kernel, out_shape, args, flops, moved, in_specs=None, scratch=()):
    return pl.pallas_call(
        kernel,
        out_shape=out_shape,
        in_specs=in_specs or [VM] * len(args),
        out_specs=jax.tree.map(lambda _: VM, out_shape),
        scratch_shapes=scratch,
        compiler_params=params(),
        cost_estimate=pl.CostEstimate(flops=flops, bytes_accessed=moved, transcendentals=0),
    )(*args)


def shift(value, axis, by):
    size = lax.axis_size(axis)
    return lax.ppermute(value, axis, [(i, (i + by) % size) for i in range(size)])


def local(patches, upstream, gates, ids, slots, in_weights, out_weights):
    everywhere = ("zlo", "y", "zhi")
    wi, wo = in_weights[0], out_weights[0]
    sent = call(
        pack_rows_kernel, shape((SEND, HALF_W)), (patches, upstream, gates, ids, slots), 500_000_000, 2_000_000
    )
    got = lax.all_to_all(sent, everywhere, split_axis=0, concat_axis=0, tiled=True)
    own = call(unpack_rows_kernel, shape((2 * ROWS, D)), (got,), 300_000_000, 2_000_000)
    blocks = [own] + [shift(own, "x", by) for by in (1, 2, 3)]
    wi1, wo1 = shift(wi, "core", 1), shift(wo, "core", 1)
    scratch = (
        pltpu.VMEM((X * ROWS, D), BF16),
        pltpu.VMEM((X * ROWS, D), BF16),
        pltpu.SemaphoreType.DMA((2, X)),
    )
    hidden = shape((2, X * ROWS, HS))
    *parts, pg, hid = call(
        expert_kernel,
        [shape((ROWS, GW))] * X + [hidden, hidden],
        (*blocks, wi, wi1, wo, wo1),
        2_200_000_000,
        9_000_000,
        in_specs=[ANY] * X + [VM] * 4,
        scratch=scratch,
    )
    returned = [parts[0]] + [shift(parts[by], "x", X - by) for by in (1, 2, 3)]
    own_in, own_out, other = call(
        weight_kernel,
        [shape((HS, D), F32), shape((HS, D), F32), shape((2 * HS, D))],
        (*blocks, pg, hid),
        1_400_000_000,
        9_000_000,
        in_specs=[ANY] * X + [VM] * 2,
        scratch=scratch,
    )
    other = shift(other, "core", 1)
    grad_in, grad_out = call(
        weight_sum_kernel, [shape((HS, D)), shape((HS, D))], (own_in, own_out, other), 1_000_000, 6_000_000
    )
    back = call(pack_back_kernel, shape((SEND, QW)), returned, 300_000_000, 2_500_000)
    back = lax.all_to_all(back, everywhere, split_axis=0, concat_axis=0, tiled=True)
    patch_grad, gate_grad = call(
        unpack_back_kernel,
        [shape((T, D)), shape((T, 2), F32)],
        (back, gates, ids, slots),
        300_000_000,
        1_000_000,
    )
    return patch_grad, gate_grad, grad_in[None], grad_out[None]


def solution(mesh):
    names = ("zlo", "y", "x", "core", "zhi")
    split = Mesh(mesh.devices.reshape(4, 8, 4, 2, 2), names)
    tokens = P(names, None)
    weights = P(("zlo", "y"), ("x", "core", "zhi"), None)
    return jax.shard_map(
        local,
        mesh=split,
        in_specs=(tokens,) * 5 + (weights,) * 2,
        out_specs=(tokens, tokens, weights, weights),
        check_vma=False,
    )
```

time: 720 us -> 174 us (0.24)
  the two profiles are of different devices: /device:TPU:6 before, /device:TPU:8 now
where the time goes in v1:
time: 174 us; the launch traced here: 173 us
  waiting for transfers between devices  59.1 us (34%)
  blocking collectives  45.4 us (26%)
  starting transfers between devices  29.6 us (17%)
  Pallas kernels  28.8 us (17%)
  local copies, waits for them, and re-layouts  9.27 us (5%)
    all_to_all x1, blocking collectives, local(): lax.all_to_all(sent, everywhere, split_axis=0, concat_axis=0, tiled=True)  45.4 us
    ppermute x9, waiting for transfers between devices, shift(): lax.ppermute(value, axis, [(i, (i + by) % size) for i in range(size)])  43.2 us
    pallas_call x7, Pallas kernels, call(): pl.pallas_call(kernel, out_shape=out_shape, in_specs=in_specs or [VM] * l...  28.8 us
    ppermute x9, starting transfers between devices, shift(): lax.ppermute(value, axis, [(i, (i + by) % size) for i in range(size)])  24.3 us
    all_to_all x1, waiting for transfers between devices, local(): lax.all_to_all(back, everywhere, split_axis=0, concat_axis=0, tiled=True)  15.9 us
    unnamed x28, local copies, waits for them, and re-layouts  9.27 us
    all_to_all x1, starting transfers between devices, local(): lax.all_to_all(back, everywhere, split_axis=0, concat_axis=0, tiled=True)  5.29 us
  transfers between devices with their start and end apart: 10, of which 6 were waited for; matrix products, arithmetic and copies ran while one was open for 0% of the time, Pallas kernels for 7%

profile of v1, /device:TPU:8, one launch (start us, length us, event | category | flops | bytes accessed | tf_op | source)
XLA Modules:
  0.0 173.1 jit_solution(11234012468764035513)
XLA Ops:
  0.6 1.4 copy.11.gates
  2.0 1.4 copy.12.ids
  3.4 1.4 copy.13.slots
  4.8 3.4 %shard_map.102 = bf16[512,896]{1,0:T(8,128)(2,1)} custom-call(bf16[128,1664]{1,0:T(8,128)(2,1)} %patches.1, bf16[128,1664]{1,0:T(8,128)(2,1)} %upstream.1, bf16[128,2]{1,0:T(8,128)(2,1)} %copy.11.gates, s32[128,2]{1,0:T(8,128)} %copy.12.ids, s32[128,2]{1,0:T(8,128)} %copy.13.slots), custom_call_target="tpu_custom_call" | custom-call | flops 500000000 | bytes 2000000 | tf_op jit(solution)/shard_map/pallas_call | solution.py:186
  8.2 45.4 %all_to_all.22 = bf16[64,8,896]{2,1,0:T(8,128)(2,1)} all-to-all(bf16[64,8,896]{2,1,0:T(8,128)(2,1)} %bitcast.9), channel_id=1, replica_groups=mesh['zlo'=4,'y'=8,'x'=4,'core'=2,'zhi'=2] {'zlo','y','zhi'}, dimensions={0} | all-to-all | bytes 1835008 | tf_op jit(solution)/shard_map/all_to_all | solution.py:208
  53.6 2.5 %shard_map.103.r0 = bf16[256,1664]{1,0:T(8,128)(2,1)} custom-call(bf16[512,896]{1,0:T(8,128)(2,1)} %bitcast.8), custom_call_target="tpu_custom_call" | custom-call | flops 300000000 | bytes 2000000 | tf_op jit(solution)/shard_map/pallas_call | solution.py:186
  56.1 4.7 %collective-permute-start.2 = (bf16[256,1664]{1,0:T(8,128)(2,1)}, bf16[256,1664]{1,0:T(8,128)(2,1)S(1)}, u32[]{:S(2)}, u32[]{:S(2)}) collective-permute-start(bf16[256,1664]{1,0:T(8,128)(2,1)} %shard_map.103.r0), channel_id=1, source_target_pairs={{0,12},{4,0},{8,4},{12,8},{1,13},{5,1},{9,5},{13,9},{2,14},{6,2},{... | collective-permute-start | bytes 2555912 | tf_op jit(solution)/shard_map/ppermute | solution.py:199
  60.8 2.7 %collective-permute-start.1 = (bf16[256,1664]{1,0:T(8,128)(2,1)}, bf16[256,1664]{1,0:T(8,128)(2,1)S(1)}, u32[]{:S(2)}, u32[]{:S(2)}) collective-permute-start(bf16[256,1664]{1,0:T(8,128)(2,1)} %shard_map.103.r0), channel_id=1, source_target_pairs={{0,8},{4,12},{8,0},{12,4},{1,9},{5,13},{9,1},{13,5},{2,10},{6,14},... | collective-permute-start | bytes 2555912 | tf_op jit(solution)/shard_map/ppermute | solution.py:199
  63.5 2.8 %collective-permute-start = (bf16[256,1664]{1,0:T(8,128)(2,1)}, bf16[256,1664]{1,0:T(8,128)(2,1)S(1)}, u32[]{:S(2)}, u32[]{:S(2)}) collective-permute-start(bf16[256,1664]{1,0:T(8,128)(2,1)} %shard_map.103.r0), channel_id=1, source_target_pairs={{0,4},{4,8},{8,12},{12,0},{1,5},{5,9},{9,13},{13,1},{2,6},{6,10},{... | collective-permute-start | bytes 2555912 | tf_op jit(solution)/shard_map/ppermute | solution.py:199
  66.3 0.0 copy-done.8
  66.3 1.9 %collective-permute-start.3 = (bf16[208,1664]{1,0:T(8,128)(2,1)S(1)}, bf16[208,1664]{1,0:T(8,128)(2,1)S(1)}, u32[]{:S(2)}, u32[]{:S(2)}) collective-permute-start(bf16[208,1664]{1,0:T(8,128)(2,1)S(1)} %bitcast.13), channel_id=1, source_target_pairs={{0,2},{2,0},{1,3},{3,1},{4,6},{6,4},{5,7},{7,5},{8,10},{10,8},{9,1... | collective-permute-start | bytes 2076680 | tf_op jit(solution)/shard_map/ppermute | solution.py:199
  68.2 0.0 copy-done.9
  68.3 2.4 %collective-permute-start.4 = (bf16[208,1664]{1,0:T(8,128)(2,1)S(1)}, bf16[208,1664]{1,0:T(8,128)(2,1)S(1)}, u32[]{:S(2)}, u32[]{:S(2)}) collective-permute-start(bf16[208,1664]{1,0:T(8,128)(2,1)S(1)} %bitcast.15), channel_id=1, source_target_pairs={{0,2},{2,0},{1,3},{3,1},{4,6},{6,4},{5,7},{7,5},{8,10},{10,8},{9,1... | collective-permute-start | bytes 2076680 | tf_op jit(solution)/shard_map/ppermute | solution.py:199
  70.7 0.0 collective-permute-done.3.wi1
  70.7 0.0 copy-start.10
  70.7 1.7 %collective-permute-done.4.wo1 = bf16[208,1664]{1,0:T(8,128)(2,1)S(1)} collective-permute-done((bf16[208,1664]{1,0:T(8,128)(2,1)S(1)}, bf16[208,1664]{1,0:T(8,128)(2,1)S(1)}, u32[]{:S(2)}, u32[]{:S(2)}) %collective-permute-start.4) | collective-permute-done | bytes 692256 | tf_op jit(solution)/shard_map/ppermute | solution.py:199
  72.4 24.1 %collective-permute-done.2.r3 = bf16[256,1664]{1,0:T(8,128)(2,1)S(1)} collective-permute-done((bf16[256,1664]{1,0:T(8,128)(2,1)}, bf16[256,1664]{1,0:T(8,128)(2,1)S(1)}, u32[]{:S(2)}, u32[]{:S(2)}) %collective-permute-start.2) | collective-permute-done | bytes 852000 | tf_op jit(solution)/shard_map/ppermute | solution.py:199
  96.6 0.0 collective-permute-done.1.r2
  96.6 5.5 %collective-permute-done.r1 = bf16[256,1664]{1,0:T(8,128)(2,1)S(1)} collective-permute-done((bf16[256,1664]{1,0:T(8,128)(2,1)}, bf16[256,1664]{1,0:T(8,128)(2,1)S(1)}, u32[]{:S(2)}, u32[]{:S(2)}) %collective-permute-start) | collective-permute-done | bytes 852000 | tf_op jit(solution)/shard_map/ppermute | solution.py:199
  102.0 0.0 copy-done.10
  102.0 0.0 copy-done.11
  102.0 0.0 copy-done.5
  102.0 0.0 copy-done.6
  102.1 0.0 copy-start.7
  102.1 0.9 copy-done.7
  103.0 8.2 %shard_map.104 = (bf16[128,1792]{1,0:T(8,128)(2,1)}, bf16[128,1792]{1,0:T(8,128)(2,1)}, bf16[128,1792]{1,0:T(8,128)(2,1)}, bf16[128,1792]{1,0:T(8,128)(2,1)}, bf...) custom-call(bf16[256,1664]{1,0:T(8,128)(2,1)} %shard_map.103.r0, bf16[256,1664]{1,0:T(8,128)(2,1)} %copy-done.7, ...), custom_call_target="tpu_custom_call" | custom-call | flops 2200000000 | bytes 9000000 | tf_op jit(solution)/shard_map/pallas_call | solution.py:186
  111.2 2.5 %collective-permute-start.5 = (bf16[128,1792]{1,0:T(8,128)(2,1)}, bf16[128,1792]{1,0:T(8,128)(2,1)S(1)}, u32[]{:S(2)}, u32[]{:S(2)}) collective-permute-start(bf16[128,1792]{1,0:T(8,128)(2,1)} %get-tuple-element.18), channel_id=1, source_target_pairs={{0,12},{4,0},{8,4},{12,8},{1,13},{5,1},{9,5},{13,9},{2,14},{6,2},{... | collective-permute-start | bytes 1376264 | tf_op jit(solution)/shard_map/ppermute | solution.py:199
  113.8 2.7 %collective-permute-start.6 = (bf16[128,1792]{1,0:T(8,128)(2,1)}, bf16[128,1792]{1,0:T(8,128)(2,1)S(1)}, u32[]{:S(2)}, u32[]{:S(2)}) collective-permute-start(bf16[128,1792]{1,0:T(8,128)(2,1)} %get-tuple-element.19), channel_id=1, source_target_pairs={{0,8},{4,12},{8,0},{12,4},{1,9},{5,13},{9,1},{13,5},{2,10},{6,14},... | collective-permute-start | bytes 1376264 | tf_op jit(solution)/shard_map/ppermute | solution.py:199
  116.5 2.7 %collective-permute-start.7 = (bf16[128,1792]{1,0:T(8,128)(2,1)}, bf16[128,1792]{1,0:T(8,128)(2,1)S(1)}, u32[]{:S(2)}, u32[]{:S(2)}) collective-permute-start(bf16[128,1792]{1,0:T(8,128)(2,1)} %get-tuple-element.20), channel_id=1, source_target_pairs={{0,4},{4,8},{8,12},{12,0},{1,5},{5,9},{9,13},{13,1},{2,6},{6,10},{... | collective-permute-start | bytes 1376264 | tf_op jit(solution)/shard_map/ppermute | solution.py:199
  119.2 6.0 %shard_map.107 = (f32[208,1664]{1,0:T(8,128)}, f32[208,1664]{1,0:T(8,128)}, bf16[416,1664]{1,0:T(8,128)(2,1)}) custom-call(bf16[256,1664]{1,0:T(8,128)(2,1)} %shard_map.103.r0, bf16[256,1664]{1,0:T(8,128)(2,1)} %copy-done.7, bf16[256,1664]{1,0:T(8,128)(2,1)} %copy-done.6, bf16[256,1664]{1,0:T(8,128)(2,1)} %copy-done.5, ...), custom_call_target="tpu_custom_call" | custom-call | flops 1400000000 | bytes 9000000 | tf_op jit(solution)/shard_map/pallas_call | solution.py:186
  125.2 1.9 %collective-permute-start.8 = (bf16[416,1664]{1,0:T(8,128)(2,1)}, bf16[416,1664]{1,0:T(8,128)(2,1)S(1)}, u32[]{:S(2)}, u32[]{:S(2)}) collective-permute-start(bf16[416,1664]{1,0:T(8,128)(2,1)} %get-tuple-element.27), channel_id=1, source_target_pairs={{0,2},{2,0},{1,3},{3,1},{4,6},{6,4},{5,7},{7,5},{8,10},{10,8},{9,1... | collective-permute-start | bytes 4153352 | tf_op jit(solution)/shard_map/ppermute | solution.py:199
  127.2 0.0 collective-permute-done.5.i1
  127.2 0.0 copy-start.2
  127.2 3.7 %collective-permute-done.6.i2 = bf16[128,1792]{1,0:T(8,128)(2,1)S(1)} collective-permute-done((bf16[128,1792]{1,0:T(8,128)(2,1)}, bf16[128,1792]{1,0:T(8,128)(2,1)S(1)}, u32[]{:S(2)}, u32[]{:S(2)}) %collective-permute-start.6) | collective-permute-done | bytes 458784 | tf_op jit(solution)/shard_map/ppermute | solution.py:199
  130.9 8.2 %collective-permute-done.7.i3 = bf16[128,1792]{1,0:T(8,128)(2,1)S(1)} collective-permute-done((bf16[128,1792]{1,0:T(8,128)(2,1)}, bf16[128,1792]{1,0:T(8,128)(2,1)S(1)}, u32[]{:S(2)}, u32[]{:S(2)}) %collective-permute-start.7) | collective-permute-done | bytes 458784 | tf_op jit(solution)/shard_map/ppermute | solution.py:199
  139.1 0.0 copy-done.2
  139.1 0.0 copy-done.3
  139.1 0.8 copy-done.4
  139.8 3.0 %shard_map.105 = bf16[512,512]{1,0:T(8,128)(2,1)} custom-call(bf16[128,1792]{1,0:T(8,128)(2,1)} %get-tuple-element.17.i0, bf16[128,1792]{1,0:T(8,128)(2,1)} %copy-done.2, bf16[128,1792]{1,0:T(8,128)(2,1)} %copy-done.3, bf16[128,1792]{1,0:T(8,128)(2,1)} %copy-done.4), custom_call_target="tpu_custom_call" | custom-call | flops 300000000 | bytes 2500000 | tf_op jit(solution)/shard_map/pallas_call | solution.py:186
  142.8 5.3 %all-to-all-start.1 = ((bf16[64,8,512]{2,1,0:T(8,128)(2,1)}), bf16[64,8,512]{2,1,0:T(8,128)(2,1)S(1)}, u32[]{:S(2)}, u32[]{:S(2)}) async-start(bf16[64,8,512]{2,1,0:T(8,128)(2,1)} %bitcast.10), calls=%async_computation.1 | async-start | bytes 1048576 | tf_op jit(solution)/shard_map/all_to_all | solution.py:242
  148.1 0.0 collective-permute-done.8.got
  148.1 0.0 copy-start
  148.1 1.1 copy-done
  149.2 3.4 %shard_map.108 = (bf16[208,1664]{1,0:T(8,128)(2,1)}, bf16[208,1664]{1,0:T(8,128)(2,1)}) custom-call(f32[208,1664]{1,0:T(8,128)} %get-tuple-element.25.own_in, f32[208,1664]{1,0:T(8,128)} %get-tuple-element.26.own_out, bf16[416,1664]{1,0:T(8,128)(2,1)} %copy-done), custom_call_target="tpu_custom_call" | custom-call | flops 1000000 | bytes 6000000 | tf_op jit(solution)/shard_map/pallas_call | solution.py:186
  152.5 15.9 %all-to-all-done.1 = bf16[64,8,512]{2,1,0:T(8,128)(2,1)S(1)} async-done(((bf16[64,8,512]{2,1,0:T(8,128)(2,1)}), bf16[64,8,512]{2,1,0:T(8,128)(2,1)S(1)}, u32[]{:S(2)}, u32[]{:S(2)}) %all-to-all-start.1) | async-done | bytes 524320 | tf_op jit(solution)/shard_map/all_to_all | solution.py:242
  168.5 0.8 copy-done.1
  169.3 2.3 %shard_map.106 = (bf16[128,1664]{1,0:T(8,128)(2,1)}, f32[128,2]{1,0:T(8,128)}) custom-call(bf16[512,512]{1,0:T(8,128)(2,1)} %bitcast.11, bf16[128,2]{1,0:T(8,128)(2,1)} %copy.11.gates, s32[128,2]{1,0:T(8,128)} %copy.12.ids, s32[128,2]{1,0:T(8,128)} %copy.13.slots), custom_call_target="tpu_custom_call" | custom-call | flops 300000000 | bytes 1000000 | tf_op jit(solution)/shard_map/pallas_call | solution.py:186
  171.6 1.5 copy.17
  (8 shorter events, 0.0 us)
Async XLA Ops:
  8.2 58.1 %copy-start.8 = (bf16[1,208,1664]{2,1,0:T(8,128)(2,1)S(1)}, bf16[1,208,1664]{2,1,0:T(8,128)(2,1)}, u32[]{:S(2)}) copy-start(bf16[1,208,1664]{2,1,0:T(8,128)(2,1)} %param.12) | copy-start | bytes 2076676
  8.2 60.0 %copy-start.9 = (bf16[1,208,1664]{2,1,0:T(8,128)(2,1)S(1)}, bf16[1,208,1664]{2,1,0:T(8,128)(2,1)}, u32[]{:S(2)}) copy-start(bf16[1,208,1664]{2,1,0:T(8,128)(2,1)} %param.13) | copy-start | bytes 2076676
  56.1 40.4 %collective-permute-start.2 = (bf16[256,1664]{1,0:T(8,128)(2,1)}, bf16[256,1664]{1,0:T(8,128)(2,1)S(1)}, u32[]{:S(2)}, u32[]{:S(2)}) collective-permute-start(bf16[256,1664]{1,0:T(8,128)(2,1)} %shard_map.103.r0), channel_id=1, source_target_pairs={{0,12},{4,0},{8,4},{12,8},{1,13},{5,1},{9,5},{13,9},{2,14},{6,2},{... | collective-permute-start | bytes 2555912 | tf_op jit(solution)/shard_map/ppermute | solution.py:199
  60.8 35.8 %collective-permute-start.1 = (bf16[256,1664]{1,0:T(8,128)(2,1)}, bf16[256,1664]{1,0:T(8,128)(2,1)S(1)}, u32[]{:S(2)}, u32[]{:S(2)}) collective-permute-start(bf16[256,1664]{1,0:T(8,128)(2,1)} %shard_map.103.r0), channel_id=1, source_target_pairs={{0,8},{4,12},{8,0},{12,4},{1,9},{5,13},{9,1},{13,5},{2,10},{6,14},... | collective-permute-start | bytes 2555912 | tf_op jit(solution)/shard_map/ppermute | solution.py:199
  63.5 38.5 %collective-permute-start = (bf16[256,1664]{1,0:T(8,128)(2,1)}, bf16[256,1664]{1,0:T(8,128)(2,1)S(1)}, u32[]{:S(2)}, u32[]{:S(2)}) collective-permute-start(bf16[256,1664]{1,0:T(8,128)(2,1)} %shard_map.103.r0), channel_id=1, source_target_pairs={{0,4},{4,8},{8,12},{12,0},{1,5},{5,9},{9,13},{13,1},{2,6},{6,10},{... | collective-permute-start | bytes 2555912 | tf_op jit(solution)/shard_map/ppermute | solution.py:199
  66.3 4.4 %collective-permute-start.3 = (bf16[208,1664]{1,0:T(8,128)(2,1)S(1)}, bf16[208,1664]{1,0:T(8,128)(2,1)S(1)}, u32[]{:S(2)}, u32[]{:S(2)}) collective-permute-start(bf16[208,1664]{1,0:T(8,128)(2,1)S(1)} %bitcast.13), channel_id=1, source_target_pairs={{0,2},{2,0},{1,3},{3,1},{4,6},{6,4},{5,7},{7,5},{8,10},{10,8},{9,1... | collective-permute-start | bytes 2076680 | tf_op jit(solution)/shard_map/ppermute | solution.py:199
  68.3 4.2 %collective-permute-start.4 = (bf16[208,1664]{1,0:T(8,128)(2,1)S(1)}, bf16[208,1664]{1,0:T(8,128)(2,1)S(1)}, u32[]{:S(2)}, u32[]{:S(2)}) collective-permute-start(bf16[208,1664]{1,0:T(8,128)(2,1)S(1)} %bitcast.15), channel_id=1, source_target_pairs={{0,2},{2,0},{1,3},{3,1},{4,6},{6,4},{5,7},{7,5},{8,10},{10,8},{9,1... | collective-permute-start | bytes 2076680 | tf_op jit(solution)/shard_map/ppermute | solution.py:199
  70.7 31.4 %copy-start.10 = (bf16[208,1664]{1,0:T(8,128)(2,1)}, bf16[208,1664]{1,0:T(8,128)(2,1)S(1)}, u32[]{:S(2)}) copy-start(bf16[208,1664]{1,0:T(8,128)(2,1)S(1)} %collective-permute-done.3.wi1) | copy-start | bytes 2076676
  72.4 29.6 %copy-start.11 = (bf16[208,1664]{1,0:T(8,128)(2,1)}, bf16[208,1664]{1,0:T(8,128)(2,1)S(1)}, u32[]{:S(2)}) copy-start(bf16[208,1664]{1,0:T(8,128)(2,1)S(1)} %collective-permute-done.4.wo1) | copy-start | bytes 2076676
  96.6 5.5 %copy-start.5 = (bf16[256,1664]{1,0:T(8,128)(2,1)}, bf16[256,1664]{1,0:T(8,128)(2,1)S(1)}, u32[]{:S(2)}) copy-start(bf16[256,1664]{1,0:T(8,128)(2,1)S(1)} %collective-permute-done.2.r3) | copy-start | bytes 2555908
  96.6 5.5 %copy-start.6 = (bf16[256,1664]{1,0:T(8,128)(2,1)}, bf16[256,1664]{1,0:T(8,128)(2,1)S(1)}, u32[]{:S(2)}) copy-start(bf16[256,1664]{1,0:T(8,128)(2,1)S(1)} %collective-permute-done.1.r2) | copy-start | bytes 2555908
  102.1 0.9 copy-start.7
  111.2 15.9 %collective-permute-start.5 = (bf16[128,1792]{1,0:T(8,128)(2,1)}, bf16[128,1792]{1,0:T(8,128)(2,1)S(1)}, u32[]{:S(2)}, u32[]{:S(2)}) collective-permute-start(bf16[128,1792]{1,0:T(8,128)(2,1)} %get-tuple-element.18), channel_id=1, source_target_pairs={{0,12},{4,0},{8,4},{12,8},{1,13},{5,1},{9,5},{13,9},{2,14},{6,2},{... | collective-permute-start | bytes 1376264 | tf_op jit(solution)/shard_map/ppermute | solution.py:199
  113.8 17.1 %collective-permute-start.6 = (bf16[128,1792]{1,0:T(8,128)(2,1)}, bf16[128,1792]{1,0:T(8,128)(2,1)S(1)}, u32[]{:S(2)}, u32[]{:S(2)}) collective-permute-start(bf16[128,1792]{1,0:T(8,128)(2,1)} %get-tuple-element.19), channel_id=1, source_target_pairs={{0,8},{4,12},{8,0},{12,4},{1,9},{5,13},{9,1},{13,5},{2,10},{6,14},... | collective-permute-start | bytes 1376264 | tf_op jit(solution)/shard_map/ppermute | solution.py:199
  116.5 22.6 %collective-permute-start.7 = (bf16[128,1792]{1,0:T(8,128)(2,1)}, bf16[128,1792]{1,0:T(8,128)(2,1)S(1)}, u32[]{:S(2)}, u32[]{:S(2)}) collective-permute-start(bf16[128,1792]{1,0:T(8,128)(2,1)} %get-tuple-element.20), channel_id=1, source_target_pairs={{0,4},{4,8},{8,12},{12,0},{1,5},{5,9},{9,13},{13,1},{2,6},{6,10},{... | collective-permute-start | bytes 1376264 | tf_op jit(solution)/shard_map/ppermute | solution.py:199
  125.2 22.8 %collective-permute-start.8 = (bf16[416,1664]{1,0:T(8,128)(2,1)}, bf16[416,1664]{1,0:T(8,128)(2,1)S(1)}, u32[]{:S(2)}, u32[]{:S(2)}) collective-permute-start(bf16[416,1664]{1,0:T(8,128)(2,1)} %get-tuple-element.27), channel_id=1, source_target_pairs={{0,2},{2,0},{1,3},{3,1},{4,6},{6,4},{5,7},{7,5},{8,10},{10,8},{9,1... | collective-permute-start | bytes 4153352 | tf_op jit(solution)/shard_map/ppermute | solution.py:199
  127.2 11.9 %copy-start.2 = (bf16[128,1792]{1,0:T(8,128)(2,1)}, bf16[128,1792]{1,0:T(8,128)(2,1)S(1)}, u32[]{:S(2)}) copy-start(bf16[128,1792]{1,0:T(8,128)(2,1)S(1)} %collective-permute-done.5.i1) | copy-start | bytes 1376260
  130.9 8.2 %copy-start.3 = (bf16[128,1792]{1,0:T(8,128)(2,1)}, bf16[128,1792]{1,0:T(8,128)(2,1)S(1)}, u32[]{:S(2)}) copy-start(bf16[128,1792]{1,0:T(8,128)(2,1)S(1)} %collective-permute-done.6.i2) | copy-start | bytes 1376260
  139.1 0.8 copy-start.4
  142.8 25.7 %all-to-all-start.1 = ((bf16[64,8,512]{2,1,0:T(8,128)(2,1)}), bf16[64,8,512]{2,1,0:T(8,128)(2,1)S(1)}, u32[]{:S(2)}, u32[]{:S(2)}) async-start(bf16[64,8,512]{2,1,0:T(8,128)(2,1)} %bitcast.10), calls=%async_computation.1 | async-start | bytes 1048576 | tf_op jit(solution)/shard_map/all_to_all | solution.py:242
  148.1 1.1 copy-start
  168.5 0.8 copy-start.1

commit v2 on v1

v2 whole, which is shorter than its diff:
```python
import functools

import jax
import jax.numpy as jnp
from jax import lax
from jax.experimental import pallas as pl
from jax.experimental.pallas import tpu as pltpu
from jax.sharding import Mesh, PartitionSpec as P

F32 = jnp.float32
BF16 = jnp.bfloat16
I32 = jnp.int32

CAP = 2
ROOT_TERM = 0.7978845608028654
CUBIC_TERM = 0.044715

T = 128
D = 1664
HS = 208
SRC = 64
ROWS = SRC * CAP
SEND = SRC * 8
HALF_W = 896
QW = 512
GW = D + 128


def dot(left, right):
    return jnp.dot(left, right, preferred_element_type=F32)


def dot_rows(left, right):
    return lax.dot_general(left, right, (((0,), (0,)), ((), ())), preferred_element_type=F32)


def dot_width(left, right):
    return lax.dot_general(left, right, (((1,), (1,)), ((), ())), preferred_element_type=F32)


def slot_match(ids, slots):
    target = jnp.where(slots >= 0, ids * CAP + slots, -1)
    row = lax.broadcasted_iota(I32, (SEND, T), 0)
    slot = (row >> 4) * CAP + (row & 1)
    return target[0:1, :] == slot, target[1:2, :] == slot, row


def pack_rows_kernel(patches, upstream, gates, ids, slots, w_in, w_out, out, w_both, sems):
    copies = [
        pltpu.make_async_copy(w, w_both.at[pl.ds(k * HS, HS), :], sems.at[k]) for k, w in enumerate((w_in, w_out))
    ]
    for copy in copies:
        copy.start()
    m0, m1, row = slot_match(ids[...], slots[...])
    g = gates[...].astype(F32)
    hit = jnp.where(m0 | m1, 1.0, 0.0)
    gate = jnp.where(m0, g[0:1, :], 0.0) + jnp.where(m1, g[1:2, :], 0.0)
    is_up = (row & 2) != 0
    right = (row & 4) != 0
    p_sel = jnp.where(is_up, 0.0, hit)
    u_sel = jnp.where(is_up, gate, 0.0)
    p_l = jnp.where(right, 0.0, p_sel).astype(BF16)
    p_r = jnp.where(right, p_sel, 0.0).astype(BF16)
    u_l = jnp.where(right, 0.0, u_sel).astype(BF16)
    u_r = jnp.where(right, u_sel, 0.0).astype(BF16)
    rest = D - HALF_W
    out[:, :rest] = (
        dot(p_l, patches[:, :rest])
        + dot(u_l, upstream[:, :rest])
        + dot(p_r, patches[:, HALF_W:])
        + dot(u_r, upstream[:, HALF_W:])
    ).astype(BF16)
    out[:, rest:] = (dot(p_l, patches[:, rest:HALF_W]) + dot(u_l, upstream[:, rest:HALF_W])).astype(BF16)
    for copy in copies:
        copy.wait()


def unpack_rows_kernel(got, out):
    part = 256
    o = lax.broadcasted_iota(I32, (128, part), 0)
    c = lax.broadcasted_iota(I32, (128, part), 1)
    want = ((o & 63) >> 1) * 8 + (o >> 6) * 2 + (o & 1)
    for g in range(SEND // part):
        block = got[pl.ds(g * part, part), :]
        for h in range(2):
            sel = jnp.where(c == want + 4 * h, 1.0, 0.0).astype(BF16)
            wide = HALF_W if h == 0 else D - HALF_W
            rows = dot(sel, block[:, :wide]).astype(BF16)
            out[pl.ds(g * 64, 64), pl.ds(h * HALF_W, wide)] = rows[:64]
            out[pl.ds(ROWS + g * 64, 64), pl.ds(h * HALF_W, wide)] = rows[64:]


def gelu_and_slope(value):
    square = value * value
    tangent = jnp.tanh(ROOT_TERM * value * (1.0 + CUBIC_TERM * square))
    up = 0.5 * (1.0 + tangent)
    slope = up + 0.5 * value * (1.0 - tangent * tangent) * ROOT_TERM * (1.0 + 3.0 * CUBIC_TERM * square)
    return value * up, slope


def expert_kernel(rows, w0, w1, w2, w3, part, pg_out, hid_out):
    p, u = rows[pl.ds(0, ROWS), :], rows[pl.ds(ROWS, ROWS), :]
    gate = jnp.zeros((ROWS, 1), F32)
    total = jnp.zeros((ROWS, D), F32)
    for c, w in enumerate((w0, w1, w2, w3)):
        pre = dot_width(p, w[pl.ds(0, HS), :])
        back = dot_width(u, w[pl.ds(HS, HS), :])
        hid, slope = gelu_and_slope(pre)
        gate += jnp.sum(hid * back, axis=1, keepdims=True)
        pg = (back * slope).astype(BF16)
        pg_out[c] = pg
        hid_out[c] = hid.astype(BF16)
        total += dot(pg, w[pl.ds(0, HS), :])
    part[:, :D] = total.astype(BF16)
    lane = lax.broadcasted_iota(I32, (ROWS, 128), 1)
    part[:, D:] = jnp.where(lane == 0, gate, 0.0).astype(BF16)


def weight_grads(c, rows0, rows1, pg0, pg1, hid0, hid1):
    p0, u0 = rows0[pl.ds(0, ROWS), :], rows0[pl.ds(ROWS, ROWS), :]
    p1, u1 = rows1[pl.ds(0, ROWS), :], rows1[pl.ds(ROWS, ROWS), :]
    return (
        dot_rows(pg0[c], p0) + dot_rows(pg1[c], p1),
        dot_rows(hid0[c], u0) + dot_rows(hid1[c], u1),
    )


def weight_kernel(c, kind, add, *refs):
    out = refs[-1]
    grad_in, grad_out = weight_grads(c, *refs[:6])
    if add:
        got = refs[6]
        grad_in += got[pl.ds(0, HS), :].astype(F32)
        grad_out += got[pl.ds(HS, HS), :].astype(F32)
    out[pl.ds(0, HS), :] = grad_in.astype(kind)
    out[pl.ds(HS, HS), :] = grad_out.astype(kind)


def weight_sum_kernel(own, got, grad_in, grad_out):
    grad_in[...] = (own[pl.ds(0, HS), :] + got[pl.ds(0, HS), :].astype(F32)).astype(BF16)
    grad_out[...] = (own[pl.ds(HS, HS), :] + got[pl.ds(HS, HS), :].astype(F32)).astype(BF16)


def pack_back_kernel(i0, i1, out):
    total = (i0[...].astype(F32) + i1[...].astype(F32)).astype(BF16)
    row = lax.broadcasted_iota(I32, (SEND, ROWS), 0)
    col = lax.broadcasted_iota(I32, (SEND, ROWS), 1)
    want = (row >> 3) * 2 + (row & 1)
    quarter = (row >> 1) & 3
    sels = [jnp.where((col == want) & (quarter == q), 1.0, 0.0).astype(BF16) for q in range(4)]
    last = GW - 3 * QW
    narrow = sum(dot(sels[q], total[:, q * QW : q * QW + last]) for q in range(4))
    wide = sum(dot(sels[q], total[:, q * QW + last : (q + 1) * QW]) for q in range(3))
    out[:, :last] = narrow.astype(BF16)
    out[:, last:] = wide.astype(BF16)


def unpack_back_kernel(got, gates, ids, slots, patch_grad, gate_grad):
    m0, m1, row = slot_match(ids[...], slots[...])
    quarter = (row >> 1) & 3
    hit = jnp.where(m0 | m1, 1.0, 0.0)
    for q in range(4):
        wide = QW if q < 3 else D - 3 * QW
        sel = jnp.where(quarter == q, hit, 0.0).astype(BF16)
        patch_grad[:, pl.ds(q * QW, wide)] = dot_rows(sel, got[:, :wide]).astype(BF16)
    gate_block = got[:, D - 3 * QW : GW - 3 * QW]
    g = gates[...].astype(F32)
    for k, m in enumerate((m0, m1)):
        sel = jnp.where((quarter == 3) & m, 1.0, 0.0).astype(BF16)
        gate_grad[k : k + 1, :] = dot_rows(gate_block, sel)[0:1, :] / g[k : k + 1, :]


def shape(dims, kind=BF16):
    return jax.ShapeDtypeStruct(dims, kind)


ANY = pl.BlockSpec(memory_space=pl.ANY)
VM = pl.BlockSpec(memory_space=pltpu.VMEM)


def call(kernel, out_shape, args, flops, moved, vmem, in_specs=None, out_specs=None, scratch=()):
    return pl.pallas_call(
        kernel,
        out_shape=out_shape,
        in_specs=in_specs or [VM] * len(args),
        out_specs=out_specs or jax.tree.map(lambda _: VM, out_shape),
        scratch_shapes=scratch,
        compiler_params=pltpu.CompilerParams(vmem_limit_bytes=vmem * 1024 * 1024),
        cost_estimate=pl.CostEstimate(flops=flops, bytes_accessed=moved, transcendentals=0),
    )(*args)


def swap(value, axis, partner):
    return lax.ppermute(value, axis, [(i, partner(i)) for i in range(lax.axis_size(axis))])


def swap_rows(value):
    return swap(value, "x", lambda i: i ^ 1)


def swap_weights(value):
    return swap(value, "x", lambda i: 3 - i)


def swap_core(value):
    return swap(value, "core", lambda i: 1 - i)


def local(patches, upstream, gates, ids, slots, in_weights, out_weights):
    everywhere = ("zlo", "y", "zhi")
    gates, ids, slots = gates.T, ids.T, slots.T
    both = shape((2 * HS, D))
    sent, w00 = call(
        pack_rows_kernel,
        [shape((SEND, HALF_W)), both],
        (patches, upstream, gates, ids, slots, in_weights[0], out_weights[0]),
        500_000_000,
        5_000_000,
        16,
        in_specs=[VM] * 5 + [ANY] * 2,
        out_specs=[VM, ANY],
        scratch=[pltpu.SemaphoreType.DMA((2,))],
    )
    w01 = swap_weights(w00)
    got = lax.all_to_all(sent, everywhere, split_axis=0, concat_axis=0, tiled=True)
    own = call(unpack_rows_kernel, shape((2 * ROWS, D)), (got,), 300_000_000, 2_000_000, 16)
    other = swap_rows(own)
    w10, w11 = swap_core(w00), swap_core(w01)
    hidden = shape((4, ROWS, HS))
    expert_out = [shape((ROWS, GW)), hidden, hidden]
    weights = (w00, w10, w01, w11)
    part_own, pg_own, hid_own = call(expert_kernel, expert_out, (own, *weights), 1_100_000_000, 8_000_000, 24)
    part_other, pg_other, hid_other = call(
        expert_kernel, expert_out, (other, *weights), 1_100_000_000, 8_000_000, 24
    )
    part_back = swap_rows(part_other)
    saved = (own, other, pg_own, pg_other, hid_own, hid_other)

    def weight_call(c, kind, add=()):
        return call(
            functools.partial(weight_kernel, c, kind, len(add)),
            shape((2 * HS, D), kind),
            (*saved, *add),
            700_000_000,
            4_000_000,
            24,
        )

    far = swap_core(weight_call(3, BF16))
    near = swap_core(weight_call(1, BF16))
    far = swap_weights(weight_call(2, BF16, (far,)))
    near = weight_call(0, F32, (near,))
    back = call(pack_back_kernel, shape((SEND, QW)), (part_own, part_back), 300_000_000, 2_500_000, 16)
    back = lax.all_to_all(back, everywhere, split_axis=0, concat_axis=0, tiled=True)
    grad_in, grad_out = call(
        weight_sum_kernel, [shape((HS, D)), shape((HS, D))], (near, far), 1_000_000, 6_000_000, 16
    )
    patch_grad, gate_grad = call(
        unpack_back_kernel,
        [shape((T, D)), shape((2, T), F32)],
        (back, gates, ids, slots),
        300_000_000,
        1_000_000,
        16,
    )
    return patch_grad, gate_grad.T, grad_in[None], grad_out[None]


def solution(mesh):
    names = ("zlo", "y", "x", "core", "zhi")
    split = Mesh(mesh.devices.reshape(4, 8, 4, 2, 2), names)
    tokens = P(names, None)
    weights = P(("zlo", "y"), ("x", "core", "zhi"), None)
    return jax.shard_map(
        local,
        mesh=split,
        in_specs=(tokens,) * 5 + (weights,) * 2,
        out_specs=(tokens, tokens, weights, weights),
        check_vma=False,
    )
```

time: 174 us -> 140 us (0.80)
  the two profiles are of different devices: /device:TPU:8 before, /device:TPU:6 now
where the time goes in v2:
time: 140 us; the launch traced here: 138 us
  waiting for transfers between devices  52.9 us (38%)
  starting transfers between devices  47.9 us (34%)
  Pallas kernels  24.8 us (18%)
  local copies, waits for them, and re-layouts  11.7 us (8%)
    ppermute x8, waiting for transfers between devices, swap(): lax.ppermute(value, axis, [(i, partner(i)) for i in range(lax.axis_size(a...  26.7 us
    ppermute x8, starting transfers between devices, swap(): lax.ppermute(value, axis, [(i, partner(i)) for i in range(lax.axis_size(a...  25.4 us
    pallas_call x11, Pallas kernels, call(): pl.pallas_call(kernel, out_shape=out_shape, in_specs=in_specs or [VM] * l...  24.8 us
    all_to_all x1, waiting for transfers between devices, local(): lax.all_to_all(back, everywhere, split_axis=0, concat_axis=0, tiled=True)  16.4 us
    unnamed x42, local copies, waits for them, and re-layouts  11.7 us
    all_to_all x1, starting transfers between devices, local(): lax.all_to_all(back, everywhere, split_axis=0, concat_axis=0, tiled=True)  11.3 us
    all_to_all x1, starting transfers between devices, local(): lax.all_to_all(sent, everywhere, split_axis=0, concat_axis=0, tiled=True)  11.2 us
    all_to_all x1, waiting for transfers between devices, local(): lax.all_to_all(sent, everywhere, split_axis=0, concat_axis=0, tiled=True)  9.83 us
  transfers between devices with their start and end apart: 10, of which 5 were waited for; matrix products, arithmetic and copies ran while one was open for 0% of the time, Pallas kernels for 11%

profile of v2, /device:TPU:6, one launch (start us, length us, event | category | flops | bytes accessed | tf_op | source)
XLA Modules:
  0.0 138.4 jit_solution(4572768098204687429)
XLA Ops:
  0.6 1.1 copy-done.11
  1.7 1.1 copy-done.12
  2.8 1.0 copy-done.13
  3.8 1.0 copy-done.14
  4.9 0.7 copy-done.15
  5.5 0.7 copy-done.17
  6.2 0.7 copy-done.19
  6.9 1.6 %shard_map.102 = (bf16[512,896]{1,0:T(8,128)(2,1)S(1)}, bf16[416,1664]{1,0:T(8,128)(2,1)S(1)}) custom-call(bf16[128,1664]{1,0:T(8,128)(2,1)S(1)} %copy-done.13, bf16[128,1664]{1,0:T(8,128)(2,1)S(1)} %copy-done.14, bf16[2,128]{1,0:T(2,128)(2,1)S(1)} %bitcast.21, s32[2,128]{1,0:T(2,128)S(1)} %bitcast.17, s32[2,128]{1,0:T(2,128)S(1)} %bitcast.19, ...), custom_call_target="tpu_custom_call" | custom-call | flops 500000000 | bytes 5000000 | tf_op jit(solution)/shard_map/pallas_call | solution.py:182
  8.5 7.8 %collective-permute-start.1 = (bf16[416,1664]{1,0:T(8,128)(2,1)S(1)}, bf16[416,1664]{1,0:T(8,128)(2,1)}, u32[]{:S(2)}, u32[]{:S(2)}) collective-permute-start(bf16[416,1664]{1,0:T(8,128)(2,1)S(1)} %get-tuple-element.17.w0), channel_id=1, source_target_pairs={{0,12},{4,8},{8,4},{12,0},{1,13},{5,9},{9,5},{13,1},{2,14},{6,10},... | collective-permute-start | bytes 4153352 | tf_op jit(solution)/shard_map/ppermute | solution.py:194
  16.3 11.2 %all-to-all-start = ((bf16[64,8,896]{2,1,0:T(8,128)(2,1)}), bf16[64,8,896]{2,1,0:T(8,128)(2,1)S(1)}, u32[]{:S(2)}, u32[]{:S(2)}) async-start(bf16[64,8,896]{2,1,0:T(8,128)(2,1)} %bitcast.13), calls=%async_computation | async-start | bytes 1835008 | tf_op jit(solution)/shard_map/all_to_all | solution.py:225
  27.5 1.9 %collective-permute-start = (bf16[416,1664]{1,0:T(8,128)(2,1)S(1)}, bf16[416,1664]{1,0:T(8,128)(2,1)}, u32[]{:S(2)}, u32[]{:S(2)}) collective-permute-start(bf16[416,1664]{1,0:T(8,128)(2,1)S(1)} %get-tuple-element.17.w0), channel_id=1, source_target_pairs={{0,2},{2,0},{1,3},{3,1},{4,6},{6,4},{5,7},{7,5},{8,10},{10,8},{9,1... | collective-permute-start | bytes 4153352 | tf_op jit(solution)/shard_map/ppermute | solution.py:194
  29.4 14.4 %collective-permute-done.1.w2 = bf16[416,1664]{1,0:T(8,128)(2,1)} collective-permute-done((bf16[416,1664]{1,0:T(8,128)(2,1)S(1)}, bf16[416,1664]{1,0:T(8,128)(2,1)}, u32[]{:S(2)}, u32[]{:S(2)}) %collective-permute-start.1) | collective-permute-done | bytes 1384480 | tf_op jit(solution)/shard_map/ppermute | solution.py:194
  43.8 1.9 %collective-permute-start.2 = (bf16[416,1664]{1,0:T(8,128)(2,1)}, bf16[416,1664]{1,0:T(8,128)(2,1)}, u32[]{:S(2)}, u32[]{:S(2)}) collective-permute-start(bf16[416,1664]{1,0:T(8,128)(2,1)} %collective-permute-done.1.w2), channel_id=1, source_target_pairs={{0,2},{2,0},{1,3},{3,1},{4,6},{6,4},{5,7},{7,5},{8,10},{10,8},{9,1... | collective-permute-start | bytes 4153352 | tf_op jit(solution)/shard_map/ppermute | solution.py:194
  45.7 9.8 %all-to-all-done = bf16[64,8,896]{2,1,0:T(8,128)(2,1)S(1)} async-done(((bf16[64,8,896]{2,1,0:T(8,128)(2,1)}), bf16[64,8,896]{2,1,0:T(8,128)(2,1)S(1)}, u32[]{:S(2)}, u32[]{:S(2)}) %all-to-all-start) | async-done | bytes 917536 | tf_op jit(solution)/shard_map/all_to_all | solution.py:225
  55.5 1.0 copy-done.8
  56.5 1.2 copy-done.9
  57.7 0.4 shard_map.103.rows.refs_0_
  58.1 2.8 %collective-permute-start.3 = (bf16[256,1664]{1,0:T(8,128)(2,1)S(1)}, bf16[256,1664]{1,0:T(8,128)(2,1)S(1)}, u32[]{:S(2)}, u32[]{:S(2)}) collective-permute-start(bf16[256,1664]{1,0:T(8,128)(2,1)S(1)} %shard_map.103.rows.refs_0_), channel_id=1, source_target_pairs={{0,4},{4,0},{8,12},{12,8},{1,5},{5,1},{9,13},{13,9},{2,6},{6,2},{1... | collective-permute-start | bytes 2555912 | tf_op jit(solution)/shard_map/ppermute | solution.py:194
  60.9 0.0 collective-permute-done.w1
  60.9 0.0 collective-permute-done.2.w3
  61.0 5.1 %shard_map.104 = (bf16[128,1792]{1,0:T(8,128)(2,1)S(1)}, bf16[4,128,208]{2,1,0:T(8,128)(2,1)S(1)}, bf16[4,128,208]{2,1,0:T(8,128)(2,1)S(1)}) custom-call(bf16[256,1664]{1,0:T(8,128)(2,1)S(1)} %shard_map.103.rows.refs_0_, bf16[416,1664]{1,0:T(8,128)(2,1)S(1)} %get-tuple-element.17.w0, bf16[416,1664]{1,0:T(8,128)(2,1)} %collective-permute-done.w1, ...), custom_call_target="tpu_custom_call" | custom-call | flops 1100000000 | bytes 8000000 | tf_op jit(solution)/shard_map/pallas_call | solution.py:182
  66.0 0.0 copy-start.2
  66.1 10.8 %collective-permute-done.3.rows.refs_1_ = bf16[256,1664]{1,0:T(8,128)(2,1)S(1)} collective-permute-done((bf16[256,1664]{1,0:T(8,128)(2,1)S(1)}, bf16[256,1664]{1,0:T(8,128)(2,1)S(1)}, u32[]{:S(2)}, u32[]{:S(2)}) %collective-permute-start.3) | collective-permute-done | bytes 852000 | tf_op jit(solution)/shard_map/ppermute | solution.py:194
  76.9 5.1 %shard_map.105 = (bf16[128,1792]{1,0:T(8,128)(2,1)S(1)}, bf16[4,128,208]{2,1,0:T(8,128)(2,1)S(1)}, bf16[4,128,208]{2,1,0:T(8,128)(2,1)S(1)}) custom-call(bf16[256,1664]{1,0:T(8,128)(2,1)S(1)} %collective-permute-done.3.rows.refs_1_, bf16[416,1664]{1,0:T(8,128)(2,1)S(1)} %get-tuple-element.17.w0, bf16[416,1664]{1,0:T(8,128)(2,1)} %collective-permute-done.w1, ...), custom_call_target="tpu_custom_call" | custom-call | flops 1100000000 | bytes 8000000 | tf_op jit(solution)/shard_map/pallas_call | solution.py:182
  81.9 0.0 copy-start.4
  82.0 1.0 shard_map.110
  82.9 1.9 %collective-permute-start.6 = (bf16[416,1664]{1,0:T(8,128)(2,1)S(1)}, bf16[416,1664]{1,0:T(8,128)(2,1)S(1)}, u32[]{:S(2)}, u32[]{:S(2)}) collective-permute-start(bf16[416,1664]{1,0:T(8,128)(2,1)S(1)} %shard_map.110), channel_id=1, source_target_pairs={{0,2},{2,0},{1,3},{3,1},{4,6},{6,4},{5,7},{7,5},{8,10},{10,8},{9,1... | collective-permute-start | bytes 4153352 | tf_op jit(solution)/shard_map/ppermute | solution.py:194
  84.8 2.8 %collective-permute-start.4 = (bf16[128,1792]{1,0:T(8,128)(2,1)S(1)}, bf16[128,1792]{1,0:T(8,128)(2,1)S(1)}, u32[]{:S(2)}, u32[]{:S(2)}) collective-permute-start(bf16[128,1792]{1,0:T(8,128)(2,1)S(1)} %get-tuple-element.19), channel_id=1, source_target_pairs={{0,4},{4,0},{8,12},{12,8},{1,5},{5,1},{9,13},{13,9},{2,6},{6,2},{1... | collective-permute-start | bytes 1376264 | tf_op jit(solution)/shard_map/ppermute | solution.py:194
  87.6 2.1 %shard_map.108 = bf16[416,1664]{1,0:T(8,128)(2,1)} custom-call(bf16[256,1664]{1,0:T(8,128)(2,1)S(1)} %shard_map.103.rows.refs_0_, bf16[256,1664]{1,0:T(8,128)(2,1)S(1)} %collective-permute-done.3.rows.refs_1_, bf16[4,128,208]{2,1,0:T(8,128)(2,1)S(1)} %get-tuple-element.22.refs_2_, bf16[4,128,208]{2,1,0:T(8,128)(2,1)S(1)} %get-tuple-element.23.refs_3_, ...), custom_call_target="tpu_custom_call" | custom-call | flops 700000000 | bytes 4000000 | tf_op jit(solution)/shard_map/pallas_call | solution.py:182
  89.7 2.1 %collective-permute-start.5 = (bf16[416,1664]{1,0:T(8,128)(2,1)}, bf16[416,1664]{1,0:T(8,128)(2,1)}, u32[]{:S(2)}, u32[]{:S(2)}) collective-permute-start(bf16[416,1664]{1,0:T(8,128)(2,1)} %shard_map.108), channel_id=1, source_target_pairs={{0,2},{2,0},{1,3},{3,1},{4,6},{6,4},{5,7},{7,5},{8,10},{10,8},{9,1... | collective-permute-start | bytes 4153352 | tf_op jit(solution)/shard_map/ppermute | solution.py:194
  91.8 0.0 collective-permute-done.6.refs_6_
  91.8 0.0 copy-done.2
  91.9 2.0 %shard_map.111 = bf16[416,1664]{1,0:T(8,128)(2,1)} custom-call(bf16[256,1664]{1,0:T(8,128)(2,1)S(1)} %shard_map.103.rows.refs_0_, bf16[256,1664]{1,0:T(8,128)(2,1)S(1)} %collective-permute-done.3.rows.refs_1_, bf16[4,128,208]{2,1,0:T(8,128)(2,1)S(1)} %get-tuple-element.22.refs_2_, bf16[4,128,208]{2,1,0:T(8,128)(2,1)S(1)} %get-tuple-element.23.refs_3_, ...), custom_call_target="tpu_custom_call" | custom-call | flops 700000000 | bytes 4000000 | tf_op jit(solution)/shard_map/pallas_call | solution.py:182
  93.9 4.2 %collective-permute-start.7 = (bf16[416,1664]{1,0:T(8,128)(2,1)}, bf16[416,1664]{1,0:T(8,128)(2,1)}, u32[]{:S(2)}, u32[]{:S(2)}) collective-permute-start(bf16[416,1664]{1,0:T(8,128)(2,1)} %shard_map.111), channel_id=1, source_target_pairs={{0,12},{4,8},{8,4},{12,0},{1,13},{5,9},{9,5},{13,1},{2,14},{6,10},... | collective-permute-start | bytes 4153352 | tf_op jit(solution)/shard_map/ppermute | solution.py:194
  98.1 1.5 %collective-permute-done.4.i1 = bf16[128,1792]{1,0:T(8,128)(2,1)S(1)} collective-permute-done((bf16[128,1792]{1,0:T(8,128)(2,1)S(1)}, bf16[128,1792]{1,0:T(8,128)(2,1)S(1)}, u32[]{:S(2)}, u32[]{:S(2)}) %collective-permute-start.4) | collective-permute-done | bytes 458784 | tf_op jit(solution)/shard_map/ppermute | solution.py:194
  99.7 1.5 %shard_map.106 = bf16[512,512]{1,0:T(8,128)(2,1)} custom-call(bf16[128,1792]{1,0:T(8,128)(2,1)S(1)} %get-tuple-element.18.i0, bf16[128,1792]{1,0:T(8,128)(2,1)S(1)} %collective-permute-done.4.i1), custom_call_target="tpu_custom_call" | custom-call | flops 300000000 | bytes 2500000 | tf_op jit(solution)/shard_map/pallas_call | solution.py:182
  101.1 11.3 %all-to-all-start.1 = ((bf16[64,8,512]{2,1,0:T(8,128)(2,1)}), bf16[64,8,512]{2,1,0:T(8,128)(2,1)S(1)}, u32[]{:S(2)}, u32[]{:S(2)}) async-start(bf16[64,8,512]{2,1,0:T(8,128)(2,1)} %bitcast.7), calls=%async_computation.1 | async-start | bytes 1048576 | tf_op jit(solution)/shard_map/all_to_all | solution.py:254
  112.4 0.0 copy-start.16
  112.4 0.0 copy-start.18
  112.4 0.0 copy-start.20
  112.5 0.0 collective-permute-done.5.refs_6_
  112.5 2.3 %shard_map.109.own = f32[416,1664]{1,0:T(8,128)S(1)} custom-call(bf16[256,1664]{1,0:T(8,128)(2,1)S(1)} %shard_map.103.rows.refs_0_, bf16[256,1664]{1,0:T(8,128)(2,1)S(1)} %collective-permute-done.3.rows.refs_1_, bf16[4,128,208]{2,1,0:T(8,128)(2,1)S(1)} %get-tuple-element.22.refs_2_, bf16[4,128,208]{2,1,0:T(8,128)(2,1)S(1)} %copy-done.5, ...), custom_call_target="tpu_custom_call" | custom-call | flops 700000000 | bytes 4000000 | tf_op jit(solution)/shard_map/pallas_call | solution.py:182
  114.8 1.5 %copy-done = f32[416,1664]{1,0:T(8,128)} copy-done((f32[416,1664]{1,0:T(8,128)}, f32[416,1664]{1,0:T(8,128)S(1)}, u32[]{:S(2)}) %copy-start) | copy-done | bytes 2768920
  116.3 16.4 %all-to-all-done.1 = bf16[64,8,512]{2,1,0:T(8,128)(2,1)S(1)} async-done(((bf16[64,8,512]{2,1,0:T(8,128)(2,1)}), bf16[64,8,512]{2,1,0:T(8,128)(2,1)S(1)}, u32[]{:S(2)}, u32[]{:S(2)}) %all-to-all-start.1) | async-done | bytes 524320 | tf_op jit(solution)/shard_map/all_to_all | solution.py:254
  132.8 1.3 shard_map.107
  134.0 0.0 collective-permute-done.7.got
  134.0 1.8 %copy-done.1 = f32[416,1664]{1,0:T(8,128)S(1)} copy-done((f32[416,1664]{1,0:T(8,128)S(1)}, f32[416,1664]{1,0:T(8,128)}, u32[]{:S(2)}) %copy-start.1) | copy-done | bytes 2768920
  135.8 2.5 %shard_map.112 = (bf16[208,1664]{1,0:T(8,128)(2,1)}, bf16[208,1664]{1,0:T(8,128)(2,1)}) custom-call(f32[416,1664]{1,0:T(8,128)S(1)} %copy-done.1, bf16[416,1664]{1,0:T(8,128)(2,1)} %collective-permute-done.7.got), custom_call_target="tpu_custom_call" | custom-call | flops 1000000 | bytes 6000000 | tf_op jit(solution)/shard_map/pallas_call | solution.py:182
  (25 shorter events, 0.0 us)
Async XLA Ops:
  0.6 1.1 copy-start.11
  1.7 1.1 copy-start.12
  2.8 1.0 copy-start.13
  3.8 1.0 copy-start.14
  4.8 0.7 copy-start.15
  5.5 0.7 copy-start.17
  6.2 0.7 copy-start.19
  8.5 7.8 %copy-start.10 = (bf16[512,896]{1,0:T(8,128)(2,1)}, bf16[512,896]{1,0:T(8,128)(2,1)S(1)}, u32[]{:S(2)}) copy-start(bf16[512,896]{1,0:T(8,128)(2,1)S(1)} %get-tuple-element.16) | copy-start | bytes 2752516
  8.5 35.3 %collective-permute-start.1 = (bf16[416,1664]{1,0:T(8,128)(2,1)S(1)}, bf16[416,1664]{1,0:T(8,128)(2,1)}, u32[]{:S(2)}, u32[]{:S(2)}) collective-permute-start(bf16[416,1664]{1,0:T(8,128)(2,1)S(1)} %get-tuple-element.17.w0), channel_id=1, source_target_pairs={{0,12},{4,8},{8,4},{12,0},{1,13},{5,9},{9,5},{13,1},{2,14},{6,10},... | collective-permute-start | bytes 4153352 | tf_op jit(solution)/shard_map/ppermute | solution.py:194
  16.3 39.3 %all-to-all-start = ((bf16[64,8,896]{2,1,0:T(8,128)(2,1)}), bf16[64,8,896]{2,1,0:T(8,128)(2,1)S(1)}, u32[]{:S(2)}, u32[]{:S(2)}) async-start(bf16[64,8,896]{2,1,0:T(8,128)(2,1)} %bitcast.13), calls=%async_computation | async-start | bytes 1835008 | tf_op jit(solution)/shard_map/all_to_all | solution.py:225
  27.5 33.4 %collective-permute-start = (bf16[416,1664]{1,0:T(8,128)(2,1)S(1)}, bf16[416,1664]{1,0:T(8,128)(2,1)}, u32[]{:S(2)}, u32[]{:S(2)}) collective-permute-start(bf16[416,1664]{1,0:T(8,128)(2,1)S(1)} %get-tuple-element.17.w0), channel_id=1, source_target_pairs={{0,2},{2,0},{1,3},{3,1},{4,6},{6,4},{5,7},{7,5},{8,10},{10,8},{9,1... | collective-permute-start | bytes 4153352 | tf_op jit(solution)/shard_map/ppermute | solution.py:194
  43.8 17.2 %collective-permute-start.2 = (bf16[416,1664]{1,0:T(8,128)(2,1)}, bf16[416,1664]{1,0:T(8,128)(2,1)}, u32[]{:S(2)}, u32[]{:S(2)}) collective-permute-start(bf16[416,1664]{1,0:T(8,128)(2,1)} %collective-permute-done.1.w2), channel_id=1, source_target_pairs={{0,2},{2,0},{1,3},{3,1},{4,6},{6,4},{5,7},{7,5},{8,10},{10,8},{9,1... | collective-permute-start | bytes 4153352 | tf_op jit(solution)/shard_map/ppermute | solution.py:194
  55.5 1.0 copy-start.8
  56.5 1.2 copy-start.9
  58.1 18.7 %collective-permute-start.3 = (bf16[256,1664]{1,0:T(8,128)(2,1)S(1)}, bf16[256,1664]{1,0:T(8,128)(2,1)S(1)}, u32[]{:S(2)}, u32[]{:S(2)}) collective-permute-start(bf16[256,1664]{1,0:T(8,128)(2,1)S(1)} %shard_map.103.rows.refs_0_), channel_id=1, source_target_pairs={{0,4},{4,0},{8,12},{12,8},{1,5},{5,1},{9,13},{13,9},{2,6},{6,2},{1... | collective-permute-start | bytes 2555912 | tf_op jit(solution)/shard_map/ppermute | solution.py:194
  66.0 25.8 %copy-start.2 = (bf16[4,128,208]{2,1,0:T(8,128)(2,1)}, bf16[4,128,208]{2,1,0:T(8,128)(2,1)S(1)}, u32[]{:S(2)}) copy-start(bf16[4,128,208]{2,1,0:T(8,128)(2,1)S(1)} %get-tuple-element.24.refs_4_) | copy-start | bytes 638980
  81.9 9.9 %copy-start.4 = (bf16[4,128,208]{2,1,0:T(8,128)(2,1)}, bf16[4,128,208]{2,1,0:T(8,128)(2,1)S(1)}, u32[]{:S(2)}) copy-start(bf16[4,128,208]{2,1,0:T(8,128)(2,1)S(1)} %get-tuple-element.23.refs_3_) | copy-start | bytes 638980
  81.9 9.9 %copy-start.6 = (bf16[4,128,208]{2,1,0:T(8,128)(2,1)}, bf16[4,128,208]{2,1,0:T(8,128)(2,1)S(1)}, u32[]{:S(2)}) copy-start(bf16[4,128,208]{2,1,0:T(8,128)(2,1)S(1)} %get-tuple-element.25.refs_5_) | copy-start | bytes 638980
  82.9 8.9 %collective-permute-start.6 = (bf16[416,1664]{1,0:T(8,128)(2,1)S(1)}, bf16[416,1664]{1,0:T(8,128)(2,1)S(1)}, u32[]{:S(2)}, u32[]{:S(2)}) collective-permute-start(bf16[416,1664]{1,0:T(8,128)(2,1)S(1)} %shard_map.110), channel_id=1, source_target_pairs={{0,2},{2,0},{1,3},{3,1},{4,6},{6,4},{5,7},{7,5},{8,10},{10,8},{9,1... | collective-permute-start | bytes 4153352 | tf_op jit(solution)/shard_map/ppermute | solution.py:194
  84.8 14.8 %collective-permute-start.4 = (bf16[128,1792]{1,0:T(8,128)(2,1)S(1)}, bf16[128,1792]{1,0:T(8,128)(2,1)S(1)}, u32[]{:S(2)}, u32[]{:S(2)}) collective-permute-start(bf16[128,1792]{1,0:T(8,128)(2,1)S(1)} %get-tuple-element.19), channel_id=1, source_target_pairs={{0,4},{4,0},{8,12},{12,8},{1,5},{5,1},{9,13},{13,9},{2,6},{6,2},{1... | collective-permute-start | bytes 1376264 | tf_op jit(solution)/shard_map/ppermute | solution.py:194
  89.7 22.8 %collective-permute-start.5 = (bf16[416,1664]{1,0:T(8,128)(2,1)}, bf16[416,1664]{1,0:T(8,128)(2,1)}, u32[]{:S(2)}, u32[]{:S(2)}) collective-permute-start(bf16[416,1664]{1,0:T(8,128)(2,1)} %shard_map.108), channel_id=1, source_target_pairs={{0,2},{2,0},{1,3},{3,1},{4,6},{6,4},{5,7},{7,5},{8,10},{10,8},{9,1... | collective-permute-start | bytes 4153352 | tf_op jit(solution)/shard_map/ppermute | solution.py:194
  93.9 18.6 %copy-start.3 = (bf16[4,128,208]{2,1,0:T(8,128)(2,1)S(1)}, bf16[4,128,208]{2,1,0:T(8,128)(2,1)}, u32[]{:S(2)}) copy-start(bf16[4,128,208]{2,1,0:T(8,128)(2,1)} %copy-done.2) | copy-start | bytes 638980
  93.9 18.6 %copy-start.5 = (bf16[4,128,208]{2,1,0:T(8,128)(2,1)S(1)}, bf16[4,128,208]{2,1,0:T(8,128)(2,1)}, u32[]{:S(2)}) copy-start(bf16[4,128,208]{2,1,0:T(8,128)(2,1)} %copy-done.4) | copy-start | bytes 638980
  93.9 18.6 %copy-start.7 = (bf16[4,128,208]{2,1,0:T(8,128)(2,1)S(1)}, bf16[4,128,208]{2,1,0:T(8,128)(2,1)}, u32[]{:S(2)}) copy-start(bf16[4,128,208]{2,1,0:T(8,128)(2,1)} %copy-done.6) | copy-start | bytes 638980
  93.9 40.1 %collective-permute-start.7 = (bf16[416,1664]{1,0:T(8,128)(2,1)}, bf16[416,1664]{1,0:T(8,128)(2,1)}, u32[]{:S(2)}, u32[]{:S(2)}) collective-permute-start(bf16[416,1664]{1,0:T(8,128)(2,1)} %shard_map.111), channel_id=1, source_target_pairs={{0,12},{4,8},{8,4},{12,0},{1,13},{5,9},{9,5},{13,1},{2,14},{6,10},... | collective-permute-start | bytes 4153352 | tf_op jit(solution)/shard_map/ppermute | solution.py:194
  101.1 31.6 %all-to-all-start.1 = ((bf16[64,8,512]{2,1,0:T(8,128)(2,1)}), bf16[64,8,512]{2,1,0:T(8,128)(2,1)S(1)}, u32[]{:S(2)}, u32[]{:S(2)}) async-start(bf16[64,8,512]{2,1,0:T(8,128)(2,1)} %bitcast.7), calls=%async_computation.1 | async-start | bytes 1048576 | tf_op jit(solution)/shard_map/all_to_all | solution.py:254
  112.4 20.3 %copy-start.16 = (s32[128,2]{0,1:T(2,128)S(1)}, s32[128,2]{0,1:T(2,128)}, u32[]{:S(2)}) copy-start(s32[128,2]{0,1:T(2,128)} %param.10) | copy-start | bytes 3076
  112.4 20.3 %copy-start.18 = (s32[128,2]{0,1:T(2,128)S(1)}, s32[128,2]{0,1:T(2,128)}, u32[]{:S(2)}) copy-start(s32[128,2]{0,1:T(2,128)} %param.11) | copy-start | bytes 3076
  112.4 20.3 %copy-start.20 = (bf16[128,2]{0,1:T(2,128)(2,1)S(1)}, bf16[128,2]{0,1:T(2,128)(2,1)}, u32[]{:S(2)}) copy-start(bf16[128,2]{0,1:T(2,128)(2,1)} %param.9) | copy-start | bytes 1540
  114.8 1.5 %copy-start = (f32[416,1664]{1,0:T(8,128)}, f32[416,1664]{1,0:T(8,128)S(1)}, u32[]{:S(2)}) copy-start(f32[416,1664]{1,0:T(8,128)S(1)} %shard_map.109.own) | copy-start | bytes 8306692
  134.0 1.8 %copy-start.1 = (f32[416,1664]{1,0:T(8,128)S(1)}, f32[416,1664]{1,0:T(8,128)}, u32[]{:S(2)}) copy-start(f32[416,1664]{1,0:T(8,128)} %copy-done) | copy-start | bytes 8306692

commit v3 on v2

--- a/solution.py
+++ b/solution.py
@@ -21,6 +21,7 @@
 SRC = 64
 ROWS = SRC * CAP
 SEND = SRC * 8
+PAD = 256
 HALF_W = 896
 QW = 512
 GW = D + 128
@@ -45,12 +46,29 @@
     return target[0:1, :] == slot, target[1:2, :] == slot, row
 
 
-def pack_rows_kernel(patches, upstream, gates, ids, slots, w_in, w_out, out, w_both, sems):
-    copies = [
-        pltpu.make_async_copy(w, w_both.at[pl.ds(k * HS, HS), :], sems.at[k]) for k, w in enumerate((w_in, w_out))
-    ]
+def start_copies(pairs, sems):
+    copies = [pltpu.make_async_copy(source, place, sems.at[k]) for k, (source, place) in enumerate(pairs)]
     for copy in copies:
         copy.start()
+    return copies
+
+
+def pack_rows_kernel(
+    gates_in, ids_in, slots_in, patches_in, upstream_in, out,
+    gates, ids, slots, patches, upstream, packed, sems, out_sem,
+):
+    copies = start_copies(
+        [
+            (gates_in, gates),
+            (ids_in, ids),
+            (slots_in, slots),
+            (patches_in, patches),
+            (upstream_in, upstream),
+        ],
+        sems,
+    )
+    for copy in copies[:3]:
+        copy.wait()
     m0, m1, row = slot_match(ids[...], slots[...])
     g = gates[...].astype(F32)
     hit = jnp.where(m0 | m1, 1.0, 0.0)
@@ -63,24 +81,31 @@
     p_r = jnp.where(right, p_sel, 0.0).astype(BF16)
     u_l = jnp.where(right, 0.0, u_sel).astype(BF16)
     u_r = jnp.where(right, u_sel, 0.0).astype(BF16)
+    for copy in copies[3:]:
+        copy.wait()
     rest = D - HALF_W
-    out[:, :rest] = (
+    packed[:, :rest] = (
         dot(p_l, patches[:, :rest])
         + dot(u_l, upstream[:, :rest])
         + dot(p_r, patches[:, HALF_W:])
         + dot(u_r, upstream[:, HALF_W:])
     ).astype(BF16)
-    out[:, rest:] = (dot(p_l, patches[:, rest:HALF_W]) + dot(u_l, upstream[:, rest:HALF_W])).astype(BF16)
-    for copy in copies:
-        copy.wait()
-
-
-def unpack_rows_kernel(got, out):
+    packed[:, rest:] = (dot(p_l, patches[:, rest:HALF_W]) + dot(u_l, upstream[:, rest:HALF_W])).astype(BF16)
+    done = pltpu.make_async_copy(packed, out, out_sem)
+    done.start()
+    done.wait()
+
+
+def unpack_rows_kernel(got_in, out, got, sems):
     part = 256
+    copies = start_copies(
+        [(got_in.at[pl.ds(g * part, part), :], got.at[pl.ds(g * part, part), :]) for g in range(SEND // part)], sems
+    )
     o = lax.broadcasted_iota(I32, (128, part), 0)
     c = lax.broadcasted_iota(I32, (128, part), 1)
     want = ((o & 63) >> 1) * 8 + (o >> 6) * 2 + (o & 1)
     for g in range(SEND // part):
+        copies[g].wait()
         block = got[pl.ds(g * part, part), :]
         for h in range(2):
             sel = jnp.where(c == want + 4 * h, 1.0, 0.0).astype(BF16)
@@ -98,19 +123,30 @@
     return value * up, slope
 
 
-def expert_kernel(rows, w0, w1, w2, w3, part, pg_out, hid_out):
+def turn_kernel(in0, in1, out0, out1, in_turned, out_turned):
+    for turned, parts in ((in_turned, (in0, in1)), (out_turned, (out0, out1))):
+        for k, part in enumerate(parts):
+            turned[:, pl.ds(k * PAD, HS)] = part[...].T
+            turned[:, pl.ds(k * PAD + HS, PAD - HS)] = jnp.zeros((D, PAD - HS), BF16)
+
+
+def expert_kernel(rows, t_in0, t_in1, t_out0, t_out1, w0, w1, w2, w3, part, pg_out, hid_out):
     p, u = rows[pl.ds(0, ROWS), :], rows[pl.ds(ROWS, ROWS), :]
     gate = jnp.zeros((ROWS, 1), F32)
-    total = jnp.zeros((ROWS, D), F32)
-    for c, w in enumerate((w0, w1, w2, w3)):
-        pre = dot_width(p, w[pl.ds(0, HS), :])
-        back = dot_width(u, w[pl.ds(HS, HS), :])
+    grads = []
+    for c, (t_in, t_out) in enumerate(((t_in0, t_out0), (t_in1, t_out1))):
+        pre = dot(p, t_in[...])
+        back = dot(u, t_out[...])
         hid, slope = gelu_and_slope(pre)
         gate += jnp.sum(hid * back, axis=1, keepdims=True)
         pg = (back * slope).astype(BF16)
-        pg_out[c] = pg
-        hid_out[c] = hid.astype(BF16)
-        total += dot(pg, w[pl.ds(0, HS), :])
+        hid = hid.astype(BF16)
+        for k in range(2):
+            own = slice(k * PAD, k * PAD + HS)
+            pg_out[2 * c + k] = pg[:, own]
+            hid_out[2 * c + k] = hid[:, own]
+            grads.append(pg[:, own])
+    total = sum(dot(grad, w[...]) for grad, w in zip(grads, (w0, w1, w2, w3)))
     part[:, :D] = total.astype(BF16)
     lane = lax.broadcasted_iota(I32, (ROWS, 128), 1)
     part[:, D:] = jnp.where(lane == 0, gate, 0.0).astype(BF16)
@@ -125,20 +161,23 @@
     )
 
 
-def weight_kernel(c, kind, add, *refs):
+def weight_kernel(c, add, *refs):
     out = refs[-1]
     grad_in, grad_out = weight_grads(c, *refs[:6])
     if add:
         got = refs[6]
         grad_in += got[pl.ds(0, HS), :].astype(F32)
         grad_out += got[pl.ds(HS, HS), :].astype(F32)
-    out[pl.ds(0, HS), :] = grad_in.astype(kind)
-    out[pl.ds(HS, HS), :] = grad_out.astype(kind)
-
-
-def weight_sum_kernel(own, got, grad_in, grad_out):
-    grad_in[...] = (own[pl.ds(0, HS), :] + got[pl.ds(0, HS), :].astype(F32)).astype(BF16)
-    grad_out[...] = (own[pl.ds(HS, HS), :] + got[pl.ds(HS, HS), :].astype(F32)).astype(BF16)
+    out[pl.ds(0, HS), :] = grad_in.astype(BF16)
+    out[pl.ds(HS, HS), :] = grad_out.astype(BF16)
+
+
+def last_weight_kernel(*refs):
+    near, far, out_in, out_out = refs[6:]
+    grad_in, grad_out = weight_grads(0, *refs[:6])
+    top, low = pl.ds(0, HS), pl.ds(HS, HS)
+    out_in[...] = (grad_in + near[top, :].astype(F32) + far[top, :].astype(F32)).astype(BF16)
+    out_out[...] = (grad_out + near[low, :].astype(F32) + far[low, :].astype(F32)).astype(BF16)
 
 
 def pack_back_kernel(i0, i1, out):
@@ -175,6 +214,7 @@
 
 
 ANY = pl.BlockSpec(memory_space=pl.ANY)
+HBM = pl.BlockSpec(memory_space=pltpu.HBM)
 VM = pl.BlockSpec(memory_space=pltpu.VMEM)
 
 
@@ -210,50 +250,83 @@
     everywhere = ("zlo", "y", "zhi")
     gates, ids, slots = gates.T, ids.T, slots.T
     both = shape((2 * HS, D))
-    sent, w00 = call(
+    wi00, wo00 = in_weights[0], out_weights[0]
+    wi01, wo01 = swap_weights(wi00), swap_weights(wo00)
+    wi10, wo10 = swap_core(wi00), swap_core(wo00)
+    sent = call(
         pack_rows_kernel,
-        [shape((SEND, HALF_W)), both],
-        (patches, upstream, gates, ids, slots, in_weights[0], out_weights[0]),
+        shape((SEND, HALF_W)),
+        (gates, ids, slots, patches, upstream),
         500_000_000,
         5_000_000,
+        60,
+        in_specs=[HBM] * 5,
+        out_specs=HBM,
+        scratch=[
+            pltpu.VMEM((2, T), BF16),
+            pltpu.VMEM((2, T), I32),
+            pltpu.VMEM((2, T), I32),
+            pltpu.VMEM((T, D), BF16),
+            pltpu.VMEM((T, D), BF16),
+            pltpu.VMEM((SEND, HALF_W), BF16),
+            pltpu.SemaphoreType.DMA((5,)),
+            pltpu.SemaphoreType.DMA,
+        ],
+    )
+    got = lax.all_to_all(sent, everywhere, split_axis=0, concat_axis=0, tiled=True)
+    own = call(
+        unpack_rows_kernel,
+        shape((2 * ROWS, D)),
+        (got,),
+        300_000_000,
+        2_000_000,
         16,
-        in_specs=[VM] * 5 + [ANY] * 2,
-        out_specs=[VM, ANY],
-        scratch=[pltpu.SemaphoreType.DMA((2,))],
-    )
-    w01 = swap_weights(w00)
-    got = lax.all_to_all(sent, everywhere, split_axis=0, concat_axis=0, tiled=True)
-    own = call(unpack_rows_kernel, shape((2 * ROWS, D)), (got,), 300_000_000, 2_000_000, 16)
+        in_specs=[HBM],
+        scratch=[pltpu.VMEM((SEND, HALF_W), BF16), pltpu.SemaphoreType.DMA((2,))],
+    )
     other = swap_rows(own)
-    w10, w11 = swap_core(w00), swap_core(w01)
+    wi11, wo11 = swap_core(wi01), swap_core(wo01)
     hidden = shape((4, ROWS, HS))
-    expert_out = [shape((ROWS, GW)), hidden, hidden]
-    weights = (w00, w10, w01, w11)
-    part_own, pg_own, hid_own = call(expert_kernel, expert_out, (own, *weights), 1_100_000_000, 8_000_000, 24)
-    part_other, pg_other, hid_other = call(
-        expert_kernel, expert_out, (other, *weights), 1_100_000_000, 8_000_000, 24
-    )
+    turned = shape((D, 2 * PAD))
+
+    def turn_call(*args):
+        return call(turn_kernel, [turned, turned], args, 1_000_000, 5_000_000, 16)
+
+    t_in0, t_out0 = turn_call(wi00, wi10, wo00, wo10)
+    t_in1, t_out1 = turn_call(wi01, wi11, wo01, wo11)
+
+    def expert_call(rows):
+        return call(
+            expert_kernel,
+            [shape((ROWS, GW)), hidden, hidden],
+            (rows, t_in0, t_in1, t_out0, t_out1, wi00, wi10, wi01, wi11),
+            1_100_000_000,
+            8_000_000,
+            16,
+        )
+
+    part_own, pg_own, hid_own = expert_call(own)
+    part_other, pg_other, hid_other = expert_call(other)
     part_back = swap_rows(part_other)
     saved = (own, other, pg_own, pg_other, hid_own, hid_other)
 
-    def weight_call(c, kind, add=()):
+    def weight_call(c, *add):
         return call(
-            functools.partial(weight_kernel, c, kind, len(add)),
-            shape((2 * HS, D), kind),
-            (*saved, *add),
-            700_000_000,
-            4_000_000,
-            24,
+            functools.partial(weight_kernel, c, len(add)), both, (*saved, *add), 700_000_000, 4_000_000, 16
         )
 
-    far = swap_core(weight_call(3, BF16))
-    near = swap_core(weight_call(1, BF16))
-    far = swap_weights(weight_call(2, BF16, (far,)))
-    near = weight_call(0, F32, (near,))
+    far = swap_core(weight_call(3))
+    near = swap_core(weight_call(1))
+    far = swap_weights(weight_call(2, far))
     back = call(pack_back_kernel, shape((SEND, QW)), (part_own, part_back), 300_000_000, 2_500_000, 16)
     back = lax.all_to_all(back, everywhere, split_axis=0, concat_axis=0, tiled=True)
     grad_in, grad_out = call(
-        weight_sum_kernel, [shape((HS, D)), shape((HS, D))], (near, far), 1_000_000, 6_000_000, 16
+        last_weight_kernel,
+        [shape((HS, D)), shape((HS, D))],
+        (*saved, near, far),
+        700_000_000,
+        6_000_000,
+        16,
     )
     patch_grad, gate_grad = call(
         unpack_back_kernel,

time: 140 us -> 122 us (0.87)
  blocking collectives: 0 us -> 28.2 us
  waiting for transfers between devices: 52.9 us -> 28.8 us
  local copies, waits for them, and re-layouts: 11.7 us -> 0.03 us
  Pallas kernels: 24.8 us -> 17.7 us
  starting transfers between devices: 47.9 us -> 45 us
    all_to_all x0 -> x1, blocking collectives: none -> 28.2 us  [local(): lax.all_to_all(back, everywhere, split_axis=0, concat_axis=0, tiled=True)]
    ppermute x8 -> x11, waiting for transfers between devices: 26.7 us -> 7.42 us  [swap(): lax.ppermute(value, axis, [(i, partner(i)) for i in range(lax.axis_size(a...]
    all_to_all x1 -> x0, waiting for transfers between devices: 16.4 us -> none  [local(): lax.all_to_all(back, everywhere, split_axis=0, concat_axis=0, tiled=True)]
    unnamed x42 -> x10, local copies, waits for them, and re-layouts: 11.7 us -> 0.03 us
    all_to_all x1, waiting for transfers between devices: 9.83 us -> 21.4 us  [local(): lax.all_to_all(sent, everywhere, split_axis=0, concat_axis=0, tiled=True)]
    all_to_all x1 -> x0, starting transfers between devices: 11.3 us -> none  [local(): lax.all_to_all(back, everywhere, split_axis=0, concat_axis=0, tiled=True)]
    pallas_call x11 -> x12, Pallas kernels: 24.8 us -> 17.7 us  [call(): pl.pallas_call(kernel, out_shape=out_shape, in_specs=in_specs or [VM] * l...]
    all_to_all x1, starting transfers between devices: 11.2 us -> 16.6 us  [local(): lax.all_to_all(sent, everywhere, split_axis=0, concat_axis=0, tiled=True)]
  transfers between devices with their start and end apart: 10 -> 12, of which waited for: 5 -> 4; matrix products, arithmetic and copies ran while one was open for 0% -> 0% of each run, Pallas kernels for 11% -> 8%
where the time goes in v3:
time: 122 us; the launch traced here: 121 us
  starting transfers between devices  45 us (37%)
  waiting for transfers between devices  28.8 us (24%)
  blocking collectives  28.2 us (23%)
  Pallas kernels  17.7 us (15%)
    ppermute x11, starting transfers between devices, swap(): lax.ppermute(value, axis, [(i, partner(i)) for i in range(lax.axis_size(a...  28.4 us
    all_to_all x1, blocking collectives, local(): lax.all_to_all(back, everywhere, split_axis=0, concat_axis=0, tiled=True)  28.2 us
    all_to_all x1, waiting for transfers between devices, local(): lax.all_to_all(sent, everywhere, split_axis=0, concat_axis=0, tiled=True)  21.4 us
    pallas_call x12, Pallas kernels, call(): pl.pallas_call(kernel, out_shape=out_shape, in_specs=in_specs or [VM] * l...  17.7 us
    all_to_all x1, starting transfers between devices, local(): lax.all_to_all(sent, everywhere, split_axis=0, concat_axis=0, tiled=True)  16.6 us
    ppermute x11, waiting for transfers between devices, swap(): lax.ppermute(value, axis, [(i, partner(i)) for i in range(lax.axis_size(a...  7.42 us
  transfers between devices with their start and end apart: 12, of which 4 were waited for; matrix products, arithmetic and copies ran while one was open for 0% of the time, Pallas kernels for 8%

profile of v3, /device:TPU:6, one launch (start us, length us, event | category | flops | bytes accessed | tf_op | source)
XLA Modules:
  0.0 120.7 jit_solution(17697492505069829923)
XLA Ops:
  0.6 0.0 copy-start
  0.6 0.0 copy-start.1
  0.7 3.3 %shard_map.102 = bf16[512,896]{1,0:T(8,128)(2,1)} custom-call(bf16[2,128]{1,0:T(2,128)(2,1)} %bitcast.27, s32[2,128]{1,0:T(2,128)} %bitcast.23, s32[2,128]{1,0:T(2,128)} %bitcast.25, bf16[128,1664]{1,0:T(8,128)(2,1)} %patches_in.1, bf16[128,1664]{1,0:T(8,128)(2,1)} %upstream_in.1), custom_call_target="tpu_custom_call" | custom-call | flops 500000000 | bytes 5000000 | tf_op jit(solution)/shard_map/pallas_call | solution.py:222
  4.0 16.6 %all-to-all-start = ((bf16[64,8,896]{2,1,0:T(8,128)(2,1)}), bf16[64,8,896]{2,1,0:T(8,128)(2,1)S(1)}, u32[]{:S(2)}, u32[]{:S(2)}) async-start(bf16[64,8,896]{2,1,0:T(8,128)(2,1)} %bitcast.29), calls=%async_computation | async-start | bytes 1835008 | tf_op jit(solution)/shard_map/all_to_all | solution.py:276
  20.6 0.0 copy-done
  20.6 2.4 %collective-permute-start.2 = (bf16[208,1664]{1,0:T(8,128)(2,1)S(1)}, bf16[208,1664]{1,0:T(8,128)(2,1)S(1)}, u32[]{:S(2)}, u32[]{:S(2)}) collective-permute-start(bf16[208,1664]{1,0:T(8,128)(2,1)S(1)} %bitcast.12), channel_id=1, source_target_pairs={{0,12},{4,8},{8,4},{12,0},{1,13},{5,9},{9,5},{13,1},{2,14},{6,10},... | collective-permute-start | bytes 2076680 | tf_op jit(solution)/shard_map/ppermute | solution.py:234
  23.0 0.0 copy-done.1
  23.0 4.7 %collective-permute-start.4 = (bf16[208,1664]{1,0:T(8,128)(2,1)S(1)}, bf16[208,1664]{1,0:T(8,128)(2,1)}, u32[]{:S(2)}, u32[]{:S(2)}) collective-permute-start(bf16[208,1664]{1,0:T(8,128)(2,1)S(1)} %bitcast.19), channel_id=1, source_target_pairs={{0,12},{4,8},{8,4},{12,0},{1,13},{5,9},{9,5},{13,1},{2,14},{6,10},... | collective-permute-start | bytes 2076680 | tf_op jit(solution)/shard_map/ppermute | solution.py:234
  27.7 21.4 %all-to-all-done = bf16[64,8,896]{2,1,0:T(8,128)(2,1)S(1)} async-done(((bf16[64,8,896]{2,1,0:T(8,128)(2,1)}), bf16[64,8,896]{2,1,0:T(8,128)(2,1)S(1)}, u32[]{:S(2)}, u32[]{:S(2)}) %all-to-all-start) | async-done | bytes 917536 | tf_op jit(solution)/shard_map/all_to_all | solution.py:276
  49.1 1.2 shard_map.103.rows.refs_0_
  50.3 2.8 %collective-permute-start.6 = (bf16[256,1664]{1,0:T(8,128)(2,1)S(1)}, bf16[256,1664]{1,0:T(8,128)(2,1)S(1)}, u32[]{:S(2)}, u32[]{:S(2)}) collective-permute-start(bf16[256,1664]{1,0:T(8,128)(2,1)S(1)} %shard_map.103.rows.refs_0_), channel_id=1, source_target_pairs={{0,4},{4,0},{8,12},{12,8},{1,5},{5,1},{9,13},{13,9},{2,6},{6,2},{1... | collective-permute-start | bytes 2555912 | tf_op jit(solution)/shard_map/ppermute | solution.py:234
  53.0 1.9 %collective-permute-start = (bf16[208,1664]{1,0:T(8,128)(2,1)S(1)}, bf16[208,1664]{1,0:T(8,128)(2,1)S(1)}, u32[]{:S(2)}, u32[]{:S(2)}) collective-permute-start(bf16[208,1664]{1,0:T(8,128)(2,1)S(1)} %bitcast.13), channel_id=1, source_target_pairs={{0,2},{2,0},{1,3},{3,1},{4,6},{6,4},{5,7},{7,5},{8,10},{10,8},{9,1... | collective-permute-start | bytes 2076680 | tf_op jit(solution)/shard_map/ppermute | solution.py:234
  55.0 2.4 %collective-permute-start.1 = (bf16[208,1664]{1,0:T(8,128)(2,1)S(1)}, bf16[208,1664]{1,0:T(8,128)(2,1)S(1)}, u32[]{:S(2)}, u32[]{:S(2)}) collective-permute-start(bf16[208,1664]{1,0:T(8,128)(2,1)S(1)} %bitcast.20), channel_id=1, source_target_pairs={{0,2},{2,0},{1,3},{3,1},{4,6},{6,4},{5,7},{7,5},{8,10},{10,8},{9,1... | collective-permute-start | bytes 2076680 | tf_op jit(solution)/shard_map/ppermute | solution.py:234
  57.4 0.0 collective-permute-done.2.in0.w2
  57.4 1.9 %collective-permute-start.3 = (bf16[208,1664]{1,0:T(8,128)(2,1)S(1)}, bf16[208,1664]{1,0:T(8,128)(2,1)S(1)}, u32[]{:S(2)}, u32[]{:S(2)}) collective-permute-start(bf16[208,1664]{1,0:T(8,128)(2,1)S(1)} %collective-permute-done.2.in0.w2), channel_id=1, source_target_pairs={{0,2},{2,0},{1,3},{3,1},{4,6},{6,4},{5,7},{7,5},{8,10},{10,8},{9,1... | collective-permute-start | bytes 2076680 | tf_op jit(solution)/shard_map/ppermute | solution.py:234
  59.3 0.0 collective-permute-done.4.out0
  59.3 2.4 %collective-permute-start.5 = (bf16[208,1664]{1,0:T(8,128)(2,1)}, bf16[208,1664]{1,0:T(8,128)(2,1)S(1)}, u32[]{:S(2)}, u32[]{:S(2)}) collective-permute-start(bf16[208,1664]{1,0:T(8,128)(2,1)} %collective-permute-done.4.out0), channel_id=1, source_target_pairs={{0,2},{2,0},{1,3},{3,1},{4,6},{6,4},{5,7},{7,5},{8,10},{10,8},{9,1... | collective-permute-start | bytes 2076680 | tf_op jit(solution)/shard_map/ppermute | solution.py:234
  61.7 0.0 collective-permute-done.in1.w1
  61.7 0.0 collective-permute-done.1.out1
  61.8 1.0 shard_map.104
  62.8 0.0 collective-permute-done.3.in1.w3
  62.8 0.9 collective-permute-done.5.out1
  63.7 2.1 %shard_map.105 = (bf16[1664,512]{1,0:T(8,128)(2,1)S(1)}, bf16[1664,512]{1,0:T(8,128)(2,1)S(1)}) custom-call(bf16[208,1664]{1,0:T(8,128)(2,1)S(1)} %collective-permute-done.2.in0.w2, bf16[208,1664]{1,0:T(8,128)(2,1)S(1)} %collective-permute-done.3.in1.w3, bf16[208,1664]{1,0:T(8,128)(2,1)} %collective-permute-done.4.out0, ...), custom_call_target="tpu_custom_call" | custom-call | flops 1000000 | bytes 5000000 | tf_op jit(solution)/shard_map/pallas_call | solution.py:222
  65.8 1.7 %shard_map.106 = (bf16[128,1792]{1,0:T(8,128)(2,1)S(1)}, bf16[4,128,208]{2,1,0:T(8,128)(2,1)S(1)}, bf16[4,128,208]{2,1,0:T(8,128)(2,1)S(1)}) custom-call(bf16[256,1664]{1,0:T(8,128)(2,1)S(1)} %shard_map.103.rows.refs_0_, bf16[1664,512]{1,0:T(8,128)(2,1)S(1)} %get-tuple-element.18.t_in0, bf16[1664,512]{1,0:T(8,128)(2,1)S(1)} %get-tuple-element.19.t_in1, ...), custom_call_target="tpu_custom_call" | custom-call | flops 1100000000 | bytes 8000000 | tf_op jit(solution)/shard_map/pallas_call | solution.py:222
  67.5 1.7 %collective-permute-done.6.rows.refs_1_ = bf16[256,1664]{1,0:T(8,128)(2,1)S(1)} collective-permute-done((bf16[256,1664]{1,0:T(8,128)(2,1)S(1)}, bf16[256,1664]{1,0:T(8,128)(2,1)S(1)}, u32[]{:S(2)}, u32[]{:S(2)}) %collective-permute-start.6) | collective-permute-done | bytes 852000 | tf_op jit(solution)/shard_map/ppermute | solution.py:234
  69.2 1.7 %shard_map.107 = (bf16[128,1792]{1,0:T(8,128)(2,1)S(1)}, bf16[4,128,208]{2,1,0:T(8,128)(2,1)S(1)}, bf16[4,128,208]{2,1,0:T(8,128)(2,1)S(1)}) custom-call(bf16[256,1664]{1,0:T(8,128)(2,1)S(1)} %collective-permute-done.6.rows.refs_1_, bf16[1664,512]{1,0:T(8,128)(2,1)S(1)} %get-tuple-element.18.t_in0, bf16[1664,512]{1,0:T(8,128)(2,1)S(1)} %get-tuple-element.19.t_in1, ...), custom_call_target="tpu_custom_call" | custom-call | flops 1100000000 | bytes 8000000 | tf_op jit(solution)/shard_map/pallas_call | solution.py:222
  70.8 1.0 shard_map.111
  71.8 1.9 %collective-permute-start.9 = (bf16[416,1664]{1,0:T(8,128)(2,1)S(1)}, bf16[416,1664]{1,0:T(8,128)(2,1)S(1)}, u32[]{:S(2)}, u32[]{:S(2)}) collective-permute-start(bf16[416,1664]{1,0:T(8,128)(2,1)S(1)} %shard_map.111), channel_id=1, source_target_pairs={{0,2},{2,0},{1,3},{3,1},{4,6},{6,4},{5,7},{7,5},{8,10},{10,8},{9,1... | collective-permute-start | bytes 4153352 | tf_op jit(solution)/shard_map/ppermute | solution.py:234
  73.7 2.7 %collective-permute-start.7 = (bf16[128,1792]{1,0:T(8,128)(2,1)S(1)}, bf16[128,1792]{1,0:T(8,128)(2,1)S(1)}, u32[]{:S(2)}, u32[]{:S(2)}) collective-permute-start(bf16[128,1792]{1,0:T(8,128)(2,1)S(1)} %get-tuple-element.23), channel_id=1, source_target_pairs={{0,4},{4,0},{8,12},{12,8},{1,5},{5,1},{9,13},{13,9},{2,6},{6,2},{1... | collective-permute-start | bytes 1376264 | tf_op jit(solution)/shard_map/ppermute | solution.py:234
  76.5 1.0 shard_map.110
  77.4 2.1 %collective-permute-start.8 = (bf16[416,1664]{1,0:T(8,128)(2,1)S(1)}, bf16[416,1664]{1,0:T(8,128)(2,1)S(1)}, u32[]{:S(2)}, u32[]{:S(2)}) collective-permute-start(bf16[416,1664]{1,0:T(8,128)(2,1)S(1)} %shard_map.110), channel_id=1, source_target_pairs={{0,2},{2,0},{1,3},{3,1},{4,6},{6,4},{5,7},{7,5},{8,10},{10,8},{9,1... | collective-permute-start | bytes 4153352 | tf_op jit(solution)/shard_map/ppermute | solution.py:234
  79.6 0.0 collective-permute-done.9.refs_6_
  79.6 1.0 shard_map.112
  80.5 0.0 copy-start.2
  80.6 0.0 copy-start.3
  80.6 0.0 copy-start.4
  80.6 3.2 %collective-permute-start.10 = (bf16[416,1664]{1,0:T(8,128)(2,1)S(1)}, bf16[416,1664]{1,0:T(8,128)(2,1)S(1)}, u32[]{:S(2)}, u32[]{:S(2)}) collective-permute-start(bf16[416,1664]{1,0:T(8,128)(2,1)S(1)} %shard_map.112), channel_id=1, source_target_pairs={{0,12},{4,8},{8,4},{12,0},{1,13},{5,9},{9,5},{13,1},{2,14},{6,10},... | collective-permute-start | bytes 4153352 | tf_op jit(solution)/shard_map/ppermute | solution.py:234
  83.8 4.8 %collective-permute-done.7.i1 = bf16[128,1792]{1,0:T(8,128)(2,1)S(1)} collective-permute-done((bf16[128,1792]{1,0:T(8,128)(2,1)S(1)}, bf16[128,1792]{1,0:T(8,128)(2,1)S(1)}, u32[]{:S(2)}, u32[]{:S(2)}) %collective-permute-start.7) | collective-permute-done | bytes 458784 | tf_op jit(solution)/shard_map/ppermute | solution.py:234
  88.6 0.7 shard_map.108
  89.2 28.2 %all_to_all.22 = bf16[64,8,512]{2,1,0:T(8,128)(2,1)S(1)} all-to-all(bf16[64,8,512]{2,1,0:T(8,128)(2,1)S(1)} %bitcast.18), channel_id=1, replica_groups=mesh['zlo'=4,'y'=8,'x'=4,'core'=2,'zhi'=2] {'zlo','y','zhi'}, dimensions={0} | all-to-all | bytes 1048576 | tf_op jit(solution)/shard_map/all_to_all | solution.py:322
  117.4 0.0 copy-done.2
  117.4 0.0 copy-done.3
  117.4 0.0 copy-done.4
  117.4 1.3 %shard_map.109 = (bf16[128,1664]{1,0:T(8,128)(2,1)}, f32[2,128]{1,0:T(2,128)}) custom-call(bf16[512,512]{1,0:T(8,128)(2,1)S(1)} %bitcast.22, bf16[2,128]{1,0:T(2,128)(2,1)S(1)} %bitcast.28, s32[2,128]{1,0:T(2,128)S(1)} %bitcast.24, s32[2,128]{1,0:T(2,128)S(1)} %bitcast.26), custom_call_target="tpu_custom_call" | custom-call | flops 300000000 | bytes 1000000 | tf_op jit(solution)/shard_map/pallas_call | solution.py:222
  118.7 0.0 collective-permute-done.8.refs_6_
  118.8 0.0 collective-permute-done.10.refs_7_
  118.8 1.9 %shard_map.113 = (bf16[208,1664]{1,0:T(8,128)(2,1)}, bf16[208,1664]{1,0:T(8,128)(2,1)}) custom-call(bf16[256,1664]{1,0:T(8,128)(2,1)S(1)} %shard_map.103.rows.refs_0_, bf16[256,1664]{1,0:T(8,128)(2,1)S(1)} %collective-permute-done.6.rows.refs_1_, bf16[4,128,208]{2,1,0:T(8,128)(2,1)S(1)} %get-tuple-element.26.refs_2_, ...), custom_call_target="tpu_custom_call" | custom-call | flops 700000000 | bytes 6000000 | tf_op jit(solution)/shard_map/pallas_call | solution.py:222
Async XLA Ops:
  0.6 20.0 %copy-start = (bf16[1,208,1664]{2,1,0:T(8,128)(2,1)S(1)}, bf16[1,208,1664]{2,1,0:T(8,128)(2,1)}, u32[]{:S(2)}) copy-start(bf16[1,208,1664]{2,1,0:T(8,128)(2,1)} %param.12) | copy-start | bytes 2076676
  0.6 22.3 %copy-start.1 = (bf16[1,208,1664]{2,1,0:T(8,128)(2,1)S(1)}, bf16[1,208,1664]{2,1,0:T(8,128)(2,1)}, u32[]{:S(2)}) copy-start(bf16[1,208,1664]{2,1,0:T(8,128)(2,1)} %param.13) | copy-start | bytes 2076676
  4.0 45.1 %all-to-all-start = ((bf16[64,8,896]{2,1,0:T(8,128)(2,1)}), bf16[64,8,896]{2,1,0:T(8,128)(2,1)S(1)}, u32[]{:S(2)}, u32[]{:S(2)}) async-start(bf16[64,8,896]{2,1,0:T(8,128)(2,1)} %bitcast.29), calls=%async_computation | async-start | bytes 1835008 | tf_op jit(solution)/shard_map/all_to_all | solution.py:276
  20.6 36.8 %collective-permute-start.2 = (bf16[208,1664]{1,0:T(8,128)(2,1)S(1)}, bf16[208,1664]{1,0:T(8,128)(2,1)S(1)}, u32[]{:S(2)}, u32[]{:S(2)}) collective-permute-start(bf16[208,1664]{1,0:T(8,128)(2,1)S(1)} %bitcast.12), channel_id=1, source_target_pairs={{0,12},{4,8},{8,4},{12,0},{1,13},{5,9},{9,5},{13,1},{2,14},{6,10},... | collective-permute-start | bytes 2076680 | tf_op jit(solution)/shard_map/ppermute | solution.py:234
  23.0 36.3 %collective-permute-start.4 = (bf16[208,1664]{1,0:T(8,128)(2,1)S(1)}, bf16[208,1664]{1,0:T(8,128)(2,1)}, u32[]{:S(2)}, u32[]{:S(2)}) collective-permute-start(bf16[208,1664]{1,0:T(8,128)(2,1)S(1)} %bitcast.19), channel_id=1, source_target_pairs={{0,12},{4,8},{8,4},{12,0},{1,13},{5,9},{9,5},{13,1},{2,14},{6,10},... | collective-permute-start | bytes 2076680 | tf_op jit(solution)/shard_map/ppermute | solution.py:234
  50.3 18.9 %collective-permute-start.6 = (bf16[256,1664]{1,0:T(8,128)(2,1)S(1)}, bf16[256,1664]{1,0:T(8,128)(2,1)S(1)}, u32[]{:S(2)}, u32[]{:S(2)}) collective-permute-start(bf16[256,1664]{1,0:T(8,128)(2,1)S(1)} %shard_map.103.rows.refs_0_), channel_id=1, source_target_pairs={{0,4},{4,0},{8,12},{12,8},{1,5},{5,1},{9,13},{13,9},{2,6},{6,2},{1... | collective-permute-start | bytes 2555912 | tf_op jit(solution)/shard_map/ppermute | solution.py:234
  53.0 8.7 %collective-permute-start = (bf16[208,1664]{1,0:T(8,128)(2,1)S(1)}, bf16[208,1664]{1,0:T(8,128)(2,1)S(1)}, u32[]{:S(2)}, u32[]{:S(2)}) collective-permute-start(bf16[208,1664]{1,0:T(8,128)(2,1)S(1)} %bitcast.13), channel_id=1, source_target_pairs={{0,2},{2,0},{1,3},{3,1},{4,6},{6,4},{5,7},{7,5},{8,10},{10,8},{9,1... | collective-permute-start | bytes 2076680 | tf_op jit(solution)/shard_map/ppermute | solution.py:234
  55.0 6.8 %collective-permute-start.1 = (bf16[208,1664]{1,0:T(8,128)(2,1)S(1)}, bf16[208,1664]{1,0:T(8,128)(2,1)S(1)}, u32[]{:S(2)}, u32[]{:S(2)}) collective-permute-start(bf16[208,1664]{1,0:T(8,128)(2,1)S(1)} %bitcast.20), channel_id=1, source_target_pairs={{0,2},{2,0},{1,3},{3,1},{4,6},{6,4},{5,7},{7,5},{8,10},{10,8},{9,1... | collective-permute-start | bytes 2076680 | tf_op jit(solution)/shard_map/ppermute | solution.py:234
  57.4 5.4 %collective-permute-start.3 = (bf16[208,1664]{1,0:T(8,128)(2,1)S(1)}, bf16[208,1664]{1,0:T(8,128)(2,1)S(1)}, u32[]{:S(2)}, u32[]{:S(2)}) collective-permute-start(bf16[208,1664]{1,0:T(8,128)(2,1)S(1)} %collective-permute-done.2.in0.w2), channel_id=1, source_target_pairs={{0,2},{2,0},{1,3},{3,1},{4,6},{6,4},{5,7},{7,5},{8,10},{10,8},{9,1... | collective-permute-start | bytes 2076680 | tf_op jit(solution)/shard_map/ppermute | solution.py:234
  59.3 4.4 %collective-permute-start.5 = (bf16[208,1664]{1,0:T(8,128)(2,1)}, bf16[208,1664]{1,0:T(8,128)(2,1)S(1)}, u32[]{:S(2)}, u32[]{:S(2)}) collective-permute-start(bf16[208,1664]{1,0:T(8,128)(2,1)} %collective-permute-done.4.out0), channel_id=1, source_target_pairs={{0,2},{2,0},{1,3},{3,1},{4,6},{6,4},{5,7},{7,5},{8,10},{10,8},{9,1... | collective-permute-start | bytes 2076680 | tf_op jit(solution)/shard_map/ppermute | solution.py:234
  71.8 7.8 %collective-permute-start.9 = (bf16[416,1664]{1,0:T(8,128)(2,1)S(1)}, bf16[416,1664]{1,0:T(8,128)(2,1)S(1)}, u32[]{:S(2)}, u32[]{:S(2)}) collective-permute-start(bf16[416,1664]{1,0:T(8,128)(2,1)S(1)} %shard_map.111), channel_id=1, source_target_pairs={{0,2},{2,0},{1,3},{3,1},{4,6},{6,4},{5,7},{7,5},{8,10},{10,8},{9,1... | collective-permute-start | bytes 4153352 | tf_op jit(solution)/shard_map/ppermute | solution.py:234
  73.7 14.8 %collective-permute-start.7 = (bf16[128,1792]{1,0:T(8,128)(2,1)S(1)}, bf16[128,1792]{1,0:T(8,128)(2,1)S(1)}, u32[]{:S(2)}, u32[]{:S(2)}) collective-permute-start(bf16[128,1792]{1,0:T(8,128)(2,1)S(1)} %get-tuple-element.23), channel_id=1, source_target_pairs={{0,4},{4,0},{8,12},{12,8},{1,5},{5,1},{9,13},{13,9},{2,6},{6,2},{1... | collective-permute-start | bytes 1376264 | tf_op jit(solution)/shard_map/ppermute | solution.py:234
  77.4 41.3 %collective-permute-start.8 = (bf16[416,1664]{1,0:T(8,128)(2,1)S(1)}, bf16[416,1664]{1,0:T(8,128)(2,1)S(1)}, u32[]{:S(2)}, u32[]{:S(2)}) collective-permute-start(bf16[416,1664]{1,0:T(8,128)(2,1)S(1)} %shard_map.110), channel_id=1, source_target_pairs={{0,2},{2,0},{1,3},{3,1},{4,6},{6,4},{5,7},{7,5},{8,10},{10,8},{9,1... | collective-permute-start | bytes 4153352 | tf_op jit(solution)/shard_map/ppermute | solution.py:234
  80.5 36.9 %copy-start.2 = (s32[128,2]{0,1:T(2,128)S(1)}, s32[128,2]{0,1:T(2,128)}, u32[]{:S(2)}) copy-start(s32[128,2]{0,1:T(2,128)} %param.10) | copy-start | bytes 3076
  80.6 36.9 %copy-start.3 = (s32[128,2]{0,1:T(2,128)S(1)}, s32[128,2]{0,1:T(2,128)}, u32[]{:S(2)}) copy-start(s32[128,2]{0,1:T(2,128)} %param.11) | copy-start | bytes 3076
  80.6 36.9 %copy-start.4 = (bf16[128,2]{0,1:T(2,128)(2,1)S(1)}, bf16[128,2]{0,1:T(2,128)(2,1)}, u32[]{:S(2)}) copy-start(bf16[128,2]{0,1:T(2,128)(2,1)} %param.9) | copy-start | bytes 1540
  80.6 38.2 %collective-permute-start.10 = (bf16[416,1664]{1,0:T(8,128)(2,1)S(1)}, bf16[416,1664]{1,0:T(8,128)(2,1)S(1)}, u32[]{:S(2)}, u32[]{:S(2)}) collective-permute-start(bf16[416,1664]{1,0:T(8,128)(2,1)S(1)} %shard_map.112), channel_id=1, source_target_pairs={{0,12},{4,8},{8,4},{12,0},{1,13},{5,9},{9,5},{13,1},{2,14},{6,10},... | collective-permute-start | bytes 4153352 | tf_op jit(solution)/shard_map/ppermute | solution.py:234

commit v4 on v3

--- a/solution.py
+++ b/solution.py
@@ -55,13 +55,13 @@
 
 def pack_rows_kernel(
     gates_in, ids_in, slots_in, patches_in, upstream_in, out,
-    gates, ids, slots, patches, upstream, packed, sems, out_sem,
+    gates, ids, slots, patches, upstream, packed, sems, out_sems,
 ):
     copies = start_copies(
         [
-            (gates_in, gates),
             (ids_in, ids),
             (slots_in, slots),
+            (gates_in, gates),
             (patches_in, patches),
             (upstream_in, upstream),
         ],
@@ -84,16 +84,23 @@
     for copy in copies[3:]:
         copy.wait()
     rest = D - HALF_W
-    packed[:, :rest] = (
-        dot(p_l, patches[:, :rest])
-        + dot(u_l, upstream[:, :rest])
-        + dot(p_r, patches[:, HALF_W:])
-        + dot(u_r, upstream[:, HALF_W:])
-    ).astype(BF16)
-    packed[:, rest:] = (dot(p_l, patches[:, rest:HALF_W]) + dot(u_l, upstream[:, rest:HALF_W])).astype(BF16)
-    done = pltpu.make_async_copy(packed, out, out_sem)
-    done.start()
-    done.wait()
+    sent = []
+    for half in range(2):
+        rows = slice(half * SEND // 2, (half + 1) * SEND // 2)
+        place = pl.ds(half * SEND // 2, SEND // 2)
+        packed[place, :rest] = (
+            dot(p_l[rows], patches[:, :rest])
+            + dot(u_l[rows], upstream[:, :rest])
+            + dot(p_r[rows], patches[:, HALF_W:])
+            + dot(u_r[rows], upstream[:, HALF_W:])
+        ).astype(BF16)
+        packed[place, rest:] = (
+            dot(p_l[rows], patches[:, rest:HALF_W]) + dot(u_l[rows], upstream[:, rest:HALF_W])
+        ).astype(BF16)
+        sent.append(pltpu.make_async_copy(packed.at[place, :], out.at[place, :], out_sems.at[half]))
+        sent[-1].start()
+    for copy in sent:
+        copy.wait()
 
 
 def unpack_rows_kernel(got_in, out, got, sems):
@@ -172,12 +179,9 @@
     out[pl.ds(HS, HS), :] = grad_out.astype(BF16)
 
 
-def last_weight_kernel(*refs):
-    near, far, out_in, out_out = refs[6:]
-    grad_in, grad_out = weight_grads(0, *refs[:6])
-    top, low = pl.ds(0, HS), pl.ds(HS, HS)
-    out_in[...] = (grad_in + near[top, :].astype(F32) + far[top, :].astype(F32)).astype(BF16)
-    out_out[...] = (grad_out + near[low, :].astype(F32) + far[low, :].astype(F32)).astype(BF16)
+def weight_sum_kernel(near, far, out_in, out_out):
+    out_in[...] = (near[pl.ds(0, HS), :].astype(F32) + far[pl.ds(0, HS), :].astype(F32)).astype(BF16)
+    out_out[...] = (near[pl.ds(HS, HS), :].astype(F32) + far[pl.ds(HS, HS), :].astype(F32)).astype(BF16)
 
 
 def pack_back_kernel(i0, i1, out):
@@ -194,7 +198,8 @@
     out[:, last:] = wide.astype(BF16)
 
 
-def unpack_back_kernel(got, gates, ids, slots, patch_grad, gate_grad):
+def unpack_back_kernel(got, gates, ids, slots, patch_grad, gate_grad, token):
+    token[...] = jnp.zeros_like(token)
     m0, m1, row = slot_match(ids[...], slots[...])
     quarter = (row >> 1) & 3
     hit = jnp.where(m0 | m1, 1.0, 0.0)
@@ -218,16 +223,21 @@
 VM = pl.BlockSpec(memory_space=pltpu.VMEM)
 
 
-def call(kernel, out_shape, args, flops, moved, vmem, in_specs=None, out_specs=None, scratch=()):
+def call(kernel, out_shape, args, flops, moved, vmem, in_specs=None, out_specs=None, scratch=(), after=()):
+    used = len(args)
+
+    def body(*refs):
+        kernel(*refs[:used], *refs[used + len(after) :])
+
     return pl.pallas_call(
-        kernel,
+        body,
         out_shape=out_shape,
-        in_specs=in_specs or [VM] * len(args),
+        in_specs=(in_specs or [VM] * used) + [ANY] * len(after),
         out_specs=out_specs or jax.tree.map(lambda _: VM, out_shape),
         scratch_shapes=scratch,
         compiler_params=pltpu.CompilerParams(vmem_limit_bytes=vmem * 1024 * 1024),
         cost_estimate=pl.CostEstimate(flops=flops, bytes_accessed=moved, transcendentals=0),
-    )(*args)
+    )(*args, *after)
 
 
 def swap(value, axis, partner):
@@ -270,7 +280,7 @@
             pltpu.VMEM((T, D), BF16),
             pltpu.VMEM((SEND, HALF_W), BF16),
             pltpu.SemaphoreType.DMA((5,)),
-            pltpu.SemaphoreType.DMA,
+            pltpu.SemaphoreType.DMA((2,)),
         ],
     )
     got = lax.all_to_all(sent, everywhere, split_axis=0, concat_axis=0, tiled=True)
@@ -283,6 +293,7 @@
         16,
         in_specs=[HBM],
         scratch=[pltpu.VMEM((SEND, HALF_W), BF16), pltpu.SemaphoreType.DMA((2,))],
+        after=(wo10,),
     )
     other = swap_rows(own)
     wi11, wo11 = swap_core(wi01), swap_core(wo01)
@@ -310,31 +321,33 @@
     part_back = swap_rows(part_other)
     saved = (own, other, pg_own, pg_other, hid_own, hid_other)
 
-    def weight_call(c, *add):
+    def weight_call(c, add=(), after=()):
         return call(
-            functools.partial(weight_kernel, c, len(add)), both, (*saved, *add), 700_000_000, 4_000_000, 16
+            functools.partial(weight_kernel, c, len(add)),
+            both,
+            (*saved, *add),
+            700_000_000,
+            4_000_000,
+            16,
+            after=after,
         )
 
-    far = swap_core(weight_call(3))
+    far = weight_call(2, (swap_core(weight_call(3)),))
     near = swap_core(weight_call(1))
-    far = swap_weights(weight_call(2, far))
+    far = swap_weights(far)
     back = call(pack_back_kernel, shape((SEND, QW)), (part_own, part_back), 300_000_000, 2_500_000, 16)
     back = lax.all_to_all(back, everywhere, split_axis=0, concat_axis=0, tiled=True)
-    grad_in, grad_out = call(
-        last_weight_kernel,
-        [shape((HS, D)), shape((HS, D))],
-        (*saved, near, far),
-        700_000_000,
-        6_000_000,
-        16,
-    )
-    patch_grad, gate_grad = call(
+    patch_grad, gate_grad, token = call(
         unpack_back_kernel,
-        [shape((T, D)), shape((2, T), F32)],
+        [shape((T, D)), shape((2, T), F32), shape((8, 128), F32)],
         (back, gates, ids, slots),
         300_000_000,
         1_000_000,
         16,
+    )
+    near = weight_call(0, (near,), (token,))
+    grad_in, grad_out = call(
+        weight_sum_kernel, [shape((HS, D))] * 2, (near, far), 1_000_000, 4_000_000, 16
     )
     return patch_grad, gate_grad.T, grad_in[None], grad_out[None]
 

time: 122 us -> 123 us (level)
  blocking collectives: 28.2 us -> 30 us
  Pallas kernels: 17.7 us -> 19 us
    all_to_all x1, waiting for transfers between devices: 21.4 us -> 19.5 us  [local(): lax.all_to_all(sent, everywhere, split_axis=0, concat_axis=0, tiled=True)]
    all_to_all x1, blocking collectives: 28.2 us -> 30 us  [local(): lax.all_to_all(back, everywhere, split_axis=0, concat_axis=0, tiled=True)]
    ppermute x11, waiting for transfers between devices: 7.42 us -> 8.78 us  [swap(): lax.ppermute(value, axis, [(i, partner(i)) for i in range(lax.axis_size(a...]
    pallas_call x12 -> x13, Pallas kernels: 17.7 us -> 19 us  [call(): pl.pallas_call(body, out_shape=out_shape, in_specs=(in_specs or [VM] * us...]
  transfers between devices with their start and end apart: 12 -> 12, of which waited for: 4 -> 5; matrix products, arithmetic and copies ran while one was open for 0% -> 0% of each run, Pallas kernels for 8% -> 10%
where the time goes in v4:
time: 123 us
  starting transfers between devices  44.5 us (36%)
  blocking collectives  30 us (24%)
  waiting for transfers between devices  28.2 us (23%)
  Pallas kernels  19 us (15%)
    all_to_all x1, blocking collectives, local(): lax.all_to_all(back, everywhere, split_axis=0, concat_axis=0, tiled=True)  30 us
    ppermute x11, starting transfers between devices, swap(): lax.ppermute(value, axis, [(i, partner(i)) for i in range(lax.axis_size(a...  27.9 us
    all_to_all x1, waiting for transfers between devices, local(): lax.all_to_all(sent, everywhere, split_axis=0, concat_axis=0, tiled=True)  19.5 us
    pallas_call x13, Pallas kernels, call(): pl.pallas_call(body, out_shape=out_shape, in_specs=(in_specs or [VM] * us...  19 us
    all_to_all x1, starting transfers between devices, local(): lax.all_to_all(sent, everywhere, split_axis=0, concat_axis=0, tiled=True)  16.6 us
    ppermute x11, waiting for transfers between devices, swap(): lax.ppermute(value, axis, [(i, partner(i)) for i in range(lax.axis_size(a...  8.78 us
  transfers between devices with their start and end apart: 12, of which 5 were waited for; matrix products, arithmetic and copies ran while one was open for 0% of the time, Pallas kernels for 10%

profile of v4, /device:TPU:6, one launch (start us, length us, event | category | flops | bytes accessed | tf_op | source)
XLA Modules:
  0.0 122.6 jit_solution(6154679231846652661)
XLA Ops:
  0.6 0.0 copy-start
  0.6 3.2 %shard_map.102 = bf16[512,896]{1,0:T(8,128)(2,1)} custom-call(bf16[2,128]{1,0:T(2,128)(2,1)} %bitcast.24, s32[2,128]{1,0:T(2,128)} %bitcast.20, s32[2,128]{1,0:T(2,128)} %bitcast.22, bf16[128,1664]{1,0:T(8,128)(2,1)} %refs_3_.1, bf16[128,1664]{1,0:T(8,128)(2,1)} %refs_4_.1), custom_call_target="tpu_custom_call" | custom-call | flops 500000000 | bytes 5000000 | tf_op jit(solution)/shard_map/pallas_call | solution.py:232
  3.9 16.6 %all-to-all-start = ((bf16[64,8,896]{2,1,0:T(8,128)(2,1)}), bf16[64,8,896]{2,1,0:T(8,128)(2,1)S(1)}, u32[]{:S(2)}, u32[]{:S(2)}) async-start(bf16[64,8,896]{2,1,0:T(8,128)(2,1)} %bitcast.26), calls=%async_computation | async-start | bytes 1835008 | tf_op jit(solution)/shard_map/all_to_all | solution.py:286
  20.5 1.9 %collective-permute-start = (bf16[208,1664]{1,0:T(8,128)(2,1)}, bf16[208,1664]{1,0:T(8,128)(2,1)S(1)}, u32[]{:S(2)}, u32[]{:S(2)}) collective-permute-start(bf16[208,1664]{1,0:T(8,128)(2,1)} %bitcast.5.refs_2_), channel_id=1, source_target_pairs={{0,2},{2,0},{1,3},{3,1},{4,6},{6,4},{5,7},{7,5},{8,10},{10,8},{9,1... | collective-permute-start | bytes 2076680 | tf_op jit(solution)/shard_map/ppermute | solution.py:244
  22.4 0.0 copy-done
  22.4 2.4 %collective-permute-start.2 = (bf16[208,1664]{1,0:T(8,128)(2,1)S(1)}, bf16[208,1664]{1,0:T(8,128)(2,1)S(1)}, u32[]{:S(2)}, u32[]{:S(2)}) collective-permute-start(bf16[208,1664]{1,0:T(8,128)(2,1)S(1)} %bitcast.12), channel_id=1, source_target_pairs={{0,12},{4,8},{8,4},{12,0},{1,13},{5,9},{9,5},{13,1},{2,14},{6,10},... | collective-permute-start | bytes 2076680 | tf_op jit(solution)/shard_map/ppermute | solution.py:244
  24.8 4.7 %collective-permute-start.4 = (bf16[208,1664]{1,0:T(8,128)(2,1)}, bf16[208,1664]{1,0:T(8,128)(2,1)}, u32[]{:S(2)}, u32[]{:S(2)}) collective-permute-start(bf16[208,1664]{1,0:T(8,128)(2,1)} %bitcast.5.refs_2_), channel_id=1, source_target_pairs={{0,12},{4,8},{8,4},{12,0},{1,13},{5,9},{9,5},{13,1},{2,14},{6,10},... | collective-permute-start | bytes 2076680 | tf_op jit(solution)/shard_map/ppermute | solution.py:244
  29.5 0.0 collective-permute-done.refs_1_.refs_3_
  29.5 19.5 %all-to-all-done = bf16[64,8,896]{2,1,0:T(8,128)(2,1)S(1)} async-done(((bf16[64,8,896]{2,1,0:T(8,128)(2,1)}), bf16[64,8,896]{2,1,0:T(8,128)(2,1)S(1)}, u32[]{:S(2)}, u32[]{:S(2)}) %all-to-all-start) | async-done | bytes 917536 | tf_op jit(solution)/shard_map/all_to_all | solution.py:286
  49.0 1.2 shard_map.103.refs_0_
  50.2 2.7 %collective-permute-start.6 = (bf16[256,1664]{1,0:T(8,128)(2,1)S(1)}, bf16[256,1664]{1,0:T(8,128)(2,1)S(1)}, u32[]{:S(2)}, u32[]{:S(2)}) collective-permute-start(bf16[256,1664]{1,0:T(8,128)(2,1)S(1)} %shard_map.103.refs_0_), channel_id=1, source_target_pairs={{0,4},{4,0},{8,12},{12,8},{1,5},{5,1},{9,13},{13,9},{2,6},{6,2},{1... | collective-permute-start | bytes 2555912 | tf_op jit(solution)/shard_map/ppermute | solution.py:244
  52.9 1.9 %collective-permute-start.1 = (bf16[208,1664]{1,0:T(8,128)(2,1)S(1)}, bf16[208,1664]{1,0:T(8,128)(2,1)S(1)}, u32[]{:S(2)}, u32[]{:S(2)}) collective-permute-start(bf16[208,1664]{1,0:T(8,128)(2,1)S(1)} %bitcast.13), channel_id=1, source_target_pairs={{0,2},{2,0},{1,3},{3,1},{4,6},{6,4},{5,7},{7,5},{8,10},{10,8},{9,1... | collective-permute-start | bytes 2076680 | tf_op jit(solution)/shard_map/ppermute | solution.py:244
  54.8 0.0 collective-permute-done.2.refs_0_.refs_7_
  54.8 2.4 %collective-permute-start.3 = (bf16[208,1664]{1,0:T(8,128)(2,1)S(1)}, bf16[208,1664]{1,0:T(8,128)(2,1)S(1)}, u32[]{:S(2)}, u32[]{:S(2)}) collective-permute-start(bf16[208,1664]{1,0:T(8,128)(2,1)S(1)} %collective-permute-done.2.refs_0_.refs_7_), channel_id=1, source_target_pairs={{0,2},{2,0},{1,3},{3,1},{4,6},{6,4},{5,7},{7,5},{8,10},{10,8},{9,1... | collective-permute-start | bytes 2076680 | tf_op jit(solution)/shard_map/ppermute | solution.py:244
  57.3 1.1 collective-permute-done.4.refs_2_
  58.4 1.9 %collective-permute-start.5 = (bf16[208,1664]{1,0:T(8,128)(2,1)}, bf16[208,1664]{1,0:T(8,128)(2,1)S(1)}, u32[]{:S(2)}, u32[]{:S(2)}) collective-permute-start(bf16[208,1664]{1,0:T(8,128)(2,1)} %collective-permute-done.4.refs_2_), channel_id=1, source_target_pairs={{0,2},{2,0},{1,3},{3,1},{4,6},{6,4},{5,7},{7,5},{8,10},{10,8},{9,1... | collective-permute-start | bytes 2076680 | tf_op jit(solution)/shard_map/ppermute | solution.py:244
  60.3 0.0 collective-permute-done.1.refs_1_.refs_6_
  60.3 2.1 %shard_map.104 = (bf16[1664,512]{1,0:T(8,128)(2,1)S(1)}, bf16[1664,512]{1,0:T(8,128)(2,1)S(1)}) custom-call(bf16[208,1664]{1,0:T(8,128)(2,1)S(1)} %bitcast.14, bf16[208,1664]{1,0:T(8,128)(2,1)S(1)} %collective-permute-done.1.refs_1_.refs_6_, bf16[208,1664]{1,0:T(8,128)(2,1)} %bitcast.5.refs_2_, bf16[208,1664]{1,0:T(8,128)(2,1)S(1)} %collective-permute-done.refs_1_.refs_3_), custom_call_target="tpu_custom_call" | custom-call | flops 1000000 | bytes 5000000 | tf_op jit(solution)/shard_map/pallas_call | solution.py:232
  62.4 0.0 collective-permute-done.3.refs_1_.refs_8_
  62.4 0.2 collective-permute-done.5.refs_3_
  62.6 2.1 %shard_map.105 = (bf16[1664,512]{1,0:T(8,128)(2,1)S(1)}, bf16[1664,512]{1,0:T(8,128)(2,1)S(1)}) custom-call(bf16[208,1664]{1,0:T(8,128)(2,1)S(1)} %collective-permute-done.2.refs_0_.refs_7_, bf16[208,1664]{1,0:T(8,128)(2,1)S(1)} %collective-permute-done.3.refs_1_.refs_8_, bf16[208,1664]{1,0:T(8,128)(2,1)} %collective-permute-done.4.refs_2_, ...), custom_call_target="tpu_custom_call" | custom-call | flops 1000000 | bytes 5000000 | tf_op jit(solution)/shard_map/pallas_call | solution.py:232
  64.7 1.7 %shard_map.106 = (bf16[128,1792]{1,0:T(8,128)(2,1)S(1)}, bf16[4,128,208]{2,1,0:T(8,128)(2,1)S(1)}, bf16[4,128,208]{2,1,0:T(8,128)(2,1)S(1)}) custom-call(bf16[256,1664]{1,0:T(8,128)(2,1)S(1)} %shard_map.103.refs_0_, bf16[1664,512]{1,0:T(8,128)(2,1)S(1)} %get-tuple-element.19.refs_1_, bf16[1664,512]{1,0:T(8,128)(2,1)S(1)} %get-tuple-element.20.refs_2_, ...), custom_call_target="tpu_custom_call" | custom-call | flops 1100000000 | bytes 8000000 | tf_op jit(solution)/shard_map/pallas_call | solution.py:232
  66.4 2.7 %collective-permute-done.6.refs_0_.refs_1_ = bf16[256,1664]{1,0:T(8,128)(2,1)S(1)} collective-permute-done((bf16[256,1664]{1,0:T(8,128)(2,1)S(1)}, bf16[256,1664]{1,0:T(8,128)(2,1)S(1)}, u32[]{:S(2)}, u32[]{:S(2)}) %collective-permute-start.6) | collective-permute-done | bytes 852000 | tf_op jit(solution)/shard_map/ppermute | solution.py:244
  69.1 1.7 %shard_map.107 = (bf16[128,1792]{1,0:T(8,128)(2,1)S(1)}, bf16[4,128,208]{2,1,0:T(8,128)(2,1)S(1)}, bf16[4,128,208]{2,1,0:T(8,128)(2,1)S(1)}) custom-call(bf16[256,1664]{1,0:T(8,128)(2,1)S(1)} %collective-permute-done.6.refs_0_.refs_1_, bf16[1664,512]{1,0:T(8,128)(2,1)S(1)} %get-tuple-element.19.refs_1_, bf16[1664,512]{1,0:T(8,128)(2,1)S(1)} %get-tuple-element.20.refs_2_, ...), custom_call_target="tpu_custom_call" | custom-call | flops 1100000000 | bytes 8000000 | tf_op jit(solution)/shard_map/pallas_call | solution.py:232
  70.7 1.0 shard_map.112
  71.7 1.9 %collective-permute-start.9 = (bf16[416,1664]{1,0:T(8,128)(2,1)S(1)}, bf16[416,1664]{1,0:T(8,128)(2,1)S(1)}, u32[]{:S(2)}, u32[]{:S(2)}) collective-permute-start(bf16[416,1664]{1,0:T(8,128)(2,1)S(1)} %shard_map.112), channel_id=1, source_target_pairs={{0,2},{2,0},{1,3},{3,1},{4,6},{6,4},{5,7},{7,5},{8,10},{10,8},{9,1... | collective-permute-start | bytes 4153352 | tf_op jit(solution)/shard_map/ppermute | solution.py:244
  73.6 2.7 %collective-permute-start.7 = (bf16[128,1792]{1,0:T(8,128)(2,1)S(1)}, bf16[128,1792]{1,0:T(8,128)(2,1)S(1)}, u32[]{:S(2)}, u32[]{:S(2)}) collective-permute-start(bf16[128,1792]{1,0:T(8,128)(2,1)S(1)} %get-tuple-element.24), channel_id=1, source_target_pairs={{0,4},{4,0},{8,12},{12,8},{1,5},{5,1},{9,13},{13,9},{2,6},{6,2},{1... | collective-permute-start | bytes 1376264 | tf_op jit(solution)/shard_map/ppermute | solution.py:244
  76.4 1.0 shard_map.110
  77.3 2.1 %collective-permute-start.8 = (bf16[416,1664]{1,0:T(8,128)(2,1)S(1)}, bf16[416,1664]{1,0:T(8,128)(2,1)S(1)}, u32[]{:S(2)}, u32[]{:S(2)}) collective-permute-start(bf16[416,1664]{1,0:T(8,128)(2,1)S(1)} %shard_map.110), channel_id=1, source_target_pairs={{0,2},{2,0},{1,3},{3,1},{4,6},{6,4},{5,7},{7,5},{8,10},{10,8},{9,1... | collective-permute-start | bytes 4153352 | tf_op jit(solution)/shard_map/ppermute | solution.py:244
  79.5 0.0 collective-permute-done.9.refs_6_
  79.5 1.0 shard_map.113
  80.4 0.0 copy-start.1
  80.5 0.0 copy-start.2
  80.5 0.0 copy-start.3
  80.5 3.2 %collective-permute-start.10 = (bf16[416,1664]{1,0:T(8,128)(2,1)S(1)}, bf16[416,1664]{1,0:T(8,128)(2,1)S(1)}, u32[]{:S(2)}, u32[]{:S(2)}) collective-permute-start(bf16[416,1664]{1,0:T(8,128)(2,1)S(1)} %shard_map.113), channel_id=1, source_target_pairs={{0,12},{4,8},{8,4},{12,0},{1,13},{5,9},{9,5},{13,1},{2,14},{6,10},... | collective-permute-start | bytes 4153352 | tf_op jit(solution)/shard_map/ppermute | solution.py:244
  83.7 4.8 %collective-permute-done.7.refs_1_ = bf16[128,1792]{1,0:T(8,128)(2,1)S(1)} collective-permute-done((bf16[128,1792]{1,0:T(8,128)(2,1)S(1)}, bf16[128,1792]{1,0:T(8,128)(2,1)S(1)}, u32[]{:S(2)}, u32[]{:S(2)}) %collective-permute-start.7) | collective-permute-done | bytes 458784 | tf_op jit(solution)/shard_map/ppermute | solution.py:244
  88.4 0.7 shard_map.108
  89.1 30.0 %all_to_all.22 = bf16[64,8,512]{2,1,0:T(8,128)(2,1)S(1)} all-to-all(bf16[64,8,512]{2,1,0:T(8,128)(2,1)S(1)} %bitcast.18), channel_id=1, replica_groups=mesh['zlo'=4,'y'=8,'x'=4,'core'=2,'zhi'=2] {'zlo','y','zhi'}, dimensions={0} | all-to-all | bytes 1048576 | tf_op jit(solution)/shard_map/all_to_all | solution.py:339
  119.1 0.0 copy-done.1
  119.1 0.0 copy-done.2
  119.1 0.0 copy-done.3
  119.1 1.3 %shard_map.109 = (bf16[128,1664]{1,0:T(8,128)(2,1)}, f32[2,128]{1,0:T(2,128)}, f32[8,128]{1,0:T(8,128)S(1)}) custom-call(bf16[512,512]{1,0:T(8,128)(2,1)S(1)} %bitcast.19, bf16[2,128]{1,0:T(2,128)(2,1)S(1)} %bitcast.25, s32[2,128]{1,0:T(2,128)S(1)} %bitcast.21, s32[2,128]{1,0:T(2,128)S(1)} %bitcast.23), custom_call_target="tpu_custom_call" | custom-call | flops 300000000 | bytes 1000000 | tf_op jit(solution)/shard_map/pallas_call | solution.py:232
  120.4 0.0 collective-permute-done.8.refs_6_
  120.4 1.0 shard_map.111.refs_0_
  121.4 0.0 collective-permute-done.10.refs_1_
  121.4 1.2 %shard_map.114 = (bf16[208,1664]{1,0:T(8,128)(2,1)}, bf16[208,1664]{1,0:T(8,128)(2,1)}) custom-call(bf16[416,1664]{1,0:T(8,128)(2,1)S(1)} %shard_map.111.refs_0_, bf16[416,1664]{1,0:T(8,128)(2,1)S(1)} %collective-permute-done.10.refs_1_), custom_call_target="tpu_custom_call" | custom-call | flops 1000000 | bytes 4000000 | tf_op jit(solution)/shard_map/pallas_call | solution.py:232
Async XLA Ops:
  0.6 21.8 %copy-start = (bf16[1,208,1664]{2,1,0:T(8,128)(2,1)S(1)}, bf16[1,208,1664]{2,1,0:T(8,128)(2,1)}, u32[]{:S(2)}) copy-start(bf16[1,208,1664]{2,1,0:T(8,128)(2,1)} %param.12) | copy-start | bytes 2076676
  3.9 45.1 %all-to-all-start = ((bf16[64,8,896]{2,1,0:T(8,128)(2,1)}), bf16[64,8,896]{2,1,0:T(8,128)(2,1)S(1)}, u32[]{:S(2)}, u32[]{:S(2)}) async-start(bf16[64,8,896]{2,1,0:T(8,128)(2,1)} %bitcast.26), calls=%async_computation | async-start | bytes 1835008 | tf_op jit(solution)/shard_map/all_to_all | solution.py:286
  20.5 9.0 %collective-permute-start = (bf16[208,1664]{1,0:T(8,128)(2,1)}, bf16[208,1664]{1,0:T(8,128)(2,1)S(1)}, u32[]{:S(2)}, u32[]{:S(2)}) collective-permute-start(bf16[208,1664]{1,0:T(8,128)(2,1)} %bitcast.5.refs_2_), channel_id=1, source_target_pairs={{0,2},{2,0},{1,3},{3,1},{4,6},{6,4},{5,7},{7,5},{8,10},{10,8},{9,1... | collective-permute-start | bytes 2076680 | tf_op jit(solution)/shard_map/ppermute | solution.py:244
  22.4 32.4 %collective-permute-start.2 = (bf16[208,1664]{1,0:T(8,128)(2,1)S(1)}, bf16[208,1664]{1,0:T(8,128)(2,1)S(1)}, u32[]{:S(2)}, u32[]{:S(2)}) collective-permute-start(bf16[208,1664]{1,0:T(8,128)(2,1)S(1)} %bitcast.12), channel_id=1, source_target_pairs={{0,12},{4,8},{8,4},{12,0},{1,13},{5,9},{9,5},{13,1},{2,14},{6,10},... | collective-permute-start | bytes 2076680 | tf_op jit(solution)/shard_map/ppermute | solution.py:244
  24.8 33.6 %collective-permute-start.4 = (bf16[208,1664]{1,0:T(8,128)(2,1)}, bf16[208,1664]{1,0:T(8,128)(2,1)}, u32[]{:S(2)}, u32[]{:S(2)}) collective-permute-start(bf16[208,1664]{1,0:T(8,128)(2,1)} %bitcast.5.refs_2_), channel_id=1, source_target_pairs={{0,12},{4,8},{8,4},{12,0},{1,13},{5,9},{9,5},{13,1},{2,14},{6,10},... | collective-permute-start | bytes 2076680 | tf_op jit(solution)/shard_map/ppermute | solution.py:244
  50.2 18.9 %collective-permute-start.6 = (bf16[256,1664]{1,0:T(8,128)(2,1)S(1)}, bf16[256,1664]{1,0:T(8,128)(2,1)S(1)}, u32[]{:S(2)}, u32[]{:S(2)}) collective-permute-start(bf16[256,1664]{1,0:T(8,128)(2,1)S(1)} %shard_map.103.refs_0_), channel_id=1, source_target_pairs={{0,4},{4,0},{8,12},{12,8},{1,5},{5,1},{9,13},{13,9},{2,6},{6,2},{1... | collective-permute-start | bytes 2555912 | tf_op jit(solution)/shard_map/ppermute | solution.py:244
  52.9 7.4 %collective-permute-start.1 = (bf16[208,1664]{1,0:T(8,128)(2,1)S(1)}, bf16[208,1664]{1,0:T(8,128)(2,1)S(1)}, u32[]{:S(2)}, u32[]{:S(2)}) collective-permute-start(bf16[208,1664]{1,0:T(8,128)(2,1)S(1)} %bitcast.13), channel_id=1, source_target_pairs={{0,2},{2,0},{1,3},{3,1},{4,6},{6,4},{5,7},{7,5},{8,10},{10,8},{9,1... | collective-permute-start | bytes 2076680 | tf_op jit(solution)/shard_map/ppermute | solution.py:244
  54.8 7.6 %collective-permute-start.3 = (bf16[208,1664]{1,0:T(8,128)(2,1)S(1)}, bf16[208,1664]{1,0:T(8,128)(2,1)S(1)}, u32[]{:S(2)}, u32[]{:S(2)}) collective-permute-start(bf16[208,1664]{1,0:T(8,128)(2,1)S(1)} %collective-permute-done.2.refs_0_.refs_7_), channel_id=1, source_target_pairs={{0,2},{2,0},{1,3},{3,1},{4,6},{6,4},{5,7},{7,5},{8,10},{10,8},{9,1... | collective-permute-start | bytes 2076680 | tf_op jit(solution)/shard_map/ppermute | solution.py:244
  58.4 4.2 %collective-permute-start.5 = (bf16[208,1664]{1,0:T(8,128)(2,1)}, bf16[208,1664]{1,0:T(8,128)(2,1)S(1)}, u32[]{:S(2)}, u32[]{:S(2)}) collective-permute-start(bf16[208,1664]{1,0:T(8,128)(2,1)} %collective-permute-done.4.refs_2_), channel_id=1, source_target_pairs={{0,2},{2,0},{1,3},{3,1},{4,6},{6,4},{5,7},{7,5},{8,10},{10,8},{9,1... | collective-permute-start | bytes 2076680 | tf_op jit(solution)/shard_map/ppermute | solution.py:244
  71.7 7.8 %collective-permute-start.9 = (bf16[416,1664]{1,0:T(8,128)(2,1)S(1)}, bf16[416,1664]{1,0:T(8,128)(2,1)S(1)}, u32[]{:S(2)}, u32[]{:S(2)}) collective-permute-start(bf16[416,1664]{1,0:T(8,128)(2,1)S(1)} %shard_map.112), channel_id=1, source_target_pairs={{0,2},{2,0},{1,3},{3,1},{4,6},{6,4},{5,7},{7,5},{8,10},{10,8},{9,1... | collective-permute-start | bytes 4153352 | tf_op jit(solution)/shard_map/ppermute | solution.py:244
  73.6 14.8 %collective-permute-start.7 = (bf16[128,1792]{1,0:T(8,128)(2,1)S(1)}, bf16[128,1792]{1,0:T(8,128)(2,1)S(1)}, u32[]{:S(2)}, u32[]{:S(2)}) collective-permute-start(bf16[128,1792]{1,0:T(8,128)(2,1)S(1)} %get-tuple-element.24), channel_id=1, source_target_pairs={{0,4},{4,0},{8,12},{12,8},{1,5},{5,1},{9,13},{13,9},{2,6},{6,2},{1... | collective-permute-start | bytes 1376264 | tf_op jit(solution)/shard_map/ppermute | solution.py:244
  77.3 43.1 %collective-permute-start.8 = (bf16[416,1664]{1,0:T(8,128)(2,1)S(1)}, bf16[416,1664]{1,0:T(8,128)(2,1)S(1)}, u32[]{:S(2)}, u32[]{:S(2)}) collective-permute-start(bf16[416,1664]{1,0:T(8,128)(2,1)S(1)} %shard_map.110), channel_id=1, source_target_pairs={{0,2},{2,0},{1,3},{3,1},{4,6},{6,4},{5,7},{7,5},{8,10},{10,8},{9,1... | collective-permute-start | bytes 4153352 | tf_op jit(solution)/shard_map/ppermute | solution.py:244
  80.4 38.7 %copy-start.1 = (s32[128,2]{0,1:T(2,128)S(1)}, s32[128,2]{0,1:T(2,128)}, u32[]{:S(2)}) copy-start(s32[128,2]{0,1:T(2,128)} %param.10) | copy-start | bytes 3076
  80.5 38.6 %copy-start.2 = (s32[128,2]{0,1:T(2,128)S(1)}, s32[128,2]{0,1:T(2,128)}, u32[]{:S(2)}) copy-start(s32[128,2]{0,1:T(2,128)} %param.11) | copy-start | bytes 3076
  80.5 38.6 %copy-start.3 = (bf16[128,2]{0,1:T(2,128)(2,1)S(1)}, bf16[128,2]{0,1:T(2,128)(2,1)}, u32[]{:S(2)}) copy-start(bf16[128,2]{0,1:T(2,128)(2,1)} %param.9) | copy-start | bytes 1540
  80.5 40.9 %collective-permute-start.10 = (bf16[416,1664]{1,0:T(8,128)(2,1)S(1)}, bf16[416,1664]{1,0:T(8,128)(2,1)S(1)}, u32[]{:S(2)}, u32[]{:S(2)}) collective-permute-start(bf16[416,1664]{1,0:T(8,128)(2,1)S(1)} %shard_map.113), channel_id=1, source_target_pairs={{0,12},{4,8},{8,4},{12,0},{1,13},{5,9},{9,5},{13,1},{2,14},{6,10},... | collective-permute-start | bytes 4153352 | tf_op jit(solution)/shard_map/ppermute | solution.py:244

commit v5 on v4

--- a/solution.py
+++ b/solution.py
@@ -20,11 +20,10 @@
 HS = 208
 SRC = 64
 ROWS = SRC * CAP
-SEND = SRC * 8
 PAD = 256
-HALF_W = 896
-QW = 512
 GW = D + 128
+SEND_BLOCKS = D // 128
+BACK_BLOCKS = GW // 128
 
 
 def dot(left, right):
@@ -39,10 +38,10 @@
     return lax.dot_general(left, right, (((1,), (1,)), ((), ())), preferred_element_type=F32)
 
 
-def slot_match(ids, slots):
+def slot_match(ids, slots, per):
     target = jnp.where(slots >= 0, ids * CAP + slots, -1)
-    row = lax.broadcasted_iota(I32, (SEND, T), 0)
-    slot = (row >> 4) * CAP + (row & 1)
+    row = lax.broadcasted_iota(I32, (SRC * per, T), 0)
+    slot = row // (2 * per) * CAP + (row & 1)
     return target[0:1, :] == slot, target[1:2, :] == slot, row
 
 
@@ -69,57 +68,41 @@
     )
     for copy in copies[:3]:
         copy.wait()
-    m0, m1, row = slot_match(ids[...], slots[...])
+    m0, m1, row = slot_match(ids[...], slots[...], 4)
     g = gates[...].astype(F32)
-    hit = jnp.where(m0 | m1, 1.0, 0.0)
     gate = jnp.where(m0, g[0:1, :], 0.0) + jnp.where(m1, g[1:2, :], 0.0)
     is_up = (row & 2) != 0
-    right = (row & 4) != 0
-    p_sel = jnp.where(is_up, 0.0, hit)
-    u_sel = jnp.where(is_up, gate, 0.0)
-    p_l = jnp.where(right, 0.0, p_sel).astype(BF16)
-    p_r = jnp.where(right, p_sel, 0.0).astype(BF16)
-    u_l = jnp.where(right, 0.0, u_sel).astype(BF16)
-    u_r = jnp.where(right, u_sel, 0.0).astype(BF16)
+    p_sel = jnp.where(is_up, 0.0, jnp.where(m0 | m1, 1.0, 0.0)).astype(BF16)
+    u_sel = jnp.where(is_up, gate, 0.0).astype(BF16)
     for copy in copies[3:]:
         copy.wait()
-    rest = D - HALF_W
     sent = []
     for half in range(2):
-        rows = slice(half * SEND // 2, (half + 1) * SEND // 2)
-        place = pl.ds(half * SEND // 2, SEND // 2)
-        packed[place, :rest] = (
-            dot(p_l[rows], patches[:, :rest])
-            + dot(u_l[rows], upstream[:, :rest])
-            + dot(p_r[rows], patches[:, HALF_W:])
-            + dot(u_r[rows], upstream[:, HALF_W:])
-        ).astype(BF16)
-        packed[place, rest:] = (
-            dot(p_l[rows], patches[:, rest:HALF_W]) + dot(u_l[rows], upstream[:, rest:HALF_W])
-        ).astype(BF16)
-        sent.append(pltpu.make_async_copy(packed.at[place, :], out.at[place, :], out_sems.at[half]))
+        part = SRC // 2
+        rows = slice(half * part * 4, (half + 1) * part * 4)
+        filled = (dot(p_sel[rows], patches[...]) + dot(u_sel[rows], upstream[...])).astype(BF16)
+        place = pl.ds(half * part, part)
+        for j in range(SEND_BLOCKS):
+            packed[place, j] = filled[:, j * 128 : (j + 1) * 128].reshape(part, 4, 128)
+        sent.append(pltpu.make_async_copy(packed.at[place], out.at[place], out_sems.at[half]))
         sent[-1].start()
     for copy in sent:
         copy.wait()
 
 
-def unpack_rows_kernel(got_in, out, got, sems):
-    part = 256
-    copies = start_copies(
-        [(got_in.at[pl.ds(g * part, part), :], got.at[pl.ds(g * part, part), :]) for g in range(SEND // part)], sems
-    )
-    o = lax.broadcasted_iota(I32, (128, part), 0)
-    c = lax.broadcasted_iota(I32, (128, part), 1)
-    want = ((o & 63) >> 1) * 8 + (o >> 6) * 2 + (o & 1)
-    for g in range(SEND // part):
+def unpack_rows_kernel(got_in, out, got, rows, sems):
+    part = SRC // 2
+    copies = start_copies([(got_in.at[pl.ds(g * part, part)], got.at[pl.ds(g * part, part)]) for g in range(2)], sems)
+    o = lax.broadcasted_iota(I32, (2 * ROWS, 4 * SRC), 0)
+    c = lax.broadcasted_iota(I32, (2 * ROWS, 4 * SRC), 1)
+    want = ((o & (ROWS - 1)) >> 1) * 4 + o // ROWS * 2 + (o & 1)
+    sel = jnp.where(c == want, 1.0, 0.0).astype(BF16)
+    for g in range(2):
         copies[g].wait()
-        block = got[pl.ds(g * part, part), :]
-        for h in range(2):
-            sel = jnp.where(c == want + 4 * h, 1.0, 0.0).astype(BF16)
-            wide = HALF_W if h == 0 else D - HALF_W
-            rows = dot(sel, block[:, :wide]).astype(BF16)
-            out[pl.ds(g * 64, 64), pl.ds(h * HALF_W, wide)] = rows[:64]
-            out[pl.ds(ROWS + g * 64, 64), pl.ds(h * HALF_W, wide)] = rows[64:]
+        for j in range(SEND_BLOCKS):
+            block = got[pl.ds(g * part, part), j].reshape(part * 4, 128)
+            rows[pl.ds(g * part * 4, part * 4), pl.ds(j * 128, 128)] = block
+    out[...] = dot(sel, rows[...]).astype(BF16)
 
 
 def gelu_and_slope(value):
@@ -186,31 +169,21 @@
 
 def pack_back_kernel(i0, i1, out):
     total = (i0[...].astype(F32) + i1[...].astype(F32)).astype(BF16)
-    row = lax.broadcasted_iota(I32, (SEND, ROWS), 0)
-    col = lax.broadcasted_iota(I32, (SEND, ROWS), 1)
-    want = (row >> 3) * 2 + (row & 1)
-    quarter = (row >> 1) & 3
-    sels = [jnp.where((col == want) & (quarter == q), 1.0, 0.0).astype(BF16) for q in range(4)]
-    last = GW - 3 * QW
-    narrow = sum(dot(sels[q], total[:, q * QW : q * QW + last]) for q in range(4))
-    wide = sum(dot(sels[q], total[:, q * QW + last : (q + 1) * QW]) for q in range(3))
-    out[:, :last] = narrow.astype(BF16)
-    out[:, last:] = wide.astype(BF16)
+    for j in range(BACK_BLOCKS):
+        out[:, j] = total[:, j * 128 : (j + 1) * 128].reshape(SRC, CAP, 128)
 
 
 def unpack_back_kernel(got, gates, ids, slots, patch_grad, gate_grad, token):
     token[...] = jnp.zeros_like(token)
-    m0, m1, row = slot_match(ids[...], slots[...])
-    quarter = (row >> 1) & 3
-    hit = jnp.where(m0 | m1, 1.0, 0.0)
-    for q in range(4):
-        wide = QW if q < 3 else D - 3 * QW
-        sel = jnp.where(quarter == q, hit, 0.0).astype(BF16)
-        patch_grad[:, pl.ds(q * QW, wide)] = dot_rows(sel, got[:, :wide]).astype(BF16)
-    gate_block = got[:, D - 3 * QW : GW - 3 * QW]
+    m0, m1, _ = slot_match(ids[...], slots[...], CAP)
+    sel = jnp.where(m0 | m1, 1.0, 0.0).astype(BF16)
+    for j in range(SEND_BLOCKS):
+        rows = got[:, j].reshape(ROWS, 128)
+        patch_grad[:, pl.ds(j * 128, 128)] = dot_rows(sel, rows).astype(BF16)
+    gate_block = got[:, SEND_BLOCKS].reshape(ROWS, 128)
     g = gates[...].astype(F32)
     for k, m in enumerate((m0, m1)):
-        sel = jnp.where((quarter == 3) & m, 1.0, 0.0).astype(BF16)
+        sel = jnp.where(m, 1.0, 0.0).astype(BF16)
         gate_grad[k : k + 1, :] = dot_rows(gate_block, sel)[0:1, :] / g[k : k + 1, :]
 
 
@@ -265,7 +238,7 @@
     wi10, wo10 = swap_core(wi00), swap_core(wo00)
     sent = call(
         pack_rows_kernel,
-        shape((SEND, HALF_W)),
+        shape((SRC, SEND_BLOCKS, 4, 128)),
         (gates, ids, slots, patches, upstream),
         500_000_000,
         5_000_000,
@@ -278,7 +251,7 @@
             pltpu.VMEM((2, T), I32),
             pltpu.VMEM((T, D), BF16),
             pltpu.VMEM((T, D), BF16),
-            pltpu.VMEM((SEND, HALF_W), BF16),
+            pltpu.VMEM((SRC, SEND_BLOCKS, 4, 128), BF16),
             pltpu.SemaphoreType.DMA((5,)),
             pltpu.SemaphoreType.DMA((2,)),
         ],
@@ -292,8 +265,11 @@
         2_000_000,
         16,
         in_specs=[HBM],
-        scratch=[pltpu.VMEM((SEND, HALF_W), BF16), pltpu.SemaphoreType.DMA((2,))],
-        after=(wo10,),
+        scratch=[
+            pltpu.VMEM((SRC, SEND_BLOCKS, 4, 128), BF16),
+            pltpu.VMEM((4 * SRC, D), BF16),
+            pltpu.SemaphoreType.DMA((2,)),
+        ],
     )
     other = swap_rows(own)
     wi11, wo11 = swap_core(wi01), swap_core(wo01)
@@ -335,7 +311,7 @@
     far = weight_call(2, (swap_core(weight_call(3)),))
     near = swap_core(weight_call(1))
     far = swap_weights(far)
-    back = call(pack_back_kernel, shape((SEND, QW)), (part_own, part_back), 300_000_000, 2_500_000, 16)
+    back = call(pack_back_kernel, shape((SRC, BACK_BLOCKS, CAP, 128)), (part_own, part_back), 300_000_000, 2_500_000, 16)
     back = lax.all_to_all(back, everywhere, split_axis=0, concat_axis=0, tiled=True)
     patch_grad, gate_grad, token = call(
         unpack_back_kernel,

time: 123 us -> 120 us (0.976)
  the two profiles are of different devices: /device:TPU:6 before, /device:TPU:8 now
where the time goes in v5:
time: 120 us; the launch traced here: 119 us
  starting transfers between devices  47.3 us (39%)
  waiting for transfers between devices  30.3 us (25%)
  blocking collectives  23.7 us (20%)
  Pallas kernels  16.9 us (14%)
    ppermute x11, starting transfers between devices, swap(): lax.ppermute(value, axis, [(i, partner(i)) for i in range(lax.axis_size(a...  30.7 us
    all_to_all x1, blocking collectives, local(): lax.all_to_all(back, everywhere, split_axis=0, concat_axis=0, tiled=True)  23.7 us
    all_to_all x1, waiting for transfers between devices, local(): lax.all_to_all(sent, everywhere, split_axis=0, concat_axis=0, tiled=True)  20.1 us
    pallas_call x13, Pallas kernels, call(): pl.pallas_call(body, out_shape=out_shape, in_specs=(in_specs or [VM] * us...  16.9 us
    all_to_all x1, starting transfers between devices, local(): lax.all_to_all(sent, everywhere, split_axis=0, concat_axis=0, tiled=True)  16.6 us
    ppermute x11, waiting for transfers between devices, swap(): lax.ppermute(value, axis, [(i, partner(i)) for i in range(lax.axis_size(a...  10.1 us
  transfers between devices with their start and end apart: 12, of which 5 were waited for; matrix products, arithmetic and copies ran while one was open for 0% of the time, Pallas kernels for 9%

profile of v5, /device:TPU:8, one launch (start us, length us, event | category | flops | bytes accessed | tf_op | source)
XLA Modules:
  0.0 119.1 jit_solution(14732787657948381676)
XLA Ops:
  0.6 0.0 copy-start
  0.6 0.0 copy-start.1
  0.7 2.7 %shard_map.102 = bf16[64,13,4,128]{3,2,1,0:T(4,128)(2,1)} custom-call(bf16[2,128]{1,0:T(2,128)(2,1)} %bitcast.20, s32[2,128]{1,0:T(2,128)} %bitcast.16, s32[2,128]{1,0:T(2,128)} %bitcast.18, bf16[128,1664]{1,0:T(8,128)(2,1)} %refs_3_.1, bf16[128,1664]{1,0:T(8,128)(2,1)} %refs_4_.1), custom_call_target="tpu_custom_call" | custom-call | flops 500000000 | bytes 5000000 | tf_op jit(solution)/shard_map/pallas_call | solution.py:205
  3.4 16.6 %all-to-all-start = ((bf16[64,13,4,128]{3,2,1,0:T(4,128)(2,1)}), bf16[64,13,4,128]{3,2,1,0:T(4,128)(2,1)S(1)}, u32[]{:S(2)}, u32[]{:S(2)}) async-start(bf16[64,13,4,128]{3,2,1,0:T(4,128)(2,1)} %shard_map.102), calls=%async_computation | async-start | bytes 1703936 | tf_op jit(solution)/shard_map/all_to_all | solution.py:259
  20.0 0.0 copy-done
  20.0 4.7 %collective-permute-start.2 = (bf16[208,1664]{1,0:T(8,128)(2,1)S(1)}, bf16[208,1664]{1,0:T(8,128)(2,1)S(1)}, u32[]{:S(2)}, u32[]{:S(2)}) collective-permute-start(bf16[208,1664]{1,0:T(8,128)(2,1)S(1)} %bitcast.8), channel_id=1, source_target_pairs={{0,12},{4,8},{8,4},{12,0},{1,13},{5,9},{9,5},{13,1},{2,14},{6,10},... | collective-permute-start | bytes 2076680 | tf_op jit(solution)/shard_map/ppermute | solution.py:217
  24.7 0.0 copy-done.1
  24.7 2.4 %collective-permute-start.4 = (bf16[208,1664]{1,0:T(8,128)(2,1)S(1)}, bf16[208,1664]{1,0:T(8,128)(2,1)}, u32[]{:S(2)}, u32[]{:S(2)}) collective-permute-start(bf16[208,1664]{1,0:T(8,128)(2,1)S(1)} %bitcast.13), channel_id=1, source_target_pairs={{0,12},{4,8},{8,4},{12,0},{1,13},{5,9},{9,5},{13,1},{2,14},{6,10},... | collective-permute-start | bytes 2076680 | tf_op jit(solution)/shard_map/ppermute | solution.py:217
  27.1 20.1 %all-to-all-done.refs_0_ = bf16[64,13,4,128]{3,2,1,0:T(4,128)(2,1)S(1)} async-done(((bf16[64,13,4,128]{3,2,1,0:T(4,128)(2,1)}), bf16[64,13,4,128]{3,2,1,0:T(4,128)(2,1)S(1)}, u32[]{:S(2)}, u32[]{:S(2)}) %all-to-all-start) | async-done | bytes 852000 | tf_op jit(solution)/shard_map/all_to_all | solution.py:259
  47.2 1.2 %shard_map.103.refs_0_ = bf16[256,1664]{1,0:T(8,128)(2,1)S(1)} custom-call(bf16[64,13,4,128]{3,2,1,0:T(4,128)(2,1)S(1)} %all-to-all-done.refs_0_), custom_call_target="tpu_custom_call" | custom-call | flops 300000000 | bytes 2000000 | tf_op jit(solution)/shard_map/pallas_call | solution.py:205
  48.4 3.4 %collective-permute-start.6 = (bf16[256,1664]{1,0:T(8,128)(2,1)S(1)}, bf16[256,1664]{1,0:T(8,128)(2,1)S(1)}, u32[]{:S(2)}, u32[]{:S(2)}) collective-permute-start(bf16[256,1664]{1,0:T(8,128)(2,1)S(1)} %shard_map.103.refs_0_), channel_id=1, source_target_pairs={{0,4},{4,0},{8,12},{12,8},{1,5},{5,1},{9,13},{13,9},{2,6},{6,2},{1... | collective-permute-start | bytes 2555912 | tf_op jit(solution)/shard_map/ppermute | solution.py:217
  51.9 1.9 %collective-permute-start = (bf16[208,1664]{1,0:T(8,128)(2,1)S(1)}, bf16[208,1664]{1,0:T(8,128)(2,1)S(1)}, u32[]{:S(2)}, u32[]{:S(2)}) collective-permute-start(bf16[208,1664]{1,0:T(8,128)(2,1)S(1)} %bitcast.9), channel_id=1, source_target_pairs={{0,2},{2,0},{1,3},{3,1},{4,6},{6,4},{5,7},{7,5},{8,10},{10,8},{9,1... | collective-permute-start | bytes 2076680 | tf_op jit(solution)/shard_map/ppermute | solution.py:217
  53.8 2.4 %collective-permute-start.1 = (bf16[208,1664]{1,0:T(8,128)(2,1)S(1)}, bf16[208,1664]{1,0:T(8,128)(2,1)S(1)}, u32[]{:S(2)}, u32[]{:S(2)}) collective-permute-start(bf16[208,1664]{1,0:T(8,128)(2,1)S(1)} %bitcast.14), channel_id=1, source_target_pairs={{0,2},{2,0},{1,3},{3,1},{4,6},{6,4},{5,7},{7,5},{8,10},{10,8},{9,1... | collective-permute-start | bytes 2076680 | tf_op jit(solution)/shard_map/ppermute | solution.py:217
  56.2 0.0 collective-permute-done.2.refs_0_.refs_7_
  56.2 1.9 %collective-permute-start.3 = (bf16[208,1664]{1,0:T(8,128)(2,1)S(1)}, bf16[208,1664]{1,0:T(8,128)(2,1)S(1)}, u32[]{:S(2)}, u32[]{:S(2)}) collective-permute-start(bf16[208,1664]{1,0:T(8,128)(2,1)S(1)} %collective-permute-done.2.refs_0_.refs_7_), channel_id=1, source_target_pairs={{0,2},{2,0},{1,3},{3,1},{4,6},{6,4},{5,7},{7,5},{8,10},{10,8},{9,1... | collective-permute-start | bytes 2076680 | tf_op jit(solution)/shard_map/ppermute | solution.py:217
  58.1 0.0 collective-permute-done.4.refs_2_
  58.1 2.4 %collective-permute-start.5 = (bf16[208,1664]{1,0:T(8,128)(2,1)}, bf16[208,1664]{1,0:T(8,128)(2,1)S(1)}, u32[]{:S(2)}, u32[]{:S(2)}) collective-permute-start(bf16[208,1664]{1,0:T(8,128)(2,1)} %collective-permute-done.4.refs_2_), channel_id=1, source_target_pairs={{0,2},{2,0},{1,3},{3,1},{4,6},{6,4},{5,7},{7,5},{8,10},{10,8},{9,1... | collective-permute-start | bytes 2076680 | tf_op jit(solution)/shard_map/ppermute | solution.py:217
  60.6 0.0 collective-permute-done.refs_1_.refs_6_
  60.6 0.0 collective-permute-done.1.refs_3_
  60.6 1.0 shard_map.104
  61.6 0.0 collective-permute-done.3.refs_1_.refs_8_
  61.6 0.9 collective-permute-done.5.refs_3_
  62.5 2.1 %shard_map.105 = (bf16[1664,512]{1,0:T(8,128)(2,1)S(1)}, bf16[1664,512]{1,0:T(8,128)(2,1)S(1)}) custom-call(bf16[208,1664]{1,0:T(8,128)(2,1)S(1)} %collective-permute-done.2.refs_0_.refs_7_, bf16[208,1664]{1,0:T(8,128)(2,1)S(1)} %collective-permute-done.3.refs_1_.refs_8_, bf16[208,1664]{1,0:T(8,128)(2,1)} %collective-permute-done.4.refs_2_, ...), custom_call_target="tpu_custom_call" | custom-call | flops 1000000 | bytes 5000000 | tf_op jit(solution)/shard_map/pallas_call | solution.py:205
  64.6 1.7 %shard_map.106 = (bf16[128,1792]{1,0:T(8,128)(2,1)S(1)}, bf16[4,128,208]{2,1,0:T(8,128)(2,1)S(1)}, bf16[4,128,208]{2,1,0:T(8,128)(2,1)S(1)}) custom-call(bf16[256,1664]{1,0:T(8,128)(2,1)S(1)} %shard_map.103.refs_0_, bf16[1664,512]{1,0:T(8,128)(2,1)S(1)} %get-tuple-element.19.refs_1_, bf16[1664,512]{1,0:T(8,128)(2,1)S(1)} %get-tuple-element.20.refs_2_, ...), custom_call_target="tpu_custom_call" | custom-call | flops 1100000000 | bytes 8000000 | tf_op jit(solution)/shard_map/pallas_call | solution.py:205
  66.3 3.7 %collective-permute-done.6.refs_0_.refs_1_ = bf16[256,1664]{1,0:T(8,128)(2,1)S(1)} collective-permute-done((bf16[256,1664]{1,0:T(8,128)(2,1)S(1)}, bf16[256,1664]{1,0:T(8,128)(2,1)S(1)}, u32[]{:S(2)}, u32[]{:S(2)}) %collective-permute-start.6) | collective-permute-done | bytes 852000 | tf_op jit(solution)/shard_map/ppermute | solution.py:217
  70.0 1.7 %shard_map.107 = (bf16[128,1792]{1,0:T(8,128)(2,1)S(1)}, bf16[4,128,208]{2,1,0:T(8,128)(2,1)S(1)}, bf16[4,128,208]{2,1,0:T(8,128)(2,1)S(1)}) custom-call(bf16[256,1664]{1,0:T(8,128)(2,1)S(1)} %collective-permute-done.6.refs_0_.refs_1_, bf16[1664,512]{1,0:T(8,128)(2,1)S(1)} %get-tuple-element.19.refs_1_, bf16[1664,512]{1,0:T(8,128)(2,1)S(1)} %get-tuple-element.20.refs_2_, ...), custom_call_target="tpu_custom_call" | custom-call | flops 1100000000 | bytes 8000000 | tf_op jit(solution)/shard_map/pallas_call | solution.py:205
  71.7 1.0 shard_map.112
  72.6 1.9 %collective-permute-start.9 = (bf16[416,1664]{1,0:T(8,128)(2,1)S(1)}, bf16[416,1664]{1,0:T(8,128)(2,1)S(1)}, u32[]{:S(2)}, u32[]{:S(2)}) collective-permute-start(bf16[416,1664]{1,0:T(8,128)(2,1)S(1)} %shard_map.112), channel_id=1, source_target_pairs={{0,2},{2,0},{1,3},{3,1},{4,6},{6,4},{5,7},{7,5},{8,10},{10,8},{9,1... | collective-permute-start | bytes 4153352 | tf_op jit(solution)/shard_map/ppermute | solution.py:217
  74.6 3.4 %collective-permute-start.7 = (bf16[128,1792]{1,0:T(8,128)(2,1)S(1)}, bf16[128,1792]{1,0:T(8,128)(2,1)S(1)}, u32[]{:S(2)}, u32[]{:S(2)}) collective-permute-start(bf16[128,1792]{1,0:T(8,128)(2,1)S(1)} %get-tuple-element.24), channel_id=1, source_target_pairs={{0,4},{4,0},{8,12},{12,8},{1,5},{5,1},{9,13},{13,9},{2,6},{6,2},{1... | collective-permute-start | bytes 1376264 | tf_op jit(solution)/shard_map/ppermute | solution.py:217
  78.0 1.0 shard_map.110
  78.9 2.1 %collective-permute-start.8 = (bf16[416,1664]{1,0:T(8,128)(2,1)S(1)}, bf16[416,1664]{1,0:T(8,128)(2,1)S(1)}, u32[]{:S(2)}, u32[]{:S(2)}) collective-permute-start(bf16[416,1664]{1,0:T(8,128)(2,1)S(1)} %shard_map.110), channel_id=1, source_target_pairs={{0,2},{2,0},{1,3},{3,1},{4,6},{6,4},{5,7},{7,5},{8,10},{10,8},{9,1... | collective-permute-start | bytes 4153352 | tf_op jit(solution)/shard_map/ppermute | solution.py:217
  81.1 0.0 collective-permute-done.9.refs_6_
  81.1 1.0 shard_map.113
  82.0 0.0 copy-start.2
  82.1 0.0 copy-start.3
  82.1 0.0 copy-start.4
  82.1 4.1 %collective-permute-start.10 = (bf16[416,1664]{1,0:T(8,128)(2,1)S(1)}, bf16[416,1664]{1,0:T(8,128)(2,1)S(1)}, u32[]{:S(2)}, u32[]{:S(2)}) collective-permute-start(bf16[416,1664]{1,0:T(8,128)(2,1)S(1)} %shard_map.113), channel_id=1, source_target_pairs={{0,12},{4,8},{8,4},{12,0},{1,13},{5,9},{9,5},{13,1},{2,14},{6,10},... | collective-permute-start | bytes 4153352 | tf_op jit(solution)/shard_map/ppermute | solution.py:217
  86.2 3.2 %collective-permute-done.7.refs_1_ = bf16[128,1792]{1,0:T(8,128)(2,1)S(1)} collective-permute-done((bf16[128,1792]{1,0:T(8,128)(2,1)S(1)}, bf16[128,1792]{1,0:T(8,128)(2,1)S(1)}, u32[]{:S(2)}, u32[]{:S(2)}) %collective-permute-start.7) | collective-permute-done | bytes 458784 | tf_op jit(solution)/shard_map/ppermute | solution.py:217
  89.4 0.3 shard_map.108
  89.7 23.7 %all_to_all.10.refs_0_ = bf16[64,14,2,128]{3,2,1,0:T(2,128)(2,1)S(1)} all-to-all(bf16[64,14,2,128]{3,2,1,0:T(2,128)(2,1)S(1)} %shard_map.108), channel_id=1, replica_groups=mesh['zlo'=4,'y'=8,'x'=4,'core'=2,'zhi'=2] {'zlo','y','zhi'}, dimensions={0} | all-to-all | bytes 917504 | tf_op jit(solution)/shard_map/all_to_all | solution.py:315
  113.4 0.0 copy-done.2
  113.4 0.0 copy-done.3
  113.4 0.0 copy-done.4
  113.5 1.2 shard_map.109
  114.6 0.0 collective-permute-done.8.refs_6_
  114.6 1.0 shard_map.111.refs_0_
  115.6 2.3 %collective-permute-done.10.refs_1_ = bf16[416,1664]{1,0:T(8,128)(2,1)S(1)} collective-permute-done((bf16[416,1664]{1,0:T(8,128)(2,1)S(1)}, bf16[416,1664]{1,0:T(8,128)(2,1)S(1)}, u32[]{:S(2)}, u32[]{:S(2)}) %collective-permute-start.10) | collective-permute-done | bytes 1384480 | tf_op jit(solution)/shard_map/ppermute | solution.py:217
  117.9 1.2 %shard_map.114 = (bf16[208,1664]{1,0:T(8,128)(2,1)}, bf16[208,1664]{1,0:T(8,128)(2,1)}) custom-call(bf16[416,1664]{1,0:T(8,128)(2,1)S(1)} %shard_map.111.refs_0_, bf16[416,1664]{1,0:T(8,128)(2,1)S(1)} %collective-permute-done.10.refs_1_), custom_call_target="tpu_custom_call" | custom-call | flops 1000000 | bytes 4000000 | tf_op jit(solution)/shard_map/pallas_call | solution.py:205
Async XLA Ops:
  0.6 19.4 %copy-start = (bf16[1,208,1664]{2,1,0:T(8,128)(2,1)S(1)}, bf16[1,208,1664]{2,1,0:T(8,128)(2,1)}, u32[]{:S(2)}) copy-start(bf16[1,208,1664]{2,1,0:T(8,128)(2,1)} %param.12) | copy-start | bytes 2076676
  0.6 24.0 %copy-start.1 = (bf16[1,208,1664]{2,1,0:T(8,128)(2,1)S(1)}, bf16[1,208,1664]{2,1,0:T(8,128)(2,1)}, u32[]{:S(2)}) copy-start(bf16[1,208,1664]{2,1,0:T(8,128)(2,1)} %param.13) | copy-start | bytes 2076676
  3.4 43.8 %all-to-all-start = ((bf16[64,13,4,128]{3,2,1,0:T(4,128)(2,1)}), bf16[64,13,4,128]{3,2,1,0:T(4,128)(2,1)S(1)}, u32[]{:S(2)}, u32[]{:S(2)}) async-start(bf16[64,13,4,128]{3,2,1,0:T(4,128)(2,1)} %shard_map.102), calls=%async_computation | async-start | bytes 1703936 | tf_op jit(solution)/shard_map/all_to_all | solution.py:259
  20.0 36.2 %collective-permute-start.2 = (bf16[208,1664]{1,0:T(8,128)(2,1)S(1)}, bf16[208,1664]{1,0:T(8,128)(2,1)S(1)}, u32[]{:S(2)}, u32[]{:S(2)}) collective-permute-start(bf16[208,1664]{1,0:T(8,128)(2,1)S(1)} %bitcast.8), channel_id=1, source_target_pairs={{0,12},{4,8},{8,4},{12,0},{1,13},{5,9},{9,5},{13,1},{2,14},{6,10},... | collective-permute-start | bytes 2076680 | tf_op jit(solution)/shard_map/ppermute | solution.py:217
  24.7 33.4 %collective-permute-start.4 = (bf16[208,1664]{1,0:T(8,128)(2,1)S(1)}, bf16[208,1664]{1,0:T(8,128)(2,1)}, u32[]{:S(2)}, u32[]{:S(2)}) collective-permute-start(bf16[208,1664]{1,0:T(8,128)(2,1)S(1)} %bitcast.13), channel_id=1, source_target_pairs={{0,12},{4,8},{8,4},{12,0},{1,13},{5,9},{9,5},{13,1},{2,14},{6,10},... | collective-permute-start | bytes 2076680 | tf_op jit(solution)/shard_map/ppermute | solution.py:217
  48.4 21.6 %collective-permute-start.6 = (bf16[256,1664]{1,0:T(8,128)(2,1)S(1)}, bf16[256,1664]{1,0:T(8,128)(2,1)S(1)}, u32[]{:S(2)}, u32[]{:S(2)}) collective-permute-start(bf16[256,1664]{1,0:T(8,128)(2,1)S(1)} %shard_map.103.refs_0_), channel_id=1, source_target_pairs={{0,4},{4,0},{8,12},{12,8},{1,5},{5,1},{9,13},{13,9},{2,6},{6,2},{1... | collective-permute-start | bytes 2555912 | tf_op jit(solution)/shard_map/ppermute | solution.py:217
  51.9 8.7 %collective-permute-start = (bf16[208,1664]{1,0:T(8,128)(2,1)S(1)}, bf16[208,1664]{1,0:T(8,128)(2,1)S(1)}, u32[]{:S(2)}, u32[]{:S(2)}) collective-permute-start(bf16[208,1664]{1,0:T(8,128)(2,1)S(1)} %bitcast.9), channel_id=1, source_target_pairs={{0,2},{2,0},{1,3},{3,1},{4,6},{6,4},{5,7},{7,5},{8,10},{10,8},{9,1... | collective-permute-start | bytes 2076680 | tf_op jit(solution)/shard_map/ppermute | solution.py:217
  53.8 6.8 %collective-permute-start.1 = (bf16[208,1664]{1,0:T(8,128)(2,1)S(1)}, bf16[208,1664]{1,0:T(8,128)(2,1)S(1)}, u32[]{:S(2)}, u32[]{:S(2)}) collective-permute-start(bf16[208,1664]{1,0:T(8,128)(2,1)S(1)} %bitcast.14), channel_id=1, source_target_pairs={{0,2},{2,0},{1,3},{3,1},{4,6},{6,4},{5,7},{7,5},{8,10},{10,8},{9,1... | collective-permute-start | bytes 2076680 | tf_op jit(solution)/shard_map/ppermute | solution.py:217
  56.2 5.4 %collective-permute-start.3 = (bf16[208,1664]{1,0:T(8,128)(2,1)S(1)}, bf16[208,1664]{1,0:T(8,128)(2,1)S(1)}, u32[]{:S(2)}, u32[]{:S(2)}) collective-permute-start(bf16[208,1664]{1,0:T(8,128)(2,1)S(1)} %collective-permute-done.2.refs_0_.refs_7_), channel_id=1, source_target_pairs={{0,2},{2,0},{1,3},{3,1},{4,6},{6,4},{5,7},{7,5},{8,10},{10,8},{9,1... | collective-permute-start | bytes 2076680 | tf_op jit(solution)/shard_map/ppermute | solution.py:217
  58.1 4.4 %collective-permute-start.5 = (bf16[208,1664]{1,0:T(8,128)(2,1)}, bf16[208,1664]{1,0:T(8,128)(2,1)S(1)}, u32[]{:S(2)}, u32[]{:S(2)}) collective-permute-start(bf16[208,1664]{1,0:T(8,128)(2,1)} %collective-permute-done.4.refs_2_), channel_id=1, source_target_pairs={{0,2},{2,0},{1,3},{3,1},{4,6},{6,4},{5,7},{7,5},{8,10},{10,8},{9,1... | collective-permute-start | bytes 2076680 | tf_op jit(solution)/shard_map/ppermute | solution.py:217
  72.6 8.4 %collective-permute-start.9 = (bf16[416,1664]{1,0:T(8,128)(2,1)S(1)}, bf16[416,1664]{1,0:T(8,128)(2,1)S(1)}, u32[]{:S(2)}, u32[]{:S(2)}) collective-permute-start(bf16[416,1664]{1,0:T(8,128)(2,1)S(1)} %shard_map.112), channel_id=1, source_target_pairs={{0,2},{2,0},{1,3},{3,1},{4,6},{6,4},{5,7},{7,5},{8,10},{10,8},{9,1... | collective-permute-start | bytes 4153352 | tf_op jit(solution)/shard_map/ppermute | solution.py:217
  74.6 14.8 %collective-permute-start.7 = (bf16[128,1792]{1,0:T(8,128)(2,1)S(1)}, bf16[128,1792]{1,0:T(8,128)(2,1)S(1)}, u32[]{:S(2)}, u32[]{:S(2)}) collective-permute-start(bf16[128,1792]{1,0:T(8,128)(2,1)S(1)} %get-tuple-element.24), channel_id=1, source_target_pairs={{0,4},{4,0},{8,12},{12,8},{1,5},{5,1},{9,13},{13,9},{2,6},{6,2},{1... | collective-permute-start | bytes 1376264 | tf_op jit(solution)/shard_map/ppermute | solution.py:217
  78.9 35.7 %collective-permute-start.8 = (bf16[416,1664]{1,0:T(8,128)(2,1)S(1)}, bf16[416,1664]{1,0:T(8,128)(2,1)S(1)}, u32[]{:S(2)}, u32[]{:S(2)}) collective-permute-start(bf16[416,1664]{1,0:T(8,128)(2,1)S(1)} %shard_map.110), channel_id=1, source_target_pairs={{0,2},{2,0},{1,3},{3,1},{4,6},{6,4},{5,7},{7,5},{8,10},{10,8},{9,1... | collective-permute-start | bytes 4153352 | tf_op jit(solution)/shard_map/ppermute | solution.py:217
  82.0 31.4 %copy-start.2 = (s32[128,2]{0,1:T(2,128)S(1)}, s32[128,2]{0,1:T(2,128)}, u32[]{:S(2)}) copy-start(s32[128,2]{0,1:T(2,128)} %param.10) | copy-start | bytes 3076
  82.1 31.4 %copy-start.3 = (s32[128,2]{0,1:T(2,128)S(1)}, s32[128,2]{0,1:T(2,128)}, u32[]{:S(2)}) copy-start(s32[128,2]{0,1:T(2,128)} %param.11) | copy-start | bytes 3076
  82.1 31.4 %copy-start.4 = (bf16[128,2]{0,1:T(2,128)(2,1)S(1)}, bf16[128,2]{0,1:T(2,128)(2,1)}, u32[]{:S(2)}) copy-start(bf16[128,2]{0,1:T(2,128)(2,1)} %param.9) | copy-start | bytes 1540
  82.1 35.8 %collective-permute-start.10 = (bf16[416,1664]{1,0:T(8,128)(2,1)S(1)}, bf16[416,1664]{1,0:T(8,128)(2,1)S(1)}, u32[]{:S(2)}, u32[]{:S(2)}) collective-permute-start(bf16[416,1664]{1,0:T(8,128)(2,1)S(1)} %shard_map.113), channel_id=1, source_target_pairs={{0,12},{4,8},{8,4},{12,0},{1,13},{5,9},{9,5},{13,1},{2,14},{6,10},... | collective-permute-start | bytes 4153352 | tf_op jit(solution)/shard_map/ppermute | solution.py:217

commit v6 on v5

--- a/solution.py
+++ b/solution.py
@@ -162,9 +162,14 @@
     out[pl.ds(HS, HS), :] = grad_out.astype(BF16)
 
 
-def weight_sum_kernel(near, far, out_in, out_out):
-    out_in[...] = (near[pl.ds(0, HS), :].astype(F32) + far[pl.ds(0, HS), :].astype(F32)).astype(BF16)
-    out_out[...] = (near[pl.ds(HS, HS), :].astype(F32) + far[pl.ds(HS, HS), :].astype(F32)).astype(BF16)
+def partial_sum_kernel(own, far, out):
+    out[...] = (own[...].astype(F32) + far[...].astype(F32)).astype(BF16)
+
+
+def weight_sum_kernel(own, near, out_in, out_out):
+    for k, out in enumerate((out_in, out_out)):
+        rows = pl.ds(k * HS, HS)
+        out[...] = (own[rows, :].astype(F32) + near[rows, :].astype(F32)).astype(BF16)
 
 
 def pack_back_kernel(i0, i1, out):
@@ -309,8 +314,9 @@
         )
 
     far = weight_call(2, (swap_core(weight_call(3)),))
-    near = swap_core(weight_call(1))
+    sent = far
     far = swap_weights(far)
+    near = swap_core(weight_call(1, after=(sent,)))
     back = call(pack_back_kernel, shape((SRC, BACK_BLOCKS, CAP, 128)), (part_own, part_back), 300_000_000, 2_500_000, 16)
     back = lax.all_to_all(back, everywhere, split_axis=0, concat_axis=0, tiled=True)
     patch_grad, gate_grad, token = call(
@@ -321,9 +327,10 @@
         1_000_000,
         16,
     )
-    near = weight_call(0, (near,), (token,))
+    mine = weight_call(0, after=(token,))
+    mine = call(partial_sum_kernel, both, (mine, far), 1_000_000, 4_000_000, 16, after=(token,))
     grad_in, grad_out = call(
-        weight_sum_kernel, [shape((HS, D))] * 2, (near, far), 1_000_000, 4_000_000, 16
+        weight_sum_kernel, [shape((HS, D))] * 2, (mine, near), 1_000_000, 4_000_000, 16, after=(token,)
     )
     return patch_grad, gate_grad.T, grad_in[None], grad_out[None]
 

time: 120 us -> 118 us (0.983)
  the two profiles are of different devices: /device:TPU:8 before, /device:TPU:6 now
where the time goes in v6:
time: 118 us
  starting transfers between devices  44.5 us (38%)
  waiting for transfers between devices  28.1 us (24%)
  blocking collectives  26.8 us (23%)
  Pallas kernels  17.3 us (15%)
    ppermute x11, starting transfers between devices, swap(): lax.ppermute(value, axis, [(i, partner(i)) for i in range(lax.axis_size(a...  27.9 us
    all_to_all x1, blocking collectives, local(): lax.all_to_all(back, everywhere, split_axis=0, concat_axis=0, tiled=True)  26.8 us
    all_to_all x1, waiting for transfers between devices, local(): lax.all_to_all(sent, everywhere, split_axis=0, concat_axis=0, tiled=True)  20 us
    pallas_call x14, Pallas kernels, call(): pl.pallas_call(body, out_shape=out_shape, in_specs=(in_specs or [VM] * us...  17.3 us
    all_to_all x1, starting transfers between devices, local(): lax.all_to_all(sent, everywhere, split_axis=0, concat_axis=0, tiled=True)  16.6 us
    ppermute x11, waiting for transfers between devices, swap(): lax.ppermute(value, axis, [(i, partner(i)) for i in range(lax.axis_size(a...  8.05 us
  transfers between devices with their start and end apart: 12, of which 5 were waited for; matrix products, arithmetic and copies ran while one was open for 0% of the time, Pallas kernels for 9%

profile of v6, /device:TPU:6, one launch (start us, length us, event | category | flops | bytes accessed | tf_op | source)
XLA Modules:
  0.0 117.6 jit_solution(9892661191794369763)
XLA Ops:
  0.6 0.0 copy-start
  0.6 0.0 copy-start.1
  0.7 2.7 %shard_map.102 = bf16[64,13,4,128]{3,2,1,0:T(4,128)(2,1)} custom-call(bf16[2,128]{1,0:T(2,128)(2,1)} %bitcast.20, s32[2,128]{1,0:T(2,128)} %bitcast.16, s32[2,128]{1,0:T(2,128)} %bitcast.18, bf16[128,1664]{1,0:T(8,128)(2,1)} %refs_3_.1, bf16[128,1664]{1,0:T(8,128)(2,1)} %refs_4_.1), custom_call_target="tpu_custom_call" | custom-call | flops 500000000 | bytes 5000000 | tf_op jit(solution)/shard_map/pallas_call | solution.py:210
  3.4 16.6 %all-to-all-start = ((bf16[64,13,4,128]{3,2,1,0:T(4,128)(2,1)}), bf16[64,13,4,128]{3,2,1,0:T(4,128)(2,1)S(1)}, u32[]{:S(2)}, u32[]{:S(2)}) async-start(bf16[64,13,4,128]{3,2,1,0:T(4,128)(2,1)} %shard_map.102), calls=%async_computation | async-start | bytes 1703936 | tf_op jit(solution)/shard_map/all_to_all | solution.py:264
  20.0 0.0 copy-done
  20.0 2.4 %collective-permute-start.2 = (bf16[208,1664]{1,0:T(8,128)(2,1)S(1)}, bf16[208,1664]{1,0:T(8,128)(2,1)S(1)}, u32[]{:S(2)}, u32[]{:S(2)}) collective-permute-start(bf16[208,1664]{1,0:T(8,128)(2,1)S(1)} %bitcast.8), channel_id=1, source_target_pairs={{0,12},{4,8},{8,4},{12,0},{1,13},{5,9},{9,5},{13,1},{2,14},{6,10},... | collective-permute-start | bytes 2076680 | tf_op jit(solution)/shard_map/ppermute | solution.py:222
  22.4 0.0 copy-done.1
  22.4 4.7 %collective-permute-start.4 = (bf16[208,1664]{1,0:T(8,128)(2,1)S(1)}, bf16[208,1664]{1,0:T(8,128)(2,1)}, u32[]{:S(2)}, u32[]{:S(2)}) collective-permute-start(bf16[208,1664]{1,0:T(8,128)(2,1)S(1)} %bitcast.13), channel_id=1, source_target_pairs={{0,12},{4,8},{8,4},{12,0},{1,13},{5,9},{9,5},{13,1},{2,14},{6,10},... | collective-permute-start | bytes 2076680 | tf_op jit(solution)/shard_map/ppermute | solution.py:222
  27.1 20.0 %all-to-all-done.refs_0_ = bf16[64,13,4,128]{3,2,1,0:T(4,128)(2,1)S(1)} async-done(((bf16[64,13,4,128]{3,2,1,0:T(4,128)(2,1)}), bf16[64,13,4,128]{3,2,1,0:T(4,128)(2,1)S(1)}, u32[]{:S(2)}, u32[]{:S(2)}) %all-to-all-start) | async-done | bytes 852000 | tf_op jit(solution)/shard_map/all_to_all | solution.py:264
  47.1 1.2 %shard_map.103.refs_0_ = bf16[256,1664]{1,0:T(8,128)(2,1)S(1)} custom-call(bf16[64,13,4,128]{3,2,1,0:T(4,128)(2,1)S(1)} %all-to-all-done.refs_0_), custom_call_target="tpu_custom_call" | custom-call | flops 300000000 | bytes 2000000 | tf_op jit(solution)/shard_map/pallas_call | solution.py:210
  48.3 2.7 %collective-permute-start.6 = (bf16[256,1664]{1,0:T(8,128)(2,1)S(1)}, bf16[256,1664]{1,0:T(8,128)(2,1)S(1)}, u32[]{:S(2)}, u32[]{:S(2)}) collective-permute-start(bf16[256,1664]{1,0:T(8,128)(2,1)S(1)} %shard_map.103.refs_0_), channel_id=1, source_target_pairs={{0,4},{4,0},{8,12},{12,8},{1,5},{5,1},{9,13},{13,9},{2,6},{6,2},{1... | collective-permute-start | bytes 2555912 | tf_op jit(solution)/shard_map/ppermute | solution.py:222
  51.1 1.9 %collective-permute-start = (bf16[208,1664]{1,0:T(8,128)(2,1)S(1)}, bf16[208,1664]{1,0:T(8,128)(2,1)S(1)}, u32[]{:S(2)}, u32[]{:S(2)}) collective-permute-start(bf16[208,1664]{1,0:T(8,128)(2,1)S(1)} %bitcast.9), channel_id=1, source_target_pairs={{0,2},{2,0},{1,3},{3,1},{4,6},{6,4},{5,7},{7,5},{8,10},{10,8},{9,1... | collective-permute-start | bytes 2076680 | tf_op jit(solution)/shard_map/ppermute | solution.py:222
  53.0 2.4 %collective-permute-start.1 = (bf16[208,1664]{1,0:T(8,128)(2,1)S(1)}, bf16[208,1664]{1,0:T(8,128)(2,1)S(1)}, u32[]{:S(2)}, u32[]{:S(2)}) collective-permute-start(bf16[208,1664]{1,0:T(8,128)(2,1)S(1)} %bitcast.14), channel_id=1, source_target_pairs={{0,2},{2,0},{1,3},{3,1},{4,6},{6,4},{5,7},{7,5},{8,10},{10,8},{9,1... | collective-permute-start | bytes 2076680 | tf_op jit(solution)/shard_map/ppermute | solution.py:222
  55.4 0.0 collective-permute-done.2.refs_0_.refs_7_
  55.4 1.9 %collective-permute-start.3 = (bf16[208,1664]{1,0:T(8,128)(2,1)S(1)}, bf16[208,1664]{1,0:T(8,128)(2,1)S(1)}, u32[]{:S(2)}, u32[]{:S(2)}) collective-permute-start(bf16[208,1664]{1,0:T(8,128)(2,1)S(1)} %collective-permute-done.2.refs_0_.refs_7_), channel_id=1, source_target_pairs={{0,2},{2,0},{1,3},{3,1},{4,6},{6,4},{5,7},{7,5},{8,10},{10,8},{9,1... | collective-permute-start | bytes 2076680 | tf_op jit(solution)/shard_map/ppermute | solution.py:222
  57.4 0.0 collective-permute-done.4.refs_2_
  57.4 2.4 %collective-permute-start.5 = (bf16[208,1664]{1,0:T(8,128)(2,1)}, bf16[208,1664]{1,0:T(8,128)(2,1)S(1)}, u32[]{:S(2)}, u32[]{:S(2)}) collective-permute-start(bf16[208,1664]{1,0:T(8,128)(2,1)} %collective-permute-done.4.refs_2_), channel_id=1, source_target_pairs={{0,2},{2,0},{1,3},{3,1},{4,6},{6,4},{5,7},{7,5},{8,10},{10,8},{9,1... | collective-permute-start | bytes 2076680 | tf_op jit(solution)/shard_map/ppermute | solution.py:222
  59.8 0.0 collective-permute-done.refs_1_.refs_6_
  59.8 0.0 collective-permute-done.1.refs_3_
  59.8 1.0 shard_map.104
  60.8 0.0 collective-permute-done.3.refs_1_.refs_8_
  60.8 0.9 collective-permute-done.5.refs_3_
  61.7 2.1 %shard_map.105 = (bf16[1664,512]{1,0:T(8,128)(2,1)S(1)}, bf16[1664,512]{1,0:T(8,128)(2,1)S(1)}) custom-call(bf16[208,1664]{1,0:T(8,128)(2,1)S(1)} %collective-permute-done.2.refs_0_.refs_7_, bf16[208,1664]{1,0:T(8,128)(2,1)S(1)} %collective-permute-done.3.refs_1_.refs_8_, bf16[208,1664]{1,0:T(8,128)(2,1)} %collective-permute-done.4.refs_2_, ...), custom_call_target="tpu_custom_call" | custom-call | flops 1000000 | bytes 5000000 | tf_op jit(solution)/shard_map/pallas_call | solution.py:210
  63.8 1.7 %shard_map.106 = (bf16[128,1792]{1,0:T(8,128)(2,1)S(1)}, bf16[4,128,208]{2,1,0:T(8,128)(2,1)S(1)}, bf16[4,128,208]{2,1,0:T(8,128)(2,1)S(1)}) custom-call(bf16[256,1664]{1,0:T(8,128)(2,1)S(1)} %shard_map.103.refs_0_, bf16[1664,512]{1,0:T(8,128)(2,1)S(1)} %get-tuple-element.19.refs_1_, bf16[1664,512]{1,0:T(8,128)(2,1)S(1)} %get-tuple-element.20.refs_2_, ...), custom_call_target="tpu_custom_call" | custom-call | flops 1100000000 | bytes 8000000 | tf_op jit(solution)/shard_map/pallas_call | solution.py:210
  65.5 1.7 %collective-permute-done.6.refs_0_.refs_1_ = bf16[256,1664]{1,0:T(8,128)(2,1)S(1)} collective-permute-done((bf16[256,1664]{1,0:T(8,128)(2,1)S(1)}, bf16[256,1664]{1,0:T(8,128)(2,1)S(1)}, u32[]{:S(2)}, u32[]{:S(2)}) %collective-permute-start.6) | collective-permute-done | bytes 852000 | tf_op jit(solution)/shard_map/ppermute | solution.py:222
  67.3 1.7 %shard_map.107 = (bf16[128,1792]{1,0:T(8,128)(2,1)S(1)}, bf16[4,128,208]{2,1,0:T(8,128)(2,1)S(1)}, bf16[4,128,208]{2,1,0:T(8,128)(2,1)S(1)}) custom-call(bf16[256,1664]{1,0:T(8,128)(2,1)S(1)} %collective-permute-done.6.refs_0_.refs_1_, bf16[1664,512]{1,0:T(8,128)(2,1)S(1)} %get-tuple-element.19.refs_1_, bf16[1664,512]{1,0:T(8,128)(2,1)S(1)} %get-tuple-element.20.refs_2_, ...), custom_call_target="tpu_custom_call" | custom-call | flops 1100000000 | bytes 8000000 | tf_op jit(solution)/shard_map/pallas_call | solution.py:210
  68.9 1.0 shard_map.111
  69.9 1.9 %collective-permute-start.8 = (bf16[416,1664]{1,0:T(8,128)(2,1)S(1)}, bf16[416,1664]{1,0:T(8,128)(2,1)S(1)}, u32[]{:S(2)}, u32[]{:S(2)}) collective-permute-start(bf16[416,1664]{1,0:T(8,128)(2,1)S(1)} %shard_map.111), channel_id=1, source_target_pairs={{0,2},{2,0},{1,3},{3,1},{4,6},{6,4},{5,7},{7,5},{8,10},{10,8},{9,1... | collective-permute-start | bytes 4153352 | tf_op jit(solution)/shard_map/ppermute | solution.py:222
  71.8 2.7 %collective-permute-start.7 = (bf16[128,1792]{1,0:T(8,128)(2,1)S(1)}, bf16[128,1792]{1,0:T(8,128)(2,1)S(1)}, u32[]{:S(2)}, u32[]{:S(2)}) collective-permute-start(bf16[128,1792]{1,0:T(8,128)(2,1)S(1)} %get-tuple-element.24), channel_id=1, source_target_pairs={{0,4},{4,0},{8,12},{12,8},{1,5},{5,1},{9,13},{13,9},{2,6},{6,2},{1... | collective-permute-start | bytes 1376264 | tf_op jit(solution)/shard_map/ppermute | solution.py:222
  74.6 0.4 collective-permute-done.8.refs_6_
  74.9 0.9 shard_map.112.refs_6_
  75.9 2.7 %collective-permute-start.9 = (bf16[416,1664]{1,0:T(8,128)(2,1)S(1)}, bf16[416,1664]{1,0:T(8,128)(2,1)S(1)}, u32[]{:S(2)}, u32[]{:S(2)}) collective-permute-start(bf16[416,1664]{1,0:T(8,128)(2,1)S(1)} %shard_map.112.refs_6_), channel_id=1, source_target_pairs={{0,12},{4,8},{8,4},{12,0},{1,13},{5,9},{9,5},{13,1},{2,14},{6,10},... | collective-permute-start | bytes 4153352 | tf_op jit(solution)/shard_map/ppermute | solution.py:222
  78.6 1.0 shard_map.114
  79.6 0.0 copy-start.2
  79.6 0.0 copy-start.3
  79.6 0.0 copy-start.4
  79.6 2.1 %collective-permute-start.10 = (bf16[416,1664]{1,0:T(8,128)(2,1)S(1)}, bf16[416,1664]{1,0:T(8,128)(2,1)S(1)}, u32[]{:S(2)}, u32[]{:S(2)}) collective-permute-start(bf16[416,1664]{1,0:T(8,128)(2,1)S(1)} %shard_map.114), channel_id=1, source_target_pairs={{0,2},{2,0},{1,3},{3,1},{4,6},{6,4},{5,7},{7,5},{8,10},{10,8},{9,1... | collective-permute-start | bytes 4153352 | tf_op jit(solution)/shard_map/ppermute | solution.py:222
  81.7 5.0 %collective-permute-done.7.refs_1_ = bf16[128,1792]{1,0:T(8,128)(2,1)S(1)} collective-permute-done((bf16[128,1792]{1,0:T(8,128)(2,1)S(1)}, bf16[128,1792]{1,0:T(8,128)(2,1)S(1)}, u32[]{:S(2)}, u32[]{:S(2)}) %collective-permute-start.7) | collective-permute-done | bytes 458784 | tf_op jit(solution)/shard_map/ppermute | solution.py:222
  86.6 0.3 shard_map.108
  87.0 26.8 %all_to_all.10.refs_0_ = bf16[64,14,2,128]{3,2,1,0:T(2,128)(2,1)S(1)} all-to-all(bf16[64,14,2,128]{3,2,1,0:T(2,128)(2,1)S(1)} %shard_map.108), channel_id=1, replica_groups=mesh['zlo'=4,'y'=8,'x'=4,'core'=2,'zhi'=2] {'zlo','y','zhi'}, dimensions={0} | all-to-all | bytes 917504 | tf_op jit(solution)/shard_map/all_to_all | solution.py:321
  113.8 0.0 copy-done.2
  113.8 0.0 copy-done.3
  113.8 1.2 shard_map.109
  115.0 1.0 shard_map.110.refs_0_
  115.9 0.0 collective-permute-done.9.refs_1_
  116.0 0.4 shard_map.113.refs_0_
  116.3 0.0 collective-permute-done.10.refs_1_
  116.3 1.3 %shard_map.115 = (bf16[208,1664]{1,0:T(8,128)(2,1)}, bf16[208,1664]{1,0:T(8,128)(2,1)}) custom-call(bf16[416,1664]{1,0:T(8,128)(2,1)S(1)} %shard_map.113.refs_0_, bf16[416,1664]{1,0:T(8,128)(2,1)S(1)} %collective-permute-done.10.refs_1_, f32[8,128]{1,0:T(8,128)S(1)} %get-tuple-element.31.refs_6_.refs_2_), custom_call_target="tpu_custom_call" | custom-call | flops 1000000 | bytes 4000000 | tf_op jit(solution)/shard_map/pallas_call | solution.py:210
  (1 shorter events, 0.0 us)
Async XLA Ops:
  0.6 19.4 %copy-start = (bf16[1,208,1664]{2,1,0:T(8,128)(2,1)S(1)}, bf16[1,208,1664]{2,1,0:T(8,128)(2,1)}, u32[]{:S(2)}) copy-start(bf16[1,208,1664]{2,1,0:T(8,128)(2,1)} %param.12) | copy-start | bytes 2076676
  0.6 21.8 %copy-start.1 = (bf16[1,208,1664]{2,1,0:T(8,128)(2,1)S(1)}, bf16[1,208,1664]{2,1,0:T(8,128)(2,1)}, u32[]{:S(2)}) copy-start(bf16[1,208,1664]{2,1,0:T(8,128)(2,1)} %param.13) | copy-start | bytes 2076676
  3.4 43.7 %all-to-all-start = ((bf16[64,13,4,128]{3,2,1,0:T(4,128)(2,1)}), bf16[64,13,4,128]{3,2,1,0:T(4,128)(2,1)S(1)}, u32[]{:S(2)}, u32[]{:S(2)}) async-start(bf16[64,13,4,128]{3,2,1,0:T(4,128)(2,1)} %shard_map.102), calls=%async_computation | async-start | bytes 1703936 | tf_op jit(solution)/shard_map/all_to_all | solution.py:264
  20.0 35.4 %collective-permute-start.2 = (bf16[208,1664]{1,0:T(8,128)(2,1)S(1)}, bf16[208,1664]{1,0:T(8,128)(2,1)S(1)}, u32[]{:S(2)}, u32[]{:S(2)}) collective-permute-start(bf16[208,1664]{1,0:T(8,128)(2,1)S(1)} %bitcast.8), channel_id=1, source_target_pairs={{0,12},{4,8},{8,4},{12,0},{1,13},{5,9},{9,5},{13,1},{2,14},{6,10},... | collective-permute-start | bytes 2076680 | tf_op jit(solution)/shard_map/ppermute | solution.py:222
  22.4 34.9 %collective-permute-start.4 = (bf16[208,1664]{1,0:T(8,128)(2,1)S(1)}, bf16[208,1664]{1,0:T(8,128)(2,1)}, u32[]{:S(2)}, u32[]{:S(2)}) collective-permute-start(bf16[208,1664]{1,0:T(8,128)(2,1)S(1)} %bitcast.13), channel_id=1, source_target_pairs={{0,12},{4,8},{8,4},{12,0},{1,13},{5,9},{9,5},{13,1},{2,14},{6,10},... | collective-permute-start | bytes 2076680 | tf_op jit(solution)/shard_map/ppermute | solution.py:222
  48.3 18.9 %collective-permute-start.6 = (bf16[256,1664]{1,0:T(8,128)(2,1)S(1)}, bf16[256,1664]{1,0:T(8,128)(2,1)S(1)}, u32[]{:S(2)}, u32[]{:S(2)}) collective-permute-start(bf16[256,1664]{1,0:T(8,128)(2,1)S(1)} %shard_map.103.refs_0_), channel_id=1, source_target_pairs={{0,4},{4,0},{8,12},{12,8},{1,5},{5,1},{9,13},{13,9},{2,6},{6,2},{1... | collective-permute-start | bytes 2555912 | tf_op jit(solution)/shard_map/ppermute | solution.py:222
  51.1 8.7 %collective-permute-start = (bf16[208,1664]{1,0:T(8,128)(2,1)S(1)}, bf16[208,1664]{1,0:T(8,128)(2,1)S(1)}, u32[]{:S(2)}, u32[]{:S(2)}) collective-permute-start(bf16[208,1664]{1,0:T(8,128)(2,1)S(1)} %bitcast.9), channel_id=1, source_target_pairs={{0,2},{2,0},{1,3},{3,1},{4,6},{6,4},{5,7},{7,5},{8,10},{10,8},{9,1... | collective-permute-start | bytes 2076680 | tf_op jit(solution)/shard_map/ppermute | solution.py:222
  53.0 6.8 %collective-permute-start.1 = (bf16[208,1664]{1,0:T(8,128)(2,1)S(1)}, bf16[208,1664]{1,0:T(8,128)(2,1)S(1)}, u32[]{:S(2)}, u32[]{:S(2)}) collective-permute-start(bf16[208,1664]{1,0:T(8,128)(2,1)S(1)} %bitcast.14), channel_id=1, source_target_pairs={{0,2},{2,0},{1,3},{3,1},{4,6},{6,4},{5,7},{7,5},{8,10},{10,8},{9,1... | collective-permute-start | bytes 2076680 | tf_op jit(solution)/shard_map/ppermute | solution.py:222
  55.4 5.4 %collective-permute-start.3 = (bf16[208,1664]{1,0:T(8,128)(2,1)S(1)}, bf16[208,1664]{1,0:T(8,128)(2,1)S(1)}, u32[]{:S(2)}, u32[]{:S(2)}) collective-permute-start(bf16[208,1664]{1,0:T(8,128)(2,1)S(1)} %collective-permute-done.2.refs_0_.refs_7_), channel_id=1, source_target_pairs={{0,2},{2,0},{1,3},{3,1},{4,6},{6,4},{5,7},{7,5},{8,10},{10,8},{9,1... | collective-permute-start | bytes 2076680 | tf_op jit(solution)/shard_map/ppermute | solution.py:222
  57.4 4.4 %collective-permute-start.5 = (bf16[208,1664]{1,0:T(8,128)(2,1)}, bf16[208,1664]{1,0:T(8,128)(2,1)S(1)}, u32[]{:S(2)}, u32[]{:S(2)}) collective-permute-start(bf16[208,1664]{1,0:T(8,128)(2,1)} %collective-permute-done.4.refs_2_), channel_id=1, source_target_pairs={{0,2},{2,0},{1,3},{3,1},{4,6},{6,4},{5,7},{7,5},{8,10},{10,8},{9,1... | collective-permute-start | bytes 2076680 | tf_op jit(solution)/shard_map/ppermute | solution.py:222
  69.9 5.0 %collective-permute-start.8 = (bf16[416,1664]{1,0:T(8,128)(2,1)S(1)}, bf16[416,1664]{1,0:T(8,128)(2,1)S(1)}, u32[]{:S(2)}, u32[]{:S(2)}) collective-permute-start(bf16[416,1664]{1,0:T(8,128)(2,1)S(1)} %shard_map.111), channel_id=1, source_target_pairs={{0,2},{2,0},{1,3},{3,1},{4,6},{6,4},{5,7},{7,5},{8,10},{10,8},{9,1... | collective-permute-start | bytes 4153352 | tf_op jit(solution)/shard_map/ppermute | solution.py:222
  71.8 14.8 %collective-permute-start.7 = (bf16[128,1792]{1,0:T(8,128)(2,1)S(1)}, bf16[128,1792]{1,0:T(8,128)(2,1)S(1)}, u32[]{:S(2)}, u32[]{:S(2)}) collective-permute-start(bf16[128,1792]{1,0:T(8,128)(2,1)S(1)} %get-tuple-element.24), channel_id=1, source_target_pairs={{0,4},{4,0},{8,12},{12,8},{1,5},{5,1},{9,13},{13,9},{2,6},{6,2},{1... | collective-permute-start | bytes 1376264 | tf_op jit(solution)/shard_map/ppermute | solution.py:222
  75.9 40.1 %collective-permute-start.9 = (bf16[416,1664]{1,0:T(8,128)(2,1)S(1)}, bf16[416,1664]{1,0:T(8,128)(2,1)S(1)}, u32[]{:S(2)}, u32[]{:S(2)}) collective-permute-start(bf16[416,1664]{1,0:T(8,128)(2,1)S(1)} %shard_map.112.refs_6_), channel_id=1, source_target_pairs={{0,12},{4,8},{8,4},{12,0},{1,13},{5,9},{9,5},{13,1},{2,14},{6,10},... | collective-permute-start | bytes 4153352 | tf_op jit(solution)/shard_map/ppermute | solution.py:222
  79.6 34.3 %copy-start.2 = (s32[128,2]{0,1:T(2,128)S(1)}, s32[128,2]{0,1:T(2,128)}, u32[]{:S(2)}) copy-start(s32[128,2]{0,1:T(2,128)} %param.10) | copy-start | bytes 3076
  79.6 34.2 %copy-start.3 = (s32[128,2]{0,1:T(2,128)S(1)}, s32[128,2]{0,1:T(2,128)}, u32[]{:S(2)}) copy-start(s32[128,2]{0,1:T(2,128)} %param.11) | copy-start | bytes 3076
  79.6 34.2 %copy-start.4 = (bf16[128,2]{0,1:T(2,128)(2,1)S(1)}, bf16[128,2]{0,1:T(2,128)(2,1)}, u32[]{:S(2)}) copy-start(bf16[128,2]{0,1:T(2,128)(2,1)} %param.9) | copy-start | bytes 1540
  79.6 36.7 %collective-permute-start.10 = (bf16[416,1664]{1,0:T(8,128)(2,1)S(1)}, bf16[416,1664]{1,0:T(8,128)(2,1)S(1)}, u32[]{:S(2)}, u32[]{:S(2)}) collective-permute-start(bf16[416,1664]{1,0:T(8,128)(2,1)S(1)} %shard_map.114), channel_id=1, source_target_pairs={{0,2},{2,0},{1,3},{3,1},{4,6},{6,4},{5,7},{7,5},{8,10},{10,8},{9,1... | collective-permute-start | bytes 4153352 | tf_op jit(solution)/shard_map/ppermute | solution.py:222

commit v7 on v6

--- a/solution.py
+++ b/solution.py
@@ -317,7 +317,8 @@
     sent = far
     far = swap_weights(far)
     near = swap_core(weight_call(1, after=(sent,)))
-    back = call(pack_back_kernel, shape((SRC, BACK_BLOCKS, CAP, 128)), (part_own, part_back), 300_000_000, 2_500_000, 16)
+    mine = weight_call(0, after=(sent,))
+    back = call(pack_back_kernel, shape((SRC, BACK_BLOCKS, CAP, 128)), (part_own, part_back), 300_000_000, 2_500_000, 16, after=(mine,))
     back = lax.all_to_all(back, everywhere, split_axis=0, concat_axis=0, tiled=True)
     patch_grad, gate_grad, token = call(
         unpack_back_kernel,
@@ -327,7 +328,6 @@
         1_000_000,
         16,
     )
-    mine = weight_call(0, after=(token,))
     mine = call(partial_sum_kernel, both, (mine, far), 1_000_000, 4_000_000, 16, after=(token,))
     grad_in, grad_out = call(
         weight_sum_kernel, [shape((HS, D))] * 2, (mine, near), 1_000_000, 4_000_000, 16, after=(token,)

time: 118 us -> 117 us (level)
  no operation moved by 1% of the time
where the time goes in v7:
time: 117 us
  starting transfers between devices  44.5 us (38%)
  waiting for transfers between devices  27.1 us (23%)
  blocking collectives  26.8 us (23%)
  Pallas kernels  17.2 us (15%)
    ppermute x11, starting transfers between devices, swap(): lax.ppermute(value, axis, [(i, partner(i)) for i in range(lax.axis_size(a...  27.9 us
    all_to_all x1, blocking collectives, local(): lax.all_to_all(back, everywhere, split_axis=0, concat_axis=0, tiled=True)  26.8 us
    all_to_all x1, waiting for transfers between devices, local(): lax.all_to_all(sent, everywhere, split_axis=0, concat_axis=0, tiled=True)  20 us
    pallas_call x14, Pallas kernels, call(): pl.pallas_call(body, out_shape=out_shape, in_specs=(in_specs or [VM] * us...  17.2 us
    all_to_all x1, starting transfers between devices, local(): lax.all_to_all(sent, everywhere, split_axis=0, concat_axis=0, tiled=True)  16.6 us
    ppermute x11, waiting for transfers between devices, swap(): lax.ppermute(value, axis, [(i, partner(i)) for i in range(lax.axis_size(a...  7.09 us
  transfers between devices with their start and end apart: 12, of which 5 were waited for; matrix products, arithmetic and copies ran while one was open for 0% of the time, Pallas kernels for 9%

profile of v7, /device:TPU:6, one launch (start us, length us, event | category | flops | bytes accessed | tf_op | source)
XLA Modules:
  0.0 116.6 jit_solution(17174341938111816475)
XLA Ops:
  0.6 0.0 copy-start
  0.6 0.0 copy-start.1
  0.7 2.7 %shard_map.102 = bf16[64,13,4,128]{3,2,1,0:T(4,128)(2,1)} custom-call(bf16[2,128]{1,0:T(2,128)(2,1)} %bitcast.20, s32[2,128]{1,0:T(2,128)} %bitcast.16, s32[2,128]{1,0:T(2,128)} %bitcast.18, bf16[128,1664]{1,0:T(8,128)(2,1)} %refs_3_.1, bf16[128,1664]{1,0:T(8,128)(2,1)} %refs_4_.1), custom_call_target="tpu_custom_call" | custom-call | flops 500000000 | bytes 5000000 | tf_op jit(solution)/shard_map/pallas_call | solution.py:210
  3.4 16.6 %all-to-all-start = ((bf16[64,13,4,128]{3,2,1,0:T(4,128)(2,1)}), bf16[64,13,4,128]{3,2,1,0:T(4,128)(2,1)S(1)}, u32[]{:S(2)}, u32[]{:S(2)}) async-start(bf16[64,13,4,128]{3,2,1,0:T(4,128)(2,1)} %shard_map.102), calls=%async_computation | async-start | bytes 1703936 | tf_op jit(solution)/shard_map/all_to_all | solution.py:264
  20.0 0.0 copy-done
  20.0 2.4 %collective-permute-start.2 = (bf16[208,1664]{1,0:T(8,128)(2,1)S(1)}, bf16[208,1664]{1,0:T(8,128)(2,1)S(1)}, u32[]{:S(2)}, u32[]{:S(2)}) collective-permute-start(bf16[208,1664]{1,0:T(8,128)(2,1)S(1)} %bitcast.8), channel_id=1, source_target_pairs={{0,12},{4,8},{8,4},{12,0},{1,13},{5,9},{9,5},{13,1},{2,14},{6,10},... | collective-permute-start | bytes 2076680 | tf_op jit(solution)/shard_map/ppermute | solution.py:222
  22.4 0.0 copy-done.1
  22.4 4.7 %collective-permute-start.4 = (bf16[208,1664]{1,0:T(8,128)(2,1)S(1)}, bf16[208,1664]{1,0:T(8,128)(2,1)}, u32[]{:S(2)}, u32[]{:S(2)}) collective-permute-start(bf16[208,1664]{1,0:T(8,128)(2,1)S(1)} %bitcast.13), channel_id=1, source_target_pairs={{0,12},{4,8},{8,4},{12,0},{1,13},{5,9},{9,5},{13,1},{2,14},{6,10},... | collective-permute-start | bytes 2076680 | tf_op jit(solution)/shard_map/ppermute | solution.py:222
  27.1 20.0 %all-to-all-done.refs_0_ = bf16[64,13,4,128]{3,2,1,0:T(4,128)(2,1)S(1)} async-done(((bf16[64,13,4,128]{3,2,1,0:T(4,128)(2,1)}), bf16[64,13,4,128]{3,2,1,0:T(4,128)(2,1)S(1)}, u32[]{:S(2)}, u32[]{:S(2)}) %all-to-all-start) | async-done | bytes 852000 | tf_op jit(solution)/shard_map/all_to_all | solution.py:264
  47.1 1.2 %shard_map.103.refs_0_ = bf16[256,1664]{1,0:T(8,128)(2,1)S(1)} custom-call(bf16[64,13,4,128]{3,2,1,0:T(4,128)(2,1)S(1)} %all-to-all-done.refs_0_), custom_call_target="tpu_custom_call" | custom-call | flops 300000000 | bytes 2000000 | tf_op jit(solution)/shard_map/pallas_call | solution.py:210
  48.3 2.7 %collective-permute-start.6 = (bf16[256,1664]{1,0:T(8,128)(2,1)S(1)}, bf16[256,1664]{1,0:T(8,128)(2,1)S(1)}, u32[]{:S(2)}, u32[]{:S(2)}) collective-permute-start(bf16[256,1664]{1,0:T(8,128)(2,1)S(1)} %shard_map.103.refs_0_), channel_id=1, source_target_pairs={{0,4},{4,0},{8,12},{12,8},{1,5},{5,1},{9,13},{13,9},{2,6},{6,2},{1... | collective-permute-start | bytes 2555912 | tf_op jit(solution)/shard_map/ppermute | solution.py:222
  51.1 1.9 %collective-permute-start = (bf16[208,1664]{1,0:T(8,128)(2,1)S(1)}, bf16[208,1664]{1,0:T(8,128)(2,1)S(1)}, u32[]{:S(2)}, u32[]{:S(2)}) collective-permute-start(bf16[208,1664]{1,0:T(8,128)(2,1)S(1)} %bitcast.9), channel_id=1, source_target_pairs={{0,2},{2,0},{1,3},{3,1},{4,6},{6,4},{5,7},{7,5},{8,10},{10,8},{9,1... | collective-permute-start | bytes 2076680 | tf_op jit(solution)/shard_map/ppermute | solution.py:222
  53.0 2.4 %collective-permute-start.1 = (bf16[208,1664]{1,0:T(8,128)(2,1)S(1)}, bf16[208,1664]{1,0:T(8,128)(2,1)S(1)}, u32[]{:S(2)}, u32[]{:S(2)}) collective-permute-start(bf16[208,1664]{1,0:T(8,128)(2,1)S(1)} %bitcast.14), channel_id=1, source_target_pairs={{0,2},{2,0},{1,3},{3,1},{4,6},{6,4},{5,7},{7,5},{8,10},{10,8},{9,1... | collective-permute-start | bytes 2076680 | tf_op jit(solution)/shard_map/ppermute | solution.py:222
  55.4 0.0 collective-permute-done.2.refs_0_.refs_7_
  55.4 1.9 %collective-permute-start.3 = (bf16[208,1664]{1,0:T(8,128)(2,1)S(1)}, bf16[208,1664]{1,0:T(8,128)(2,1)S(1)}, u32[]{:S(2)}, u32[]{:S(2)}) collective-permute-start(bf16[208,1664]{1,0:T(8,128)(2,1)S(1)} %collective-permute-done.2.refs_0_.refs_7_), channel_id=1, source_target_pairs={{0,2},{2,0},{1,3},{3,1},{4,6},{6,4},{5,7},{7,5},{8,10},{10,8},{9,1... | collective-permute-start | bytes 2076680 | tf_op jit(solution)/shard_map/ppermute | solution.py:222
  57.4 0.0 collective-permute-done.4.refs_2_
  57.4 2.4 %collective-permute-start.5 = (bf16[208,1664]{1,0:T(8,128)(2,1)}, bf16[208,1664]{1,0:T(8,128)(2,1)S(1)}, u32[]{:S(2)}, u32[]{:S(2)}) collective-permute-start(bf16[208,1664]{1,0:T(8,128)(2,1)} %collective-permute-done.4.refs_2_), channel_id=1, source_target_pairs={{0,2},{2,0},{1,3},{3,1},{4,6},{6,4},{5,7},{7,5},{8,10},{10,8},{9,1... | collective-permute-start | bytes 2076680 | tf_op jit(solution)/shard_map/ppermute | solution.py:222
  59.8 0.0 collective-permute-done.refs_1_.refs_6_
  59.8 0.0 collective-permute-done.1.refs_3_
  59.8 1.0 shard_map.104
  60.8 0.0 collective-permute-done.3.refs_1_.refs_8_
  60.8 0.9 collective-permute-done.5.refs_3_
  61.7 2.1 %shard_map.105 = (bf16[1664,512]{1,0:T(8,128)(2,1)S(1)}, bf16[1664,512]{1,0:T(8,128)(2,1)S(1)}) custom-call(bf16[208,1664]{1,0:T(8,128)(2,1)S(1)} %collective-permute-done.2.refs_0_.refs_7_, bf16[208,1664]{1,0:T(8,128)(2,1)S(1)} %collective-permute-done.3.refs_1_.refs_8_, bf16[208,1664]{1,0:T(8,128)(2,1)} %collective-permute-done.4.refs_2_, ...), custom_call_target="tpu_custom_call" | custom-call | flops 1000000 | bytes 5000000 | tf_op jit(solution)/shard_map/pallas_call | solution.py:210
  63.8 1.7 %shard_map.106 = (bf16[128,1792]{1,0:T(8,128)(2,1)S(1)}, bf16[4,128,208]{2,1,0:T(8,128)(2,1)S(1)}, bf16[4,128,208]{2,1,0:T(8,128)(2,1)S(1)}) custom-call(bf16[256,1664]{1,0:T(8,128)(2,1)S(1)} %shard_map.103.refs_0_, bf16[1664,512]{1,0:T(8,128)(2,1)S(1)} %get-tuple-element.19.refs_1_, bf16[1664,512]{1,0:T(8,128)(2,1)S(1)} %get-tuple-element.20.refs_2_, ...), custom_call_target="tpu_custom_call" | custom-call | flops 1100000000 | bytes 8000000 | tf_op jit(solution)/shard_map/pallas_call | solution.py:210
  65.5 1.8 %collective-permute-done.6.refs_0_.refs_1_ = bf16[256,1664]{1,0:T(8,128)(2,1)S(1)} collective-permute-done((bf16[256,1664]{1,0:T(8,128)(2,1)S(1)}, bf16[256,1664]{1,0:T(8,128)(2,1)S(1)}, u32[]{:S(2)}, u32[]{:S(2)}) %collective-permute-start.6) | collective-permute-done | bytes 852000 | tf_op jit(solution)/shard_map/ppermute | solution.py:222
  67.3 1.7 %shard_map.107 = (bf16[128,1792]{1,0:T(8,128)(2,1)S(1)}, bf16[4,128,208]{2,1,0:T(8,128)(2,1)S(1)}, bf16[4,128,208]{2,1,0:T(8,128)(2,1)S(1)}) custom-call(bf16[256,1664]{1,0:T(8,128)(2,1)S(1)} %collective-permute-done.6.refs_0_.refs_1_, bf16[1664,512]{1,0:T(8,128)(2,1)S(1)} %get-tuple-element.19.refs_1_, bf16[1664,512]{1,0:T(8,128)(2,1)S(1)} %get-tuple-element.20.refs_2_, ...), custom_call_target="tpu_custom_call" | custom-call | flops 1100000000 | bytes 8000000 | tf_op jit(solution)/shard_map/pallas_call | solution.py:210
  68.9 1.0 shard_map.108
  69.9 1.9 %collective-permute-start.8 = (bf16[416,1664]{1,0:T(8,128)(2,1)S(1)}, bf16[416,1664]{1,0:T(8,128)(2,1)S(1)}, u32[]{:S(2)}, u32[]{:S(2)}) collective-permute-start(bf16[416,1664]{1,0:T(8,128)(2,1)S(1)} %shard_map.108), channel_id=1, source_target_pairs={{0,2},{2,0},{1,3},{3,1},{4,6},{6,4},{5,7},{7,5},{8,10},{10,8},{9,1... | collective-permute-start | bytes 4153352 | tf_op jit(solution)/shard_map/ppermute | solution.py:222
  71.8 2.7 %collective-permute-start.7 = (bf16[128,1792]{1,0:T(8,128)(2,1)S(1)}, bf16[128,1792]{1,0:T(8,128)(2,1)S(1)}, u32[]{:S(2)}, u32[]{:S(2)}) collective-permute-start(bf16[128,1792]{1,0:T(8,128)(2,1)S(1)} %get-tuple-element.24), channel_id=1, source_target_pairs={{0,4},{4,0},{8,12},{12,8},{1,5},{5,1},{9,13},{13,9},{2,6},{6,2},{1... | collective-permute-start | bytes 1376264 | tf_op jit(solution)/shard_map/ppermute | solution.py:222
  74.6 0.4 collective-permute-done.8.refs_6_
  74.9 1.0 shard_map.109.refs_6_
  75.9 2.7 %collective-permute-start.9 = (bf16[416,1664]{1,0:T(8,128)(2,1)S(1)}, bf16[416,1664]{1,0:T(8,128)(2,1)S(1)}, u32[]{:S(2)}, u32[]{:S(2)}) collective-permute-start(bf16[416,1664]{1,0:T(8,128)(2,1)S(1)} %shard_map.109.refs_6_), channel_id=1, source_target_pairs={{0,12},{4,8},{8,4},{12,0},{1,13},{5,9},{9,5},{13,1},{2,14},{6,10},... | collective-permute-start | bytes 4153352 | tf_op jit(solution)/shard_map/ppermute | solution.py:222
  78.6 1.0 shard_map.114
  79.6 2.1 %collective-permute-start.10 = (bf16[416,1664]{1,0:T(8,128)(2,1)S(1)}, bf16[416,1664]{1,0:T(8,128)(2,1)S(1)}, u32[]{:S(2)}, u32[]{:S(2)}) collective-permute-start(bf16[416,1664]{1,0:T(8,128)(2,1)S(1)} %shard_map.114), channel_id=1, source_target_pairs={{0,2},{2,0},{1,3},{3,1},{4,6},{6,4},{5,7},{7,5},{8,10},{10,8},{9,1... | collective-permute-start | bytes 4153352 | tf_op jit(solution)/shard_map/ppermute | solution.py:222
  81.7 1.0 shard_map.110.refs_2_.refs_0_
  82.6 4.0 %collective-permute-done.7.refs_1_ = bf16[128,1792]{1,0:T(8,128)(2,1)S(1)} collective-permute-done((bf16[128,1792]{1,0:T(8,128)(2,1)S(1)}, bf16[128,1792]{1,0:T(8,128)(2,1)S(1)}, u32[]{:S(2)}, u32[]{:S(2)}) %collective-permute-start.7) | collective-permute-done | bytes 458784 | tf_op jit(solution)/shard_map/ppermute | solution.py:222
  86.6 0.0 copy-start.2
  86.7 0.0 copy-start.3
  86.7 0.3 shard_map.111
  87.0 26.8 %all_to_all.10.refs_0_ = bf16[64,14,2,128]{3,2,1,0:T(2,128)(2,1)S(1)} all-to-all(bf16[64,14,2,128]{3,2,1,0:T(2,128)(2,1)S(1)} %shard_map.111), channel_id=1, replica_groups=mesh['zlo'=4,'y'=8,'x'=4,'core'=2,'zhi'=2] {'zlo','y','zhi'}, dimensions={0} | all-to-all | bytes 917504 | tf_op jit(solution)/shard_map/all_to_all | solution.py:322
  113.8 0.0 copy-done.2
  113.8 0.0 copy-done.3
  113.8 0.0 copy-done.4
  113.8 1.2 %shard_map.112 = (bf16[128,1664]{1,0:T(8,128)(2,1)}, f32[2,128]{1,0:T(2,128)}, f32[8,128]{1,0:T(8,128)S(1)}) custom-call(bf16[64,14,2,128]{3,2,1,0:T(2,128)(2,1)S(1)} %all_to_all.10.refs_0_, bf16[2,128]{1,0:T(2,128)(2,1)S(1)} %bitcast.21, s32[2,128]{1,0:T(2,128)S(1)} %bitcast.17, s32[2,128]{1,0:T(2,128)S(1)} %bitcast.19), custom_call_target="tpu_custom_call" | custom-call | flops 300000000 | bytes 1000000 | tf_op jit(solution)/shard_map/pallas_call | solution.py:210
  115.0 0.0 collective-permute-done.9.refs_1_
  115.0 0.3 shard_map.113.refs_0_
  115.3 0.0 collective-permute-done.10.refs_1_
  115.3 1.2 %shard_map.115 = (bf16[208,1664]{1,0:T(8,128)(2,1)}, bf16[208,1664]{1,0:T(8,128)(2,1)}) custom-call(bf16[416,1664]{1,0:T(8,128)(2,1)S(1)} %shard_map.113.refs_0_, bf16[416,1664]{1,0:T(8,128)(2,1)S(1)} %collective-permute-done.10.refs_1_, f32[8,128]{1,0:T(8,128)S(1)} %get-tuple-element.31.refs_2_), custom_call_target="tpu_custom_call" | custom-call | flops 1000000 | bytes 4000000 | tf_op jit(solution)/shard_map/pallas_call | solution.py:210
  (1 shorter events, 0.0 us)
Async XLA Ops:
  0.6 19.4 %copy-start = (bf16[1,208,1664]{2,1,0:T(8,128)(2,1)S(1)}, bf16[1,208,1664]{2,1,0:T(8,128)(2,1)}, u32[]{:S(2)}) copy-start(bf16[1,208,1664]{2,1,0:T(8,128)(2,1)} %param.12) | copy-start | bytes 2076676
  0.6 21.8 %copy-start.1 = (bf16[1,208,1664]{2,1,0:T(8,128)(2,1)S(1)}, bf16[1,208,1664]{2,1,0:T(8,128)(2,1)}, u32[]{:S(2)}) copy-start(bf16[1,208,1664]{2,1,0:T(8,128)(2,1)} %param.13) | copy-start | bytes 2076676
  3.4 43.7 %all-to-all-start = ((bf16[64,13,4,128]{3,2,1,0:T(4,128)(2,1)}), bf16[64,13,4,128]{3,2,1,0:T(4,128)(2,1)S(1)}, u32[]{:S(2)}, u32[]{:S(2)}) async-start(bf16[64,13,4,128]{3,2,1,0:T(4,128)(2,1)} %shard_map.102), calls=%async_computation | async-start | bytes 1703936 | tf_op jit(solution)/shard_map/all_to_all | solution.py:264
  20.0 35.4 %collective-permute-start.2 = (bf16[208,1664]{1,0:T(8,128)(2,1)S(1)}, bf16[208,1664]{1,0:T(8,128)(2,1)S(1)}, u32[]{:S(2)}, u32[]{:S(2)}) collective-permute-start(bf16[208,1664]{1,0:T(8,128)(2,1)S(1)} %bitcast.8), channel_id=1, source_target_pairs={{0,12},{4,8},{8,4},{12,0},{1,13},{5,9},{9,5},{13,1},{2,14},{6,10},... | collective-permute-start | bytes 2076680 | tf_op jit(solution)/shard_map/ppermute | solution.py:222
  22.4 34.9 %collective-permute-start.4 = (bf16[208,1664]{1,0:T(8,128)(2,1)S(1)}, bf16[208,1664]{1,0:T(8,128)(2,1)}, u32[]{:S(2)}, u32[]{:S(2)}) collective-permute-start(bf16[208,1664]{1,0:T(8,128)(2,1)S(1)} %bitcast.13), channel_id=1, source_target_pairs={{0,12},{4,8},{8,4},{12,0},{1,13},{5,9},{9,5},{13,1},{2,14},{6,10},... | collective-permute-start | bytes 2076680 | tf_op jit(solution)/shard_map/ppermute | solution.py:222
  48.3 18.9 %collective-permute-start.6 = (bf16[256,1664]{1,0:T(8,128)(2,1)S(1)}, bf16[256,1664]{1,0:T(8,128)(2,1)S(1)}, u32[]{:S(2)}, u32[]{:S(2)}) collective-permute-start(bf16[256,1664]{1,0:T(8,128)(2,1)S(1)} %shard_map.103.refs_0_), channel_id=1, source_target_pairs={{0,4},{4,0},{8,12},{12,8},{1,5},{5,1},{9,13},{13,9},{2,6},{6,2},{1... | collective-permute-start | bytes 2555912 | tf_op jit(solution)/shard_map/ppermute | solution.py:222
  51.1 8.7 %collective-permute-start = (bf16[208,1664]{1,0:T(8,128)(2,1)S(1)}, bf16[208,1664]{1,0:T(8,128)(2,1)S(1)}, u32[]{:S(2)}, u32[]{:S(2)}) collective-permute-start(bf16[208,1664]{1,0:T(8,128)(2,1)S(1)} %bitcast.9), channel_id=1, source_target_pairs={{0,2},{2,0},{1,3},{3,1},{4,6},{6,4},{5,7},{7,5},{8,10},{10,8},{9,1... | collective-permute-start | bytes 2076680 | tf_op jit(solution)/shard_map/ppermute | solution.py:222
  53.0 6.8 %collective-permute-start.1 = (bf16[208,1664]{1,0:T(8,128)(2,1)S(1)}, bf16[208,1664]{1,0:T(8,128)(2,1)S(1)}, u32[]{:S(2)}, u32[]{:S(2)}) collective-permute-start(bf16[208,1664]{1,0:T(8,128)(2,1)S(1)} %bitcast.14), channel_id=1, source_target_pairs={{0,2},{2,0},{1,3},{3,1},{4,6},{6,4},{5,7},{7,5},{8,10},{10,8},{9,1... | collective-permute-start | bytes 2076680 | tf_op jit(solution)/shard_map/ppermute | solution.py:222
  55.4 5.4 %collective-permute-start.3 = (bf16[208,1664]{1,0:T(8,128)(2,1)S(1)}, bf16[208,1664]{1,0:T(8,128)(2,1)S(1)}, u32[]{:S(2)}, u32[]{:S(2)}) collective-permute-start(bf16[208,1664]{1,0:T(8,128)(2,1)S(1)} %collective-permute-done.2.refs_0_.refs_7_), channel_id=1, source_target_pairs={{0,2},{2,0},{1,3},{3,1},{4,6},{6,4},{5,7},{7,5},{8,10},{10,8},{9,1... | collective-permute-start | bytes 2076680 | tf_op jit(solution)/shard_map/ppermute | solution.py:222
  57.4 4.4 %collective-permute-start.5 = (bf16[208,1664]{1,0:T(8,128)(2,1)}, bf16[208,1664]{1,0:T(8,128)(2,1)S(1)}, u32[]{:S(2)}, u32[]{:S(2)}) collective-permute-start(bf16[208,1664]{1,0:T(8,128)(2,1)} %collective-permute-done.4.refs_2_), channel_id=1, source_target_pairs={{0,2},{2,0},{1,3},{3,1},{4,6},{6,4},{5,7},{7,5},{8,10},{10,8},{9,1... | collective-permute-start | bytes 2076680 | tf_op jit(solution)/shard_map/ppermute | solution.py:222
  69.9 5.0 %collective-permute-start.8 = (bf16[416,1664]{1,0:T(8,128)(2,1)S(1)}, bf16[416,1664]{1,0:T(8,128)(2,1)S(1)}, u32[]{:S(2)}, u32[]{:S(2)}) collective-permute-start(bf16[416,1664]{1,0:T(8,128)(2,1)S(1)} %shard_map.108), channel_id=1, source_target_pairs={{0,2},{2,0},{1,3},{3,1},{4,6},{6,4},{5,7},{7,5},{8,10},{10,8},{9,1... | collective-permute-start | bytes 4153352 | tf_op jit(solution)/shard_map/ppermute | solution.py:222
  71.8 14.8 %collective-permute-start.7 = (bf16[128,1792]{1,0:T(8,128)(2,1)S(1)}, bf16[128,1792]{1,0:T(8,128)(2,1)S(1)}, u32[]{:S(2)}, u32[]{:S(2)}) collective-permute-start(bf16[128,1792]{1,0:T(8,128)(2,1)S(1)} %get-tuple-element.24), channel_id=1, source_target_pairs={{0,4},{4,0},{8,12},{12,8},{1,5},{5,1},{9,13},{13,9},{2,6},{6,2},{1... | collective-permute-start | bytes 1376264 | tf_op jit(solution)/shard_map/ppermute | solution.py:222
  75.9 39.1 %collective-permute-start.9 = (bf16[416,1664]{1,0:T(8,128)(2,1)S(1)}, bf16[416,1664]{1,0:T(8,128)(2,1)S(1)}, u32[]{:S(2)}, u32[]{:S(2)}) collective-permute-start(bf16[416,1664]{1,0:T(8,128)(2,1)S(1)} %shard_map.109.refs_6_), channel_id=1, source_target_pairs={{0,12},{4,8},{8,4},{12,0},{1,13},{5,9},{9,5},{13,1},{2,14},{6,10},... | collective-permute-start | bytes 4153352 | tf_op jit(solution)/shard_map/ppermute | solution.py:222
  79.6 35.7 %collective-permute-start.10 = (bf16[416,1664]{1,0:T(8,128)(2,1)S(1)}, bf16[416,1664]{1,0:T(8,128)(2,1)S(1)}, u32[]{:S(2)}, u32[]{:S(2)}) collective-permute-start(bf16[416,1664]{1,0:T(8,128)(2,1)S(1)} %shard_map.114), channel_id=1, source_target_pairs={{0,2},{2,0},{1,3},{3,1},{4,6},{6,4},{5,7},{7,5},{8,10},{10,8},{9,1... | collective-permute-start | bytes 4153352 | tf_op jit(solution)/shard_map/ppermute | solution.py:222
  86.6 27.1 %copy-start.2 = (s32[128,2]{0,1:T(2,128)S(1)}, s32[128,2]{0,1:T(2,128)}, u32[]{:S(2)}) copy-start(s32[128,2]{0,1:T(2,128)} %param.10) | copy-start | bytes 3076
  86.7 27.1 %copy-start.3 = (s32[128,2]{0,1:T(2,128)S(1)}, s32[128,2]{0,1:T(2,128)}, u32[]{:S(2)}) copy-start(s32[128,2]{0,1:T(2,128)} %param.11) | copy-start | bytes 3076
  86.7 27.1 %copy-start.4 = (bf16[128,2]{0,1:T(2,128)(2,1)S(1)}, bf16[128,2]{0,1:T(2,128)(2,1)}, u32[]{:S(2)}) copy-start(bf16[128,2]{0,1:T(2,128)(2,1)} %param.9) | copy-start | bytes 1540

commit v8 on v7

--- a/solution.py
+++ b/solution.py
@@ -90,18 +90,13 @@
         copy.wait()
 
 
-def unpack_rows_kernel(got_in, out, got, rows, sems):
-    part = SRC // 2
-    copies = start_copies([(got_in.at[pl.ds(g * part, part)], got.at[pl.ds(g * part, part)]) for g in range(2)], sems)
+def unpack_rows_kernel(got, out, rows):
     o = lax.broadcasted_iota(I32, (2 * ROWS, 4 * SRC), 0)
     c = lax.broadcasted_iota(I32, (2 * ROWS, 4 * SRC), 1)
     want = ((o & (ROWS - 1)) >> 1) * 4 + o // ROWS * 2 + (o & 1)
     sel = jnp.where(c == want, 1.0, 0.0).astype(BF16)
-    for g in range(2):
-        copies[g].wait()
-        for j in range(SEND_BLOCKS):
-            block = got[pl.ds(g * part, part), j].reshape(part * 4, 128)
-            rows[pl.ds(g * part * 4, part * 4), pl.ds(j * 128, 128)] = block
+    for j in range(SEND_BLOCKS):
+        rows[:, pl.ds(j * 128, 128)] = got[:, j].reshape(4 * SRC, 128)
     out[...] = dot(sel, rows[...]).astype(BF16)
 
 
@@ -149,6 +144,13 @@
         dot_rows(pg0[c], p0) + dot_rows(pg1[c], p1),
         dot_rows(hid0[c], u0) + dot_rows(hid1[c], u1),
     )
+
+
+def expert_and_far_kernel(*refs):
+    rows, own, pg_own, hid_own = refs[0], *refs[9:12]
+    part, pg_out, hid_out, far = refs[12:]
+    expert_kernel(*refs[:9], part, pg_out, hid_out)
+    weight_kernel(3, 0, own, rows, pg_own, pg_out, hid_own, hid_out, far)
 
 
 def weight_kernel(c, add, *refs):
@@ -269,12 +271,7 @@
         300_000_000,
         2_000_000,
         16,
-        in_specs=[HBM],
-        scratch=[
-            pltpu.VMEM((SRC, SEND_BLOCKS, 4, 128), BF16),
-            pltpu.VMEM((4 * SRC, D), BF16),
-            pltpu.SemaphoreType.DMA((2,)),
-        ],
+        scratch=[pltpu.VMEM((4 * SRC, D), BF16)],
     )
     other = swap_rows(own)
     wi11, wo11 = swap_core(wi01), swap_core(wo01)
@@ -287,18 +284,18 @@
     t_in0, t_out0 = turn_call(wi00, wi10, wo00, wo10)
     t_in1, t_out1 = turn_call(wi01, wi11, wo01, wo11)
 
-    def expert_call(rows):
-        return call(
-            expert_kernel,
-            [shape((ROWS, GW)), hidden, hidden],
-            (rows, t_in0, t_in1, t_out0, t_out1, wi00, wi10, wi01, wi11),
-            1_100_000_000,
-            8_000_000,
-            16,
-        )
-
-    part_own, pg_own, hid_own = expert_call(own)
-    part_other, pg_other, hid_other = expert_call(other)
+    weights = (t_in0, t_in1, t_out0, t_out1, wi00, wi10, wi01, wi11)
+    part_own, pg_own, hid_own = call(
+        expert_kernel, [shape((ROWS, GW)), hidden, hidden], (own, *weights), 1_100_000_000, 8_000_000, 16
+    )
+    part_other, pg_other, hid_other, far = call(
+        expert_and_far_kernel,
+        [shape((ROWS, GW)), hidden, hidden, both],
+        (other, *weights, own, pg_own, hid_own),
+        1_500_000_000,
+        10_000_000,
+        16,
+    )
     part_back = swap_rows(part_other)
     saved = (own, other, pg_own, pg_other, hid_own, hid_other)
 
@@ -313,12 +310,20 @@
             after=after,
         )
 
-    far = weight_call(2, (swap_core(weight_call(3)),))
+    far = weight_call(2, (swap_core(far),))
     sent = far
     far = swap_weights(far)
     near = swap_core(weight_call(1, after=(sent,)))
     mine = weight_call(0, after=(sent,))
-    back = call(pack_back_kernel, shape((SRC, BACK_BLOCKS, CAP, 128)), (part_own, part_back), 300_000_000, 2_500_000, 16, after=(mine,))
+    back = call(
+        pack_back_kernel,
+        shape((SRC, BACK_BLOCKS, CAP, 128)),
+        (part_own, part_back),
+        300_000_000,
+        2_500_000,
+        16,
+        after=(mine,),
+    )
     back = lax.all_to_all(back, everywhere, split_axis=0, concat_axis=0, tiled=True)
     patch_grad, gate_grad, token = call(
         unpack_back_kernel,

time: 117 us -> 117 us (level)
    pallas_call x14 -> x13, Pallas kernels: 17.2 us -> 16.6 us  [call(): pl.pallas_call(body, out_shape=out_shape, in_specs=(in_specs or [VM] * us...]
where the time goes in v8:
time: 117 us; the launch traced here: 116 us
  starting transfers between devices  44.5 us (38%)
  blocking collectives  27.3 us (23%)
  waiting for transfers between devices  27.1 us (23%)
  Pallas kernels  16.6 us (14%)
    ppermute x11, starting transfers between devices, swap(): lax.ppermute(value, axis, [(i, partner(i)) for i in range(lax.axis_size(a...  27.9 us
    all_to_all x1, blocking collectives, local(): lax.all_to_all(back, everywhere, split_axis=0, concat_axis=0, tiled=True)  27.3 us
    all_to_all x1, waiting for transfers between devices, local(): lax.all_to_all(sent, everywhere, split_axis=0, concat_axis=0, tiled=True)  20 us
    all_to_all x1, starting transfers between devices, local(): lax.all_to_all(sent, everywhere, split_axis=0, concat_axis=0, tiled=True)  16.6 us
    pallas_call x13, Pallas kernels, call(): pl.pallas_call(body, out_shape=out_shape, in_specs=(in_specs or [VM] * us...  16.6 us
    ppermute x11, waiting for transfers between devices, swap(): lax.ppermute(value, axis, [(i, partner(i)) for i in range(lax.axis_size(a...  7.08 us
  transfers between devices with their start and end apart: 12, of which 5 were waited for; matrix products, arithmetic and copies ran while one was open for 0% of the time, Pallas kernels for 9%

profile of v8, /device:TPU:6, one launch (start us, length us, event | category | flops | bytes accessed | tf_op | source)
XLA Modules:
  0.0 116.4 jit_solution(18261333791234803187)
XLA Ops:
  0.6 0.0 copy-start
  0.6 0.0 copy-start.1
  0.7 2.7 %shard_map.102 = bf16[64,13,4,128]{3,2,1,0:T(4,128)(2,1)} custom-call(bf16[2,128]{1,0:T(2,128)(2,1)} %bitcast.20, s32[2,128]{1,0:T(2,128)} %bitcast.16, s32[2,128]{1,0:T(2,128)} %bitcast.18, bf16[128,1664]{1,0:T(8,128)(2,1)} %refs_3_.1, bf16[128,1664]{1,0:T(8,128)(2,1)} %refs_4_.1), custom_call_target="tpu_custom_call" | custom-call | flops 500000000 | bytes 5000000 | tf_op jit(solution)/shard_map/pallas_call | solution.py:212
  3.4 16.6 %all-to-all-start = ((bf16[64,13,4,128]{3,2,1,0:T(4,128)(2,1)}), bf16[64,13,4,128]{3,2,1,0:T(4,128)(2,1)S(1)}, u32[]{:S(2)}, u32[]{:S(2)}) async-start(bf16[64,13,4,128]{3,2,1,0:T(4,128)(2,1)} %shard_map.102), calls=%async_computation | async-start | bytes 1703936 | tf_op jit(solution)/shard_map/all_to_all | solution.py:266
  20.0 0.0 copy-done
  20.0 2.4 %collective-permute-start.2 = (bf16[208,1664]{1,0:T(8,128)(2,1)S(1)}, bf16[208,1664]{1,0:T(8,128)(2,1)S(1)}, u32[]{:S(2)}, u32[]{:S(2)}) collective-permute-start(bf16[208,1664]{1,0:T(8,128)(2,1)S(1)} %bitcast.8), channel_id=1, source_target_pairs={{0,12},{4,8},{8,4},{12,0},{1,13},{5,9},{9,5},{13,1},{2,14},{6,10},... | collective-permute-start | bytes 2076680 | tf_op jit(solution)/shard_map/ppermute | solution.py:224
  22.4 0.0 copy-done.1
  22.4 4.7 %collective-permute-start.4 = (bf16[208,1664]{1,0:T(8,128)(2,1)S(1)}, bf16[208,1664]{1,0:T(8,128)(2,1)}, u32[]{:S(2)}, u32[]{:S(2)}) collective-permute-start(bf16[208,1664]{1,0:T(8,128)(2,1)S(1)} %bitcast.13), channel_id=1, source_target_pairs={{0,12},{4,8},{8,4},{12,0},{1,13},{5,9},{9,5},{13,1},{2,14},{6,10},... | collective-permute-start | bytes 2076680 | tf_op jit(solution)/shard_map/ppermute | solution.py:224
  27.1 20.0 %all-to-all-done.refs_0_ = bf16[64,13,4,128]{3,2,1,0:T(4,128)(2,1)S(1)} async-done(((bf16[64,13,4,128]{3,2,1,0:T(4,128)(2,1)}), bf16[64,13,4,128]{3,2,1,0:T(4,128)(2,1)S(1)}, u32[]{:S(2)}, u32[]{:S(2)}) %all-to-all-start) | async-done | bytes 852000 | tf_op jit(solution)/shard_map/all_to_all | solution.py:266
  47.1 0.7 shard_map.103.refs_0_.refs_9_
  47.8 2.7 %collective-permute-start.6 = (bf16[256,1664]{1,0:T(8,128)(2,1)S(1)}, bf16[256,1664]{1,0:T(8,128)(2,1)S(1)}, u32[]{:S(2)}, u32[]{:S(2)}) collective-permute-start(bf16[256,1664]{1,0:T(8,128)(2,1)S(1)} %shard_map.103.refs_0_.refs_9_), channel_id=1, source_target_pairs={{0,4},{4,0},{8,12},{12,8},{1,5},{5,1},{9,13},{13,9},{2,6},{6,2},{1... | collective-permute-start | bytes 2555912 | tf_op jit(solution)/shard_map/ppermute | solution.py:224
  50.6 1.9 %collective-permute-start = (bf16[208,1664]{1,0:T(8,128)(2,1)S(1)}, bf16[208,1664]{1,0:T(8,128)(2,1)S(1)}, u32[]{:S(2)}, u32[]{:S(2)}) collective-permute-start(bf16[208,1664]{1,0:T(8,128)(2,1)S(1)} %bitcast.9), channel_id=1, source_target_pairs={{0,2},{2,0},{1,3},{3,1},{4,6},{6,4},{5,7},{7,5},{8,10},{10,8},{9,1... | collective-permute-start | bytes 2076680 | tf_op jit(solution)/shard_map/ppermute | solution.py:224
  52.5 2.4 %collective-permute-start.1 = (bf16[208,1664]{1,0:T(8,128)(2,1)S(1)}, bf16[208,1664]{1,0:T(8,128)(2,1)S(1)}, u32[]{:S(2)}, u32[]{:S(2)}) collective-permute-start(bf16[208,1664]{1,0:T(8,128)(2,1)S(1)} %bitcast.14), channel_id=1, source_target_pairs={{0,2},{2,0},{1,3},{3,1},{4,6},{6,4},{5,7},{7,5},{8,10},{10,8},{9,1... | collective-permute-start | bytes 2076680 | tf_op jit(solution)/shard_map/ppermute | solution.py:224
  54.9 0.0 collective-permute-done.2.refs_0_.refs_7_
  54.9 1.9 %collective-permute-start.3 = (bf16[208,1664]{1,0:T(8,128)(2,1)S(1)}, bf16[208,1664]{1,0:T(8,128)(2,1)S(1)}, u32[]{:S(2)}, u32[]{:S(2)}) collective-permute-start(bf16[208,1664]{1,0:T(8,128)(2,1)S(1)} %collective-permute-done.2.refs_0_.refs_7_), channel_id=1, source_target_pairs={{0,2},{2,0},{1,3},{3,1},{4,6},{6,4},{5,7},{7,5},{8,10},{10,8},{9,1... | collective-permute-start | bytes 2076680 | tf_op jit(solution)/shard_map/ppermute | solution.py:224
  56.9 0.0 collective-permute-done.4.refs_2_
  56.9 2.4 %collective-permute-start.5 = (bf16[208,1664]{1,0:T(8,128)(2,1)}, bf16[208,1664]{1,0:T(8,128)(2,1)S(1)}, u32[]{:S(2)}, u32[]{:S(2)}) collective-permute-start(bf16[208,1664]{1,0:T(8,128)(2,1)} %collective-permute-done.4.refs_2_), channel_id=1, source_target_pairs={{0,2},{2,0},{1,3},{3,1},{4,6},{6,4},{5,7},{7,5},{8,10},{10,8},{9,1... | collective-permute-start | bytes 2076680 | tf_op jit(solution)/shard_map/ppermute | solution.py:224
  59.3 0.0 collective-permute-done.refs_1_.refs_6_
  59.3 0.0 collective-permute-done.1.refs_3_
  59.3 1.0 shard_map.104
  60.3 0.0 collective-permute-done.3.refs_1_.refs_8_
  60.3 0.9 collective-permute-done.5.refs_3_
  61.2 2.1 %shard_map.105 = (bf16[1664,512]{1,0:T(8,128)(2,1)S(1)}, bf16[1664,512]{1,0:T(8,128)(2,1)S(1)}) custom-call(bf16[208,1664]{1,0:T(8,128)(2,1)S(1)} %collective-permute-done.2.refs_0_.refs_7_, bf16[208,1664]{1,0:T(8,128)(2,1)S(1)} %collective-permute-done.3.refs_1_.refs_8_, bf16[208,1664]{1,0:T(8,128)(2,1)} %collective-permute-done.4.refs_2_, ...), custom_call_target="tpu_custom_call" | custom-call | flops 1000000 | bytes 5000000 | tf_op jit(solution)/shard_map/pallas_call | solution.py:212
  63.3 1.7 %shard_map.106 = (bf16[128,1792]{1,0:T(8,128)(2,1)S(1)}, bf16[4,128,208]{2,1,0:T(8,128)(2,1)S(1)}, bf16[4,128,208]{2,1,0:T(8,128)(2,1)S(1)}) custom-call(bf16[256,1664]{1,0:T(8,128)(2,1)S(1)} %shard_map.103.refs_0_.refs_9_, bf16[1664,512]{1,0:T(8,128)(2,1)S(1)} %get-tuple-element.20.refs_1_, bf16[1664,512]{1,0:T(8,128)(2,1)S(1)} %get-tuple-element.21.refs_2_, ...), custom_call_target="tpu_custom_call" | custom-call | flops 1100000000 | bytes 8000000 | tf_op jit(solution)/shard_map/pallas_call | solution.py:212
  65.0 1.8 %collective-permute-done.6.refs_0_.refs_1_ = bf16[256,1664]{1,0:T(8,128)(2,1)S(1)} collective-permute-done((bf16[256,1664]{1,0:T(8,128)(2,1)S(1)}, bf16[256,1664]{1,0:T(8,128)(2,1)S(1)}, u32[]{:S(2)}, u32[]{:S(2)}) %collective-permute-start.6) | collective-permute-done | bytes 852000 | tf_op jit(solution)/shard_map/ppermute | solution.py:224
  66.8 2.5 %shard_map.107 = (bf16[128,1792]{1,0:T(8,128)(2,1)S(1)}, bf16[4,128,208]{2,1,0:T(8,128)(2,1)S(1)}, bf16[4,128,208]{2,1,0:T(8,128)(2,1)S(1)}, bf16[416,1664]{1,0:T(8,128)(2,1)S(1)}) custom-call(bf16[256,1664]{1,0:T(8,128)(2,1)S(1)} %collective-permute-done.6.refs_0_.refs_1_, bf16[1664,512]{1,0:T(8,128)(2,1)S(1)} %get-tuple-element.20.refs_1_, ...), custom_call_target="tpu_custom_call" | custom-call | flops 1500000000 | bytes 10000000 | tf_op jit(solution)/shard_map/pallas_call | solution.py:212
  69.2 1.9 %collective-permute-start.8 = (bf16[416,1664]{1,0:T(8,128)(2,1)S(1)}, bf16[416,1664]{1,0:T(8,128)(2,1)S(1)}, u32[]{:S(2)}, u32[]{:S(2)}) collective-permute-start(bf16[416,1664]{1,0:T(8,128)(2,1)S(1)} %get-tuple-element.30), channel_id=1, source_target_pairs={{0,2},{2,0},{1,3},{3,1},{4,6},{6,4},{5,7},{7,5},{8,10},{10,8},{9,1... | collective-permute-start | bytes 4153352 | tf_op jit(solution)/shard_map/ppermute | solution.py:224
  71.2 2.7 %collective-permute-start.7 = (bf16[128,1792]{1,0:T(8,128)(2,1)S(1)}, bf16[128,1792]{1,0:T(8,128)(2,1)S(1)}, u32[]{:S(2)}, u32[]{:S(2)}) collective-permute-start(bf16[128,1792]{1,0:T(8,128)(2,1)S(1)} %get-tuple-element.27), channel_id=1, source_target_pairs={{0,4},{4,0},{8,12},{12,8},{1,5},{5,1},{9,13},{13,9},{2,6},{6,2},{1... | collective-permute-start | bytes 1376264 | tf_op jit(solution)/shard_map/ppermute | solution.py:224
  73.9 0.4 collective-permute-done.8.refs_6_
  74.3 1.0 shard_map.108.refs_6_
  75.2 2.7 %collective-permute-start.9 = (bf16[416,1664]{1,0:T(8,128)(2,1)S(1)}, bf16[416,1664]{1,0:T(8,128)(2,1)S(1)}, u32[]{:S(2)}, u32[]{:S(2)}) collective-permute-start(bf16[416,1664]{1,0:T(8,128)(2,1)S(1)} %shard_map.108.refs_6_), channel_id=1, source_target_pairs={{0,12},{4,8},{8,4},{12,0},{1,13},{5,9},{9,5},{13,1},{2,14},{6,10},... | collective-permute-start | bytes 4153352 | tf_op jit(solution)/shard_map/ppermute | solution.py:224
  77.9 1.0 shard_map.113
  78.9 2.1 %collective-permute-start.10 = (bf16[416,1664]{1,0:T(8,128)(2,1)S(1)}, bf16[416,1664]{1,0:T(8,128)(2,1)S(1)}, u32[]{:S(2)}, u32[]{:S(2)}) collective-permute-start(bf16[416,1664]{1,0:T(8,128)(2,1)S(1)} %shard_map.113), channel_id=1, source_target_pairs={{0,2},{2,0},{1,3},{3,1},{4,6},{6,4},{5,7},{7,5},{8,10},{10,8},{9,1... | collective-permute-start | bytes 4153352 | tf_op jit(solution)/shard_map/ppermute | solution.py:224
  81.0 1.0 shard_map.109.refs_2_.refs_0_
  82.0 4.0 %collective-permute-done.7.refs_1_ = bf16[128,1792]{1,0:T(8,128)(2,1)S(1)} collective-permute-done((bf16[128,1792]{1,0:T(8,128)(2,1)S(1)}, bf16[128,1792]{1,0:T(8,128)(2,1)S(1)}, u32[]{:S(2)}, u32[]{:S(2)}) %collective-permute-start.7) | collective-permute-done | bytes 458784 | tf_op jit(solution)/shard_map/ppermute | solution.py:224
  86.0 0.0 copy-start.2
  86.0 0.0 copy-start.3
  86.0 0.0 copy-start.4
  86.0 0.3 shard_map.110
  86.3 27.3 %all_to_all.10.refs_0_ = bf16[64,14,2,128]{3,2,1,0:T(2,128)(2,1)S(1)} all-to-all(bf16[64,14,2,128]{3,2,1,0:T(2,128)(2,1)S(1)} %shard_map.110), channel_id=1, replica_groups=mesh['zlo'=4,'y'=8,'x'=4,'core'=2,'zhi'=2] {'zlo','y','zhi'}, dimensions={0} | all-to-all | bytes 917504 | tf_op jit(solution)/shard_map/all_to_all | solution.py:327
  113.6 0.0 copy-done.2
  113.6 0.0 copy-done.3
  113.6 0.0 copy-done.4
  113.6 1.2 shard_map.111
  114.8 0.0 collective-permute-done.9.refs_1_
  114.8 0.3 shard_map.112.refs_0_
  115.1 0.0 collective-permute-done.10.refs_1_
  115.1 1.2 %shard_map.114 = (bf16[208,1664]{1,0:T(8,128)(2,1)}, bf16[208,1664]{1,0:T(8,128)(2,1)}) custom-call(bf16[416,1664]{1,0:T(8,128)(2,1)S(1)} %shard_map.112.refs_0_, bf16[416,1664]{1,0:T(8,128)(2,1)S(1)} %collective-permute-done.10.refs_1_, f32[8,128]{1,0:T(8,128)S(1)} %get-tuple-element.33.refs_2_), custom_call_target="tpu_custom_call" | custom-call | flops 1000000 | bytes 4000000 | tf_op jit(solution)/shard_map/pallas_call | solution.py:212
Async XLA Ops:
  0.6 19.4 %copy-start = (bf16[1,208,1664]{2,1,0:T(8,128)(2,1)S(1)}, bf16[1,208,1664]{2,1,0:T(8,128)(2,1)}, u32[]{:S(2)}) copy-start(bf16[1,208,1664]{2,1,0:T(8,128)(2,1)} %param.12) | copy-start | bytes 2076676
  0.6 21.8 %copy-start.1 = (bf16[1,208,1664]{2,1,0:T(8,128)(2,1)S(1)}, bf16[1,208,1664]{2,1,0:T(8,128)(2,1)}, u32[]{:S(2)}) copy-start(bf16[1,208,1664]{2,1,0:T(8,128)(2,1)} %param.13) | copy-start | bytes 2076676
  3.4 43.7 %all-to-all-start = ((bf16[64,13,4,128]{3,2,1,0:T(4,128)(2,1)}), bf16[64,13,4,128]{3,2,1,0:T(4,128)(2,1)S(1)}, u32[]{:S(2)}, u32[]{:S(2)}) async-start(bf16[64,13,4,128]{3,2,1,0:T(4,128)(2,1)} %shard_map.102), calls=%async_computation | async-start | bytes 1703936 | tf_op jit(solution)/shard_map/all_to_all | solution.py:266
  20.0 34.9 %collective-permute-start.2 = (bf16[208,1664]{1,0:T(8,128)(2,1)S(1)}, bf16[208,1664]{1,0:T(8,128)(2,1)S(1)}, u32[]{:S(2)}, u32[]{:S(2)}) collective-permute-start(bf16[208,1664]{1,0:T(8,128)(2,1)S(1)} %bitcast.8), channel_id=1, source_target_pairs={{0,12},{4,8},{8,4},{12,0},{1,13},{5,9},{9,5},{13,1},{2,14},{6,10},... | collective-permute-start | bytes 2076680 | tf_op jit(solution)/shard_map/ppermute | solution.py:224
  22.4 34.4 %collective-permute-start.4 = (bf16[208,1664]{1,0:T(8,128)(2,1)S(1)}, bf16[208,1664]{1,0:T(8,128)(2,1)}, u32[]{:S(2)}, u32[]{:S(2)}) collective-permute-start(bf16[208,1664]{1,0:T(8,128)(2,1)S(1)} %bitcast.13), channel_id=1, source_target_pairs={{0,12},{4,8},{8,4},{12,0},{1,13},{5,9},{9,5},{13,1},{2,14},{6,10},... | collective-permute-start | bytes 2076680 | tf_op jit(solution)/shard_map/ppermute | solution.py:224
  47.8 18.9 %collective-permute-start.6 = (bf16[256,1664]{1,0:T(8,128)(2,1)S(1)}, bf16[256,1664]{1,0:T(8,128)(2,1)S(1)}, u32[]{:S(2)}, u32[]{:S(2)}) collective-permute-start(bf16[256,1664]{1,0:T(8,128)(2,1)S(1)} %shard_map.103.refs_0_.refs_9_), channel_id=1, source_target_pairs={{0,4},{4,0},{8,12},{12,8},{1,5},{5,1},{9,13},{13,9},{2,6},{6,2},{1... | collective-permute-start | bytes 2555912 | tf_op jit(solution)/shard_map/ppermute | solution.py:224
  50.6 8.7 %collective-permute-start = (bf16[208,1664]{1,0:T(8,128)(2,1)S(1)}, bf16[208,1664]{1,0:T(8,128)(2,1)S(1)}, u32[]{:S(2)}, u32[]{:S(2)}) collective-permute-start(bf16[208,1664]{1,0:T(8,128)(2,1)S(1)} %bitcast.9), channel_id=1, source_target_pairs={{0,2},{2,0},{1,3},{3,1},{4,6},{6,4},{5,7},{7,5},{8,10},{10,8},{9,1... | collective-permute-start | bytes 2076680 | tf_op jit(solution)/shard_map/ppermute | solution.py:224
  52.5 6.8 %collective-permute-start.1 = (bf16[208,1664]{1,0:T(8,128)(2,1)S(1)}, bf16[208,1664]{1,0:T(8,128)(2,1)S(1)}, u32[]{:S(2)}, u32[]{:S(2)}) collective-permute-start(bf16[208,1664]{1,0:T(8,128)(2,1)S(1)} %bitcast.14), channel_id=1, source_target_pairs={{0,2},{2,0},{1,3},{3,1},{4,6},{6,4},{5,7},{7,5},{8,10},{10,8},{9,1... | collective-permute-start | bytes 2076680 | tf_op jit(solution)/shard_map/ppermute | solution.py:224
  54.9 5.4 %collective-permute-start.3 = (bf16[208,1664]{1,0:T(8,128)(2,1)S(1)}, bf16[208,1664]{1,0:T(8,128)(2,1)S(1)}, u32[]{:S(2)}, u32[]{:S(2)}) collective-permute-start(bf16[208,1664]{1,0:T(8,128)(2,1)S(1)} %collective-permute-done.2.refs_0_.refs_7_), channel_id=1, source_target_pairs={{0,2},{2,0},{1,3},{3,1},{4,6},{6,4},{5,7},{7,5},{8,10},{10,8},{9,1... | collective-permute-start | bytes 2076680 | tf_op jit(solution)/shard_map/ppermute | solution.py:224
  56.9 4.4 %collective-permute-start.5 = (bf16[208,1664]{1,0:T(8,128)(2,1)}, bf16[208,1664]{1,0:T(8,128)(2,1)S(1)}, u32[]{:S(2)}, u32[]{:S(2)}) collective-permute-start(bf16[208,1664]{1,0:T(8,128)(2,1)} %collective-permute-done.4.refs_2_), channel_id=1, source_target_pairs={{0,2},{2,0},{1,3},{3,1},{4,6},{6,4},{5,7},{7,5},{8,10},{10,8},{9,1... | collective-permute-start | bytes 2076680 | tf_op jit(solution)/shard_map/ppermute | solution.py:224
  69.2 5.0 %collective-permute-start.8 = (bf16[416,1664]{1,0:T(8,128)(2,1)S(1)}, bf16[416,1664]{1,0:T(8,128)(2,1)S(1)}, u32[]{:S(2)}, u32[]{:S(2)}) collective-permute-start(bf16[416,1664]{1,0:T(8,128)(2,1)S(1)} %get-tuple-element.30), channel_id=1, source_target_pairs={{0,2},{2,0},{1,3},{3,1},{4,6},{6,4},{5,7},{7,5},{8,10},{10,8},{9,1... | collective-permute-start | bytes 4153352 | tf_op jit(solution)/shard_map/ppermute | solution.py:224
  71.2 14.8 %collective-permute-start.7 = (bf16[128,1792]{1,0:T(8,128)(2,1)S(1)}, bf16[128,1792]{1,0:T(8,128)(2,1)S(1)}, u32[]{:S(2)}, u32[]{:S(2)}) collective-permute-start(bf16[128,1792]{1,0:T(8,128)(2,1)S(1)} %get-tuple-element.27), channel_id=1, source_target_pairs={{0,4},{4,0},{8,12},{12,8},{1,5},{5,1},{9,13},{13,9},{2,6},{6,2},{1... | collective-permute-start | bytes 1376264 | tf_op jit(solution)/shard_map/ppermute | solution.py:224
  75.2 39.6 %collective-permute-start.9 = (bf16[416,1664]{1,0:T(8,128)(2,1)S(1)}, bf16[416,1664]{1,0:T(8,128)(2,1)S(1)}, u32[]{:S(2)}, u32[]{:S(2)}) collective-permute-start(bf16[416,1664]{1,0:T(8,128)(2,1)S(1)} %shard_map.108.refs_6_), channel_id=1, source_target_pairs={{0,12},{4,8},{8,4},{12,0},{1,13},{5,9},{9,5},{13,1},{2,14},{6,10},... | collective-permute-start | bytes 4153352 | tf_op jit(solution)/shard_map/ppermute | solution.py:224
  78.9 36.2 %collective-permute-start.10 = (bf16[416,1664]{1,0:T(8,128)(2,1)S(1)}, bf16[416,1664]{1,0:T(8,128)(2,1)S(1)}, u32[]{:S(2)}, u32[]{:S(2)}) collective-permute-start(bf16[416,1664]{1,0:T(8,128)(2,1)S(1)} %shard_map.113), channel_id=1, source_target_pairs={{0,2},{2,0},{1,3},{3,1},{4,6},{6,4},{5,7},{7,5},{8,10},{10,8},{9,1... | collective-permute-start | bytes 4153352 | tf_op jit(solution)/shard_map/ppermute | solution.py:224
  86.0 27.6 %copy-start.2 = (s32[128,2]{0,1:T(2,128)S(1)}, s32[128,2]{0,1:T(2,128)}, u32[]{:S(2)}) copy-start(s32[128,2]{0,1:T(2,128)} %param.10) | copy-start | bytes 3076
  86.0 27.6 %copy-start.3 = (s32[128,2]{0,1:T(2,128)S(1)}, s32[128,2]{0,1:T(2,128)}, u32[]{:S(2)}) copy-start(s32[128,2]{0,1:T(2,128)} %param.11) | copy-start | bytes 3076
  86.0 27.6 %copy-start.4 = (bf16[128,2]{0,1:T(2,128)(2,1)S(1)}, bf16[128,2]{0,1:T(2,128)(2,1)}, u32[]{:S(2)}) copy-start(bf16[128,2]{0,1:T(2,128)(2,1)} %param.9) | copy-start | bytes 1540

commit v9 on v8

--- a/solution.py
+++ b/solution.py
@@ -168,30 +168,30 @@
     out[...] = (own[...].astype(F32) + far[...].astype(F32)).astype(BF16)
 
 
-def weight_sum_kernel(own, near, out_in, out_out):
-    for k, out in enumerate((out_in, out_out)):
-        rows = pl.ds(k * HS, HS)
-        out[...] = (own[rows, :].astype(F32) + near[rows, :].astype(F32)).astype(BF16)
-
-
 def pack_back_kernel(i0, i1, out):
     total = (i0[...].astype(F32) + i1[...].astype(F32)).astype(BF16)
     for j in range(BACK_BLOCKS):
         out[:, j] = total[:, j * 128 : (j + 1) * 128].reshape(SRC, CAP, 128)
 
 
-def unpack_back_kernel(got, gates, ids, slots, patch_grad, gate_grad, token):
-    token[...] = jnp.zeros_like(token)
+def mask_kernel(gates, ids, slots, masks, wide_gates):
     m0, m1, _ = slot_match(ids[...], slots[...], CAP)
-    sel = jnp.where(m0 | m1, 1.0, 0.0).astype(BF16)
+    for k, m in enumerate((m0, m1, m0 | m1)):
+        masks[k] = jnp.where(m, 1.0, 0.0).astype(BF16)
+    wide_gates[...] = gates[...].astype(F32)
+
+
+def last_kernel(got, masks, wide_gates, own, near, patch_grad, gate_grad, out_in, out_out, sums, rows, sems):
+    sums[...] = (own[...].astype(F32) + near[...].astype(F32)).astype(BF16)
+    copies = start_copies([(sums.at[pl.ds(0, HS), :], out_in), (sums.at[pl.ds(HS, HS), :], out_out)], sems)
     for j in range(SEND_BLOCKS):
-        rows = got[:, j].reshape(ROWS, 128)
-        patch_grad[:, pl.ds(j * 128, 128)] = dot_rows(sel, rows).astype(BF16)
+        rows[:, pl.ds(j * 128, 128)] = got[:, j].reshape(ROWS, 128)
+    patch_grad[...] = dot_rows(masks[2], rows[...]).astype(BF16)
     gate_block = got[:, SEND_BLOCKS].reshape(ROWS, 128)
-    g = gates[...].astype(F32)
-    for k, m in enumerate((m0, m1)):
-        sel = jnp.where(m, 1.0, 0.0).astype(BF16)
-        gate_grad[k : k + 1, :] = dot_rows(gate_block, sel)[0:1, :] / g[k : k + 1, :]
+    for k in range(2):
+        gate_grad[k : k + 1, :] = dot_rows(gate_block, masks[k])[0:1, :] / wide_gates[k : k + 1, :]
+    for copy in copies:
+        copy.wait()
 
 
 def shape(dims, kind=BF16):
@@ -315,6 +315,15 @@
     far = swap_weights(far)
     near = swap_core(weight_call(1, after=(sent,)))
     mine = weight_call(0, after=(sent,))
+    masks, wide_gates = call(
+        mask_kernel,
+        [shape((3, ROWS, T)), shape((2, T), F32)],
+        (gates, ids, slots),
+        1_000_000,
+        100_000,
+        16,
+        after=(sent,),
+    )
     back = call(
         pack_back_kernel,
         shape((SRC, BACK_BLOCKS, CAP, 128)),
@@ -322,20 +331,19 @@
         300_000_000,
         2_500_000,
         16,
-        after=(mine,),
+        after=(mine, masks),
     )
     back = lax.all_to_all(back, everywhere, split_axis=0, concat_axis=0, tiled=True)
-    patch_grad, gate_grad, token = call(
-        unpack_back_kernel,
-        [shape((T, D)), shape((2, T), F32), shape((8, 128), F32)],
-        (back, gates, ids, slots),
+    mine = call(partial_sum_kernel, both, (mine, far), 1_000_000, 4_000_000, 16, after=(back,))
+    patch_grad, gate_grad, grad_in, grad_out = call(
+        last_kernel,
+        [shape((T, D)), shape((2, T), F32), shape((HS, D)), shape((HS, D))],
+        (back, masks, wide_gates, mine, near),
         300_000_000,
-        1_000_000,
-        16,
-    )
-    mine = call(partial_sum_kernel, both, (mine, far), 1_000_000, 4_000_000, 16, after=(token,))
-    grad_in, grad_out = call(
-        weight_sum_kernel, [shape((HS, D))] * 2, (mine, near), 1_000_000, 4_000_000, 16, after=(token,)
+        6_000_000,
+        16,
+        out_specs=[VM, VM, HBM, HBM],
+        scratch=[pltpu.VMEM((2 * HS, D), BF16), pltpu.VMEM((ROWS, D), BF16), pltpu.SemaphoreType.DMA((2,))],
     )
     return patch_grad, gate_grad.T, grad_in[None], grad_out[None]
 

time: 117 us -> 118 us (level)
  transfers between devices with their start and end apart: 12 -> 12, of which waited for: 5 -> 5; matrix products, arithmetic and copies ran while one was open for 0% -> 0% of each run, Pallas kernels for 9% -> 8%
where the time goes in v9:
time: 118 us; the launch traced here: 117 us
  starting transfers between devices  44.6 us (38%)
  blocking collectives  27.3 us (23%)
  waiting for transfers between devices  26.8 us (23%)
  Pallas kernels  17.2 us (15%)
    ppermute x11, starting transfers between devices, swap(): lax.ppermute(value, axis, [(i, partner(i)) for i in range(lax.axis_size(a...  28 us
    all_to_all x1, blocking collectives, local(): lax.all_to_all(back, everywhere, split_axis=0, concat_axis=0, tiled=True)  27.3 us
    all_to_all x1, waiting for transfers between devices, local(): lax.all_to_all(sent, everywhere, split_axis=0, concat_axis=0, tiled=True)  20 us
    pallas_call x13, Pallas kernels, call(): pl.pallas_call(body, out_shape=out_shape, in_specs=(in_specs or [VM] * us...  17.2 us
    all_to_all x1, starting transfers between devices, local(): lax.all_to_all(sent, everywhere, split_axis=0, concat_axis=0, tiled=True)  16.6 us
    ppermute x11, waiting for transfers between devices, swap(): lax.ppermute(value, axis, [(i, partner(i)) for i in range(lax.axis_size(a...  6.82 us
  transfers between devices with their start and end apart: 12, of which 5 were waited for; matrix products, arithmetic and copies ran while one was open for 0% of the time, Pallas kernels for 8%

profile of v9, /device:TPU:6, one launch (start us, length us, event | category | flops | bytes accessed | tf_op | source)
XLA Modules:
  0.0 117.1 jit_solution(3691403020907451858)
XLA Ops:
  0.6 0.0 copy-start
  0.6 0.0 copy-start.1
  0.7 2.7 %shard_map.102 = bf16[64,13,4,128]{3,2,1,0:T(4,128)(2,1)} custom-call(bf16[2,128]{1,0:T(2,128)(2,1)} %bitcast.20, s32[2,128]{1,0:T(2,128)} %bitcast.16, s32[2,128]{1,0:T(2,128)} %bitcast.18, bf16[128,1664]{1,0:T(8,128)(2,1)} %refs_3_.1, bf16[128,1664]{1,0:T(8,128)(2,1)} %refs_4_.1), custom_call_target="tpu_custom_call" | custom-call | flops 500000000 | bytes 5000000 | tf_op jit(solution)/shard_map/pallas_call | solution.py:212
  3.4 16.6 %all-to-all-start = ((bf16[64,13,4,128]{3,2,1,0:T(4,128)(2,1)}), bf16[64,13,4,128]{3,2,1,0:T(4,128)(2,1)S(1)}, u32[]{:S(2)}, u32[]{:S(2)}) async-start(bf16[64,13,4,128]{3,2,1,0:T(4,128)(2,1)} %shard_map.102), calls=%async_computation | async-start | bytes 1703936 | tf_op jit(solution)/shard_map/all_to_all | solution.py:266
  20.0 0.0 copy-done
  20.0 2.4 %collective-permute-start.2 = (bf16[208,1664]{1,0:T(8,128)(2,1)S(1)}, bf16[208,1664]{1,0:T(8,128)(2,1)S(1)}, u32[]{:S(2)}, u32[]{:S(2)}) collective-permute-start(bf16[208,1664]{1,0:T(8,128)(2,1)S(1)} %bitcast.8), channel_id=1, source_target_pairs={{0,12},{4,8},{8,4},{12,0},{1,13},{5,9},{9,5},{13,1},{2,14},{6,10},... | collective-permute-start | bytes 2076680 | tf_op jit(solution)/shard_map/ppermute | solution.py:224
  22.4 0.0 copy-done.1
  22.4 4.7 %collective-permute-start.4 = (bf16[208,1664]{1,0:T(8,128)(2,1)S(1)}, bf16[208,1664]{1,0:T(8,128)(2,1)}, u32[]{:S(2)}, u32[]{:S(2)}) collective-permute-start(bf16[208,1664]{1,0:T(8,128)(2,1)S(1)} %bitcast.13), channel_id=1, source_target_pairs={{0,12},{4,8},{8,4},{12,0},{1,13},{5,9},{9,5},{13,1},{2,14},{6,10},... | collective-permute-start | bytes 2076680 | tf_op jit(solution)/shard_map/ppermute | solution.py:224
  27.1 20.0 %all-to-all-done.refs_0_ = bf16[64,13,4,128]{3,2,1,0:T(4,128)(2,1)S(1)} async-done(((bf16[64,13,4,128]{3,2,1,0:T(4,128)(2,1)}), bf16[64,13,4,128]{3,2,1,0:T(4,128)(2,1)S(1)}, u32[]{:S(2)}, u32[]{:S(2)}) %all-to-all-start) | async-done | bytes 852000 | tf_op jit(solution)/shard_map/all_to_all | solution.py:266
  47.1 0.7 shard_map.103.refs_0_.refs_9_
  47.8 2.7 %collective-permute-start.6 = (bf16[256,1664]{1,0:T(8,128)(2,1)S(1)}, bf16[256,1664]{1,0:T(8,128)(2,1)S(1)}, u32[]{:S(2)}, u32[]{:S(2)}) collective-permute-start(bf16[256,1664]{1,0:T(8,128)(2,1)S(1)} %shard_map.103.refs_0_.refs_9_), channel_id=1, source_target_pairs={{0,4},{4,0},{8,12},{12,8},{1,5},{5,1},{9,13},{13,9},{2,6},{6,2},{1... | collective-permute-start | bytes 2555912 | tf_op jit(solution)/shard_map/ppermute | solution.py:224
  50.6 1.9 %collective-permute-start = (bf16[208,1664]{1,0:T(8,128)(2,1)S(1)}, bf16[208,1664]{1,0:T(8,128)(2,1)S(1)}, u32[]{:S(2)}, u32[]{:S(2)}) collective-permute-start(bf16[208,1664]{1,0:T(8,128)(2,1)S(1)} %bitcast.9), channel_id=1, source_target_pairs={{0,2},{2,0},{1,3},{3,1},{4,6},{6,4},{5,7},{7,5},{8,10},{10,8},{9,1... | collective-permute-start | bytes 2076680 | tf_op jit(solution)/shard_map/ppermute | solution.py:224
  52.5 2.4 %collective-permute-start.1 = (bf16[208,1664]{1,0:T(8,128)(2,1)S(1)}, bf16[208,1664]{1,0:T(8,128)(2,1)S(1)}, u32[]{:S(2)}, u32[]{:S(2)}) collective-permute-start(bf16[208,1664]{1,0:T(8,128)(2,1)S(1)} %bitcast.14), channel_id=1, source_target_pairs={{0,2},{2,0},{1,3},{3,1},{4,6},{6,4},{5,7},{7,5},{8,10},{10,8},{9,1... | collective-permute-start | bytes 2076680 | tf_op jit(solution)/shard_map/ppermute | solution.py:224
  54.9 0.0 collective-permute-done.2.refs_0_.refs_7_
  54.9 1.9 %collective-permute-start.3 = (bf16[208,1664]{1,0:T(8,128)(2,1)S(1)}, bf16[208,1664]{1,0:T(8,128)(2,1)S(1)}, u32[]{:S(2)}, u32[]{:S(2)}) collective-permute-start(bf16[208,1664]{1,0:T(8,128)(2,1)S(1)} %collective-permute-done.2.refs_0_.refs_7_), channel_id=1, source_target_pairs={{0,2},{2,0},{1,3},{3,1},{4,6},{6,4},{5,7},{7,5},{8,10},{10,8},{9,1... | collective-permute-start | bytes 2076680 | tf_op jit(solution)/shard_map/ppermute | solution.py:224
  56.9 0.0 collective-permute-done.4.refs_2_
  56.9 2.4 %collective-permute-start.5 = (bf16[208,1664]{1,0:T(8,128)(2,1)}, bf16[208,1664]{1,0:T(8,128)(2,1)S(1)}, u32[]{:S(2)}, u32[]{:S(2)}) collective-permute-start(bf16[208,1664]{1,0:T(8,128)(2,1)} %collective-permute-done.4.refs_2_), channel_id=1, source_target_pairs={{0,2},{2,0},{1,3},{3,1},{4,6},{6,4},{5,7},{7,5},{8,10},{10,8},{9,1... | collective-permute-start | bytes 2076680 | tf_op jit(solution)/shard_map/ppermute | solution.py:224
  59.3 0.0 collective-permute-done.refs_1_.refs_6_
  59.3 0.0 collective-permute-done.1.refs_3_
  59.3 1.0 shard_map.104
  60.3 0.0 collective-permute-done.3.refs_1_.refs_8_
  60.3 0.9 collective-permute-done.5.refs_3_
  61.2 2.1 %shard_map.105 = (bf16[1664,512]{1,0:T(8,128)(2,1)S(1)}, bf16[1664,512]{1,0:T(8,128)(2,1)S(1)}) custom-call(bf16[208,1664]{1,0:T(8,128)(2,1)S(1)} %collective-permute-done.2.refs_0_.refs_7_, bf16[208,1664]{1,0:T(8,128)(2,1)S(1)} %collective-permute-done.3.refs_1_.refs_8_, bf16[208,1664]{1,0:T(8,128)(2,1)} %collective-permute-done.4.refs_2_, ...), custom_call_target="tpu_custom_call" | custom-call | flops 1000000 | bytes 5000000 | tf_op jit(solution)/shard_map/pallas_call | solution.py:212
  63.3 1.7 %shard_map.106 = (bf16[128,1792]{1,0:T(8,128)(2,1)S(1)}, bf16[4,128,208]{2,1,0:T(8,128)(2,1)S(1)}, bf16[4,128,208]{2,1,0:T(8,128)(2,1)S(1)}) custom-call(bf16[256,1664]{1,0:T(8,128)(2,1)S(1)} %shard_map.103.refs_0_.refs_9_, bf16[1664,512]{1,0:T(8,128)(2,1)S(1)} %get-tuple-element.21.refs_1_, bf16[1664,512]{1,0:T(8,128)(2,1)S(1)} %get-tuple-element.22.refs_2_, ...), custom_call_target="tpu_custom_call" | custom-call | flops 1100000000 | bytes 8000000 | tf_op jit(solution)/shard_map/pallas_call | solution.py:212
  65.0 1.7 %collective-permute-done.6.refs_0_.refs_1_ = bf16[256,1664]{1,0:T(8,128)(2,1)S(1)} collective-permute-done((bf16[256,1664]{1,0:T(8,128)(2,1)S(1)}, bf16[256,1664]{1,0:T(8,128)(2,1)S(1)}, u32[]{:S(2)}, u32[]{:S(2)}) %collective-permute-start.6) | collective-permute-done | bytes 852000 | tf_op jit(solution)/shard_map/ppermute | solution.py:224
  66.8 2.5 %shard_map.107 = (bf16[128,1792]{1,0:T(8,128)(2,1)S(1)}, bf16[4,128,208]{2,1,0:T(8,128)(2,1)S(1)}, bf16[4,128,208]{2,1,0:T(8,128)(2,1)S(1)}, bf16[416,1664]{1,0:T(8,128)(2,1)S(1)}) custom-call(bf16[256,1664]{1,0:T(8,128)(2,1)S(1)} %collective-permute-done.6.refs_0_.refs_1_, bf16[1664,512]{1,0:T(8,128)(2,1)S(1)} %get-tuple-element.21.refs_1_, ...), custom_call_target="tpu_custom_call" | custom-call | flops 1500000000 | bytes 10000000 | tf_op jit(solution)/shard_map/pallas_call | solution.py:212
  69.2 1.9 %collective-permute-start.8 = (bf16[416,1664]{1,0:T(8,128)(2,1)S(1)}, bf16[416,1664]{1,0:T(8,128)(2,1)S(1)}, u32[]{:S(2)}, u32[]{:S(2)}) collective-permute-start(bf16[416,1664]{1,0:T(8,128)(2,1)S(1)} %get-tuple-element.31), channel_id=1, source_target_pairs={{0,2},{2,0},{1,3},{3,1},{4,6},{6,4},{5,7},{7,5},{8,10},{10,8},{9,1... | collective-permute-start | bytes 4153352 | tf_op jit(solution)/shard_map/ppermute | solution.py:224
  71.2 2.7 %collective-permute-start.7 = (bf16[128,1792]{1,0:T(8,128)(2,1)S(1)}, bf16[128,1792]{1,0:T(8,128)(2,1)S(1)}, u32[]{:S(2)}, u32[]{:S(2)}) collective-permute-start(bf16[128,1792]{1,0:T(8,128)(2,1)S(1)} %get-tuple-element.28), channel_id=1, source_target_pairs={{0,4},{4,0},{8,12},{12,8},{1,5},{5,1},{9,13},{13,9},{2,6},{6,2},{1... | collective-permute-start | bytes 1376264 | tf_op jit(solution)/shard_map/ppermute | solution.py:224
  73.9 0.4 collective-permute-done.8.refs_6_
  74.3 1.0 shard_map.108.refs_6_.refs_3_
  75.2 0.0 copy-start.2
  75.2 0.0 copy-start.3
  75.2 0.0 copy-start.4
  75.3 2.8 %collective-permute-start.9 = (bf16[416,1664]{1,0:T(8,128)(2,1)S(1)}, bf16[416,1664]{1,0:T(8,128)(2,1)S(1)}, u32[]{:S(2)}, u32[]{:S(2)}) collective-permute-start(bf16[416,1664]{1,0:T(8,128)(2,1)S(1)} %shard_map.108.refs_6_.refs_3_), channel_id=1, source_target_pairs={{0,12},{4,8},{8,4},{12,0},{1,13},{5,9},{9,5},{13,1},{2,14},{6,10},... | collective-permute-start | bytes 4153352 | tf_op jit(solution)/shard_map/ppermute | solution.py:224
  78.1 1.0 shard_map.113
  79.1 2.1 %collective-permute-start.10 = (bf16[416,1664]{1,0:T(8,128)(2,1)S(1)}, bf16[416,1664]{1,0:T(8,128)(2,1)S(1)}, u32[]{:S(2)}, u32[]{:S(2)}) collective-permute-start(bf16[416,1664]{1,0:T(8,128)(2,1)S(1)} %shard_map.113), channel_id=1, source_target_pairs={{0,2},{2,0},{1,3},{3,1},{4,6},{6,4},{5,7},{7,5},{8,10},{10,8},{9,1... | collective-permute-start | bytes 4153352 | tf_op jit(solution)/shard_map/ppermute | solution.py:224
  81.2 0.0 copy-done.2
  81.2 0.0 copy-done.3
  81.2 0.0 copy-done.4
  81.2 1.0 shard_map.109.refs_2_.refs_0_
  82.2 3.8 %collective-permute-done.7.refs_1_ = bf16[128,1792]{1,0:T(8,128)(2,1)S(1)} collective-permute-done((bf16[128,1792]{1,0:T(8,128)(2,1)S(1)}, bf16[128,1792]{1,0:T(8,128)(2,1)S(1)}, u32[]{:S(2)}, u32[]{:S(2)}) %collective-permute-start.7) | collective-permute-done | bytes 458784 | tf_op jit(solution)/shard_map/ppermute | solution.py:224
  86.0 0.3 shard_map.111
  86.3 27.3 %all_to_all.10.refs_2_.refs_0_ = bf16[64,14,2,128]{3,2,1,0:T(2,128)(2,1)S(1)} all-to-all(bf16[64,14,2,128]{3,2,1,0:T(2,128)(2,1)S(1)} %shard_map.111), channel_id=1, replica_groups=mesh['zlo'=4,'y'=8,'x'=4,'core'=2,'zhi'=2] {'zlo','y','zhi'}, dimensions={0} | all-to-all | bytes 917504 | tf_op jit(solution)/shard_map/all_to_all | solution.py:336
  113.6 0.0 collective-permute-done.9.refs_1_
  113.6 0.3 shard_map.112.refs_3_
  113.9 0.0 collective-permute-done.10.refs_4_
  114.0 3.0 %shard_map.114 = (bf16[128,1664]{1,0:T(8,128)(2,1)}, f32[2,128]{1,0:T(2,128)}, bf16[208,1664]{1,0:T(8,128)(2,1)}, bf16[208,1664]{1,0:T(8,128)(2,1)}) custom-call(bf16[64,14,2,128]{3,2,1,0:T(2,128)(2,1)S(1)} %all_to_all.10.refs_2_.refs_0_, bf16[3,128,128]{2,1,0:T(8,128)(2,1)S(1)} %get-tuple-element.32.refs_3_.refs_1_, ...), custom_call_target="tpu_custom_call" | custom-call | flops 300000000 | bytes 6000000 | tf_op jit(solution)/shard_map/pallas_call | solution.py:212
  (1 shorter events, 0.0 us)
Async XLA Ops:
  0.6 19.4 %copy-start = (bf16[1,208,1664]{2,1,0:T(8,128)(2,1)S(1)}, bf16[1,208,1664]{2,1,0:T(8,128)(2,1)}, u32[]{:S(2)}) copy-start(bf16[1,208,1664]{2,1,0:T(8,128)(2,1)} %param.12) | copy-start | bytes 2076676
  0.6 21.8 %copy-start.1 = (bf16[1,208,1664]{2,1,0:T(8,128)(2,1)S(1)}, bf16[1,208,1664]{2,1,0:T(8,128)(2,1)}, u32[]{:S(2)}) copy-start(bf16[1,208,1664]{2,1,0:T(8,128)(2,1)} %param.13) | copy-start | bytes 2076676
  3.4 43.7 %all-to-all-start = ((bf16[64,13,4,128]{3,2,1,0:T(4,128)(2,1)}), bf16[64,13,4,128]{3,2,1,0:T(4,128)(2,1)S(1)}, u32[]{:S(2)}, u32[]{:S(2)}) async-start(bf16[64,13,4,128]{3,2,1,0:T(4,128)(2,1)} %shard_map.102), calls=%async_computation | async-start | bytes 1703936 | tf_op jit(solution)/shard_map/all_to_all | solution.py:266
  20.0 34.9 %collective-permute-start.2 = (bf16[208,1664]{1,0:T(8,128)(2,1)S(1)}, bf16[208,1664]{1,0:T(8,128)(2,1)S(1)}, u32[]{:S(2)}, u32[]{:S(2)}) collective-permute-start(bf16[208,1664]{1,0:T(8,128)(2,1)S(1)} %bitcast.8), channel_id=1, source_target_pairs={{0,12},{4,8},{8,4},{12,0},{1,13},{5,9},{9,5},{13,1},{2,14},{6,10},... | collective-permute-start | bytes 2076680 | tf_op jit(solution)/shard_map/ppermute | solution.py:224
  22.4 34.4 %collective-permute-start.4 = (bf16[208,1664]{1,0:T(8,128)(2,1)S(1)}, bf16[208,1664]{1,0:T(8,128)(2,1)}, u32[]{:S(2)}, u32[]{:S(2)}) collective-permute-start(bf16[208,1664]{1,0:T(8,128)(2,1)S(1)} %bitcast.13), channel_id=1, source_target_pairs={{0,12},{4,8},{8,4},{12,0},{1,13},{5,9},{9,5},{13,1},{2,14},{6,10},... | collective-permute-start | bytes 2076680 | tf_op jit(solution)/shard_map/ppermute | solution.py:224
  47.8 18.9 %collective-permute-start.6 = (bf16[256,1664]{1,0:T(8,128)(2,1)S(1)}, bf16[256,1664]{1,0:T(8,128)(2,1)S(1)}, u32[]{:S(2)}, u32[]{:S(2)}) collective-permute-start(bf16[256,1664]{1,0:T(8,128)(2,1)S(1)} %shard_map.103.refs_0_.refs_9_), channel_id=1, source_target_pairs={{0,4},{4,0},{8,12},{12,8},{1,5},{5,1},{9,13},{13,9},{2,6},{6,2},{1... | collective-permute-start | bytes 2555912 | tf_op jit(solution)/shard_map/ppermute | solution.py:224
  50.6 8.7 %collective-permute-start = (bf16[208,1664]{1,0:T(8,128)(2,1)S(1)}, bf16[208,1664]{1,0:T(8,128)(2,1)S(1)}, u32[]{:S(2)}, u32[]{:S(2)}) collective-permute-start(bf16[208,1664]{1,0:T(8,128)(2,1)S(1)} %bitcast.9), channel_id=1, source_target_pairs={{0,2},{2,0},{1,3},{3,1},{4,6},{6,4},{5,7},{7,5},{8,10},{10,8},{9,1... | collective-permute-start | bytes 2076680 | tf_op jit(solution)/shard_map/ppermute | solution.py:224
  52.5 6.8 %collective-permute-start.1 = (bf16[208,1664]{1,0:T(8,128)(2,1)S(1)}, bf16[208,1664]{1,0:T(8,128)(2,1)S(1)}, u32[]{:S(2)}, u32[]{:S(2)}) collective-permute-start(bf16[208,1664]{1,0:T(8,128)(2,1)S(1)} %bitcast.14), channel_id=1, source_target_pairs={{0,2},{2,0},{1,3},{3,1},{4,6},{6,4},{5,7},{7,5},{8,10},{10,8},{9,1... | collective-permute-start | bytes 2076680 | tf_op jit(solution)/shard_map/ppermute | solution.py:224
  54.9 5.4 %collective-permute-start.3 = (bf16[208,1664]{1,0:T(8,128)(2,1)S(1)}, bf16[208,1664]{1,0:T(8,128)(2,1)S(1)}, u32[]{:S(2)}, u32[]{:S(2)}) collective-permute-start(bf16[208,1664]{1,0:T(8,128)(2,1)S(1)} %collective-permute-done.2.refs_0_.refs_7_), channel_id=1, source_target_pairs={{0,2},{2,0},{1,3},{3,1},{4,6},{6,4},{5,7},{7,5},{8,10},{10,8},{9,1... | collective-permute-start | bytes 2076680 | tf_op jit(solution)/shard_map/ppermute | solution.py:224
  56.9 4.4 %collective-permute-start.5 = (bf16[208,1664]{1,0:T(8,128)(2,1)}, bf16[208,1664]{1,0:T(8,128)(2,1)S(1)}, u32[]{:S(2)}, u32[]{:S(2)}) collective-permute-start(bf16[208,1664]{1,0:T(8,128)(2,1)} %collective-permute-done.4.refs_2_), channel_id=1, source_target_pairs={{0,2},{2,0},{1,3},{3,1},{4,6},{6,4},{5,7},{7,5},{8,10},{10,8},{9,1... | collective-permute-start | bytes 2076680 | tf_op jit(solution)/shard_map/ppermute | solution.py:224
  69.2 5.0 %collective-permute-start.8 = (bf16[416,1664]{1,0:T(8,128)(2,1)S(1)}, bf16[416,1664]{1,0:T(8,128)(2,1)S(1)}, u32[]{:S(2)}, u32[]{:S(2)}) collective-permute-start(bf16[416,1664]{1,0:T(8,128)(2,1)S(1)} %get-tuple-element.31), channel_id=1, source_target_pairs={{0,2},{2,0},{1,3},{3,1},{4,6},{6,4},{5,7},{7,5},{8,10},{10,8},{9,1... | collective-permute-start | bytes 4153352 | tf_op jit(solution)/shard_map/ppermute | solution.py:224
  71.2 14.8 %collective-permute-start.7 = (bf16[128,1792]{1,0:T(8,128)(2,1)S(1)}, bf16[128,1792]{1,0:T(8,128)(2,1)S(1)}, u32[]{:S(2)}, u32[]{:S(2)}) collective-permute-start(bf16[128,1792]{1,0:T(8,128)(2,1)S(1)} %get-tuple-element.28), channel_id=1, source_target_pairs={{0,4},{4,0},{8,12},{12,8},{1,5},{5,1},{9,13},{13,9},{2,6},{6,2},{1... | collective-permute-start | bytes 1376264 | tf_op jit(solution)/shard_map/ppermute | solution.py:224
  75.2 6.0 %copy-start.2 = (s32[128,2]{0,1:T(2,128)S(1)}, s32[128,2]{0,1:T(2,128)}, u32[]{:S(2)}) copy-start(s32[128,2]{0,1:T(2,128)} %param.10) | copy-start | bytes 3076
  75.2 5.9 %copy-start.3 = (s32[128,2]{0,1:T(2,128)S(1)}, s32[128,2]{0,1:T(2,128)}, u32[]{:S(2)}) copy-start(s32[128,2]{0,1:T(2,128)} %param.11) | copy-start | bytes 3076
  75.2 5.9 %copy-start.4 = (bf16[128,2]{0,1:T(2,128)(2,1)S(1)}, bf16[128,2]{0,1:T(2,128)(2,1)}, u32[]{:S(2)}) copy-start(bf16[128,2]{0,1:T(2,128)(2,1)} %param.9) | copy-start | bytes 1540
  75.3 38.4 %collective-permute-start.9 = (bf16[416,1664]{1,0:T(8,128)(2,1)S(1)}, bf16[416,1664]{1,0:T(8,128)(2,1)S(1)}, u32[]{:S(2)}, u32[]{:S(2)}) collective-permute-start(bf16[416,1664]{1,0:T(8,128)(2,1)S(1)} %shard_map.108.refs_6_.refs_3_), channel_id=1, source_target_pairs={{0,12},{4,8},{8,4},{12,0},{1,13},{5,9},{9,5},{13,1},{2,14},{6,10},... | collective-permute-start | bytes 4153352 | tf_op jit(solution)/shard_map/ppermute | solution.py:224
  79.1 34.9 %collective-permute-start.10 = (bf16[416,1664]{1,0:T(8,128)(2,1)S(1)}, bf16[416,1664]{1,0:T(8,128)(2,1)S(1)}, u32[]{:S(2)}, u32[]{:S(2)}) collective-permute-start(bf16[416,1664]{1,0:T(8,128)(2,1)S(1)} %shard_map.113), channel_id=1, source_target_pairs={{0,2},{2,0},{1,3},{3,1},{4,6},{6,4},{5,7},{7,5},{8,10},{10,8},{9,1... | collective-permute-start | bytes 4153352 | tf_op jit(solution)/shard_map/ppermute | solution.py:224

commit v10 on v9

--- a/solution.py
+++ b/solution.py
@@ -168,6 +168,17 @@
     out[...] = (own[...].astype(F32) + far[...].astype(F32)).astype(BF16)
 
 
+def weight_sum_kernel(own, near, out_in, out_out, sums, sems):
+    copies = []
+    for k, out in enumerate((out_in, out_out)):
+        rows = pl.ds(k * HS, HS)
+        sums[rows, :] = (own[rows, :].astype(F32) + near[rows, :].astype(F32)).astype(BF16)
+        copies.append(pltpu.make_async_copy(sums.at[rows, :], out, sems.at[k]))
+        copies[-1].start()
+    for copy in copies:
+        copy.wait()
+
+
 def pack_back_kernel(i0, i1, out):
     total = (i0[...].astype(F32) + i1[...].astype(F32)).astype(BF16)
     for j in range(BACK_BLOCKS):
@@ -181,17 +192,14 @@
     wide_gates[...] = gates[...].astype(F32)
 
 
-def last_kernel(got, masks, wide_gates, own, near, patch_grad, gate_grad, out_in, out_out, sums, rows, sems):
-    sums[...] = (own[...].astype(F32) + near[...].astype(F32)).astype(BF16)
-    copies = start_copies([(sums.at[pl.ds(0, HS), :], out_in), (sums.at[pl.ds(HS, HS), :], out_out)], sems)
+def unpack_back_kernel(got, masks, wide_gates, patch_grad, gate_grad, token):
+    token[...] = jnp.zeros_like(token)
     for j in range(SEND_BLOCKS):
-        rows[:, pl.ds(j * 128, 128)] = got[:, j].reshape(ROWS, 128)
-    patch_grad[...] = dot_rows(masks[2], rows[...]).astype(BF16)
+        rows = got[:, j].reshape(ROWS, 128)
+        patch_grad[:, pl.ds(j * 128, 128)] = dot_rows(masks[2], rows).astype(BF16)
     gate_block = got[:, SEND_BLOCKS].reshape(ROWS, 128)
     for k in range(2):
         gate_grad[k : k + 1, :] = dot_rows(gate_block, masks[k])[0:1, :] / wide_gates[k : k + 1, :]
-    for copy in copies:
-        copy.wait()
 
 
 def shape(dims, kind=BF16):
@@ -334,16 +342,25 @@
         after=(mine, masks),
     )
     back = lax.all_to_all(back, everywhere, split_axis=0, concat_axis=0, tiled=True)
-    mine = call(partial_sum_kernel, both, (mine, far), 1_000_000, 4_000_000, 16, after=(back,))
-    patch_grad, gate_grad, grad_in, grad_out = call(
-        last_kernel,
-        [shape((T, D)), shape((2, T), F32), shape((HS, D)), shape((HS, D))],
-        (back, masks, wide_gates, mine, near),
+    patch_grad, gate_grad, token = call(
+        unpack_back_kernel,
+        [shape((T, D)), shape((2, T), F32), shape((8, 128), F32)],
+        (back, masks, wide_gates),
         300_000_000,
-        6_000_000,
-        16,
-        out_specs=[VM, VM, HBM, HBM],
-        scratch=[pltpu.VMEM((2 * HS, D), BF16), pltpu.VMEM((ROWS, D), BF16), pltpu.SemaphoreType.DMA((2,))],
+        1_000_000,
+        16,
+    )
+    mine = call(partial_sum_kernel, both, (mine, far), 1_000_000, 4_000_000, 16, after=(token,))
+    grad_in, grad_out = call(
+        weight_sum_kernel,
+        [shape((HS, D))] * 2,
+        (mine, near),
+        1_000_000,
+        4_000_000,
+        16,
+        out_specs=[HBM] * 2,
+        scratch=[pltpu.VMEM((2 * HS, D), BF16), pltpu.SemaphoreType.DMA((2,))],
+        after=(token,),
     )
     return patch_grad, gate_grad.T, grad_in[None], grad_out[None]
 

time: 118 us -> 117 us (level)
    pallas_call x13 -> x14, Pallas kernels: 17.2 us -> 16.7 us  [call(): pl.pallas_call(body, out_shape=out_shape, in_specs=(in_specs or [VM] * us...]
  transfers between devices with their start and end apart: 12 -> 12, of which waited for: 5 -> 5; matrix products, arithmetic and copies ran while one was open for 0% -> 0% of each run, Pallas kernels for 8% -> 9%
where the time goes in v10:
time: 117 us
  starting transfers between devices  44.6 us (38%)
  blocking collectives  27.4 us (23%)
  waiting for transfers between devices  26.8 us (23%)
  Pallas kernels  16.7 us (14%)
    ppermute x11, starting transfers between devices, swap(): lax.ppermute(value, axis, [(i, partner(i)) for i in range(lax.axis_size(a...  28 us
    all_to_all x1, blocking collectives, local(): lax.all_to_all(back, everywhere, split_axis=0, concat_axis=0, tiled=True)  27.4 us
    all_to_all x1, waiting for transfers between devices, local(): lax.all_to_all(sent, everywhere, split_axis=0, concat_axis=0, tiled=True)  20 us
    pallas_call x14, Pallas kernels, call(): pl.pallas_call(body, out_shape=out_shape, in_specs=(in_specs or [VM] * us...  16.7 us
    all_to_all x1, starting transfers between devices, local(): lax.all_to_all(sent, everywhere, split_axis=0, concat_axis=0, tiled=True)  16.6 us
    ppermute x11, waiting for transfers between devices, swap(): lax.ppermute(value, axis, [(i, partner(i)) for i in range(lax.axis_size(a...  6.82 us
  transfers between devices with their start and end apart: 12, of which 5 were waited for; matrix products, arithmetic and copies ran while one was open for 0% of the time, Pallas kernels for 9%

profile of v10, /device:TPU:6, one launch (start us, length us, event | category | flops | bytes accessed | tf_op | source)
XLA Modules:
  0.0 116.6 jit_solution(8334093406013700119)
XLA Ops:
  0.6 0.0 copy-start
  0.6 0.0 copy-start.1
  0.7 2.8 %shard_map.102 = bf16[64,13,4,128]{3,2,1,0:T(4,128)(2,1)} custom-call(bf16[2,128]{1,0:T(2,128)(2,1)} %bitcast.20, s32[2,128]{1,0:T(2,128)} %bitcast.16, s32[2,128]{1,0:T(2,128)} %bitcast.18, bf16[128,1664]{1,0:T(8,128)(2,1)} %refs_3_.1, bf16[128,1664]{1,0:T(8,128)(2,1)} %refs_4_.1), custom_call_target="tpu_custom_call" | custom-call | flops 500000000 | bytes 5000000 | tf_op jit(solution)/shard_map/pallas_call | solution.py:220
  3.4 16.6 %all-to-all-start = ((bf16[64,13,4,128]{3,2,1,0:T(4,128)(2,1)}), bf16[64,13,4,128]{3,2,1,0:T(4,128)(2,1)S(1)}, u32[]{:S(2)}, u32[]{:S(2)}) async-start(bf16[64,13,4,128]{3,2,1,0:T(4,128)(2,1)} %shard_map.102), calls=%async_computation | async-start | bytes 1703936 | tf_op jit(solution)/shard_map/all_to_all | solution.py:274
  20.0 0.0 copy-done
  20.0 2.4 %collective-permute-start.2 = (bf16[208,1664]{1,0:T(8,128)(2,1)S(1)}, bf16[208,1664]{1,0:T(8,128)(2,1)S(1)}, u32[]{:S(2)}, u32[]{:S(2)}) collective-permute-start(bf16[208,1664]{1,0:T(8,128)(2,1)S(1)} %bitcast.8), channel_id=1, source_target_pairs={{0,12},{4,8},{8,4},{12,0},{1,13},{5,9},{9,5},{13,1},{2,14},{6,10},... | collective-permute-start | bytes 2076680 | tf_op jit(solution)/shard_map/ppermute | solution.py:232
  22.4 0.0 copy-done.1
  22.4 4.7 %collective-permute-start.4 = (bf16[208,1664]{1,0:T(8,128)(2,1)S(1)}, bf16[208,1664]{1,0:T(8,128)(2,1)}, u32[]{:S(2)}, u32[]{:S(2)}) collective-permute-start(bf16[208,1664]{1,0:T(8,128)(2,1)S(1)} %bitcast.13), channel_id=1, source_target_pairs={{0,12},{4,8},{8,4},{12,0},{1,13},{5,9},{9,5},{13,1},{2,14},{6,10},... | collective-permute-start | bytes 2076680 | tf_op jit(solution)/shard_map/ppermute | solution.py:232
  27.1 20.0 %all-to-all-done.refs_0_ = bf16[64,13,4,128]{3,2,1,0:T(4,128)(2,1)S(1)} async-done(((bf16[64,13,4,128]{3,2,1,0:T(4,128)(2,1)}), bf16[64,13,4,128]{3,2,1,0:T(4,128)(2,1)S(1)}, u32[]{:S(2)}, u32[]{:S(2)}) %all-to-all-start) | async-done | bytes 852000 | tf_op jit(solution)/shard_map/all_to_all | solution.py:274
  47.1 0.7 shard_map.103.refs_0_.refs_9_
  47.8 2.7 %collective-permute-start.6 = (bf16[256,1664]{1,0:T(8,128)(2,1)S(1)}, bf16[256,1664]{1,0:T(8,128)(2,1)S(1)}, u32[]{:S(2)}, u32[]{:S(2)}) collective-permute-start(bf16[256,1664]{1,0:T(8,128)(2,1)S(1)} %shard_map.103.refs_0_.refs_9_), channel_id=1, source_target_pairs={{0,4},{4,0},{8,12},{12,8},{1,5},{5,1},{9,13},{13,9},{2,6},{6,2},{1... | collective-permute-start | bytes 2555912 | tf_op jit(solution)/shard_map/ppermute | solution.py:232
  50.6 1.9 %collective-permute-start = (bf16[208,1664]{1,0:T(8,128)(2,1)S(1)}, bf16[208,1664]{1,0:T(8,128)(2,1)S(1)}, u32[]{:S(2)}, u32[]{:S(2)}) collective-permute-start(bf16[208,1664]{1,0:T(8,128)(2,1)S(1)} %bitcast.9), channel_id=1, source_target_pairs={{0,2},{2,0},{1,3},{3,1},{4,6},{6,4},{5,7},{7,5},{8,10},{10,8},{9,1... | collective-permute-start | bytes 2076680 | tf_op jit(solution)/shard_map/ppermute | solution.py:232
  52.5 2.4 %collective-permute-start.1 = (bf16[208,1664]{1,0:T(8,128)(2,1)S(1)}, bf16[208,1664]{1,0:T(8,128)(2,1)S(1)}, u32[]{:S(2)}, u32[]{:S(2)}) collective-permute-start(bf16[208,1664]{1,0:T(8,128)(2,1)S(1)} %bitcast.14), channel_id=1, source_target_pairs={{0,2},{2,0},{1,3},{3,1},{4,6},{6,4},{5,7},{7,5},{8,10},{10,8},{9,1... | collective-permute-start | bytes 2076680 | tf_op jit(solution)/shard_map/ppermute | solution.py:232
  54.9 0.0 collective-permute-done.2.refs_0_.refs_7_
  54.9 1.9 %collective-permute-start.3 = (bf16[208,1664]{1,0:T(8,128)(2,1)S(1)}, bf16[208,1664]{1,0:T(8,128)(2,1)S(1)}, u32[]{:S(2)}, u32[]{:S(2)}) collective-permute-start(bf16[208,1664]{1,0:T(8,128)(2,1)S(1)} %collective-permute-done.2.refs_0_.refs_7_), channel_id=1, source_target_pairs={{0,2},{2,0},{1,3},{3,1},{4,6},{6,4},{5,7},{7,5},{8,10},{10,8},{9,1... | collective-permute-start | bytes 2076680 | tf_op jit(solution)/shard_map/ppermute | solution.py:232
  56.9 0.0 collective-permute-done.4.refs_2_
  56.9 2.4 %collective-permute-start.5 = (bf16[208,1664]{1,0:T(8,128)(2,1)}, bf16[208,1664]{1,0:T(8,128)(2,1)S(1)}, u32[]{:S(2)}, u32[]{:S(2)}) collective-permute-start(bf16[208,1664]{1,0:T(8,128)(2,1)} %collective-permute-done.4.refs_2_), channel_id=1, source_target_pairs={{0,2},{2,0},{1,3},{3,1},{4,6},{6,4},{5,7},{7,5},{8,10},{10,8},{9,1... | collective-permute-start | bytes 2076680 | tf_op jit(solution)/shard_map/ppermute | solution.py:232
  59.3 0.0 collective-permute-done.refs_1_.refs_6_
  59.3 0.0 collective-permute-done.1.refs_3_
  59.3 1.0 shard_map.104
  60.3 0.0 collective-permute-done.3.refs_1_.refs_8_
  60.3 0.9 collective-permute-done.5.refs_3_
  61.3 2.1 %shard_map.105 = (bf16[1664,512]{1,0:T(8,128)(2,1)S(1)}, bf16[1664,512]{1,0:T(8,128)(2,1)S(1)}) custom-call(bf16[208,1664]{1,0:T(8,128)(2,1)S(1)} %collective-permute-done.2.refs_0_.refs_7_, bf16[208,1664]{1,0:T(8,128)(2,1)S(1)} %collective-permute-done.3.refs_1_.refs_8_, bf16[208,1664]{1,0:T(8,128)(2,1)} %collective-permute-done.4.refs_2_, ...), custom_call_target="tpu_custom_call" | custom-call | flops 1000000 | bytes 5000000 | tf_op jit(solution)/shard_map/pallas_call | solution.py:220
  63.4 1.7 %shard_map.106 = (bf16[128,1792]{1,0:T(8,128)(2,1)S(1)}, bf16[4,128,208]{2,1,0:T(8,128)(2,1)S(1)}, bf16[4,128,208]{2,1,0:T(8,128)(2,1)S(1)}) custom-call(bf16[256,1664]{1,0:T(8,128)(2,1)S(1)} %shard_map.103.refs_0_.refs_9_, bf16[1664,512]{1,0:T(8,128)(2,1)S(1)} %get-tuple-element.22.refs_1_, bf16[1664,512]{1,0:T(8,128)(2,1)S(1)} %get-tuple-element.23.refs_2_, ...), custom_call_target="tpu_custom_call" | custom-call | flops 1100000000 | bytes 8000000 | tf_op jit(solution)/shard_map/pallas_call | solution.py:220
  65.1 1.7 %collective-permute-done.6.refs_0_.refs_1_ = bf16[256,1664]{1,0:T(8,128)(2,1)S(1)} collective-permute-done((bf16[256,1664]{1,0:T(8,128)(2,1)S(1)}, bf16[256,1664]{1,0:T(8,128)(2,1)S(1)}, u32[]{:S(2)}, u32[]{:S(2)}) %collective-permute-start.6) | collective-permute-done | bytes 852000 | tf_op jit(solution)/shard_map/ppermute | solution.py:232
  66.8 2.5 %shard_map.107 = (bf16[128,1792]{1,0:T(8,128)(2,1)S(1)}, bf16[4,128,208]{2,1,0:T(8,128)(2,1)S(1)}, bf16[4,128,208]{2,1,0:T(8,128)(2,1)S(1)}, bf16[416,1664]{1,0:T(8,128)(2,1)S(1)}) custom-call(bf16[256,1664]{1,0:T(8,128)(2,1)S(1)} %collective-permute-done.6.refs_0_.refs_1_, bf16[1664,512]{1,0:T(8,128)(2,1)S(1)} %get-tuple-element.22.refs_1_, ...), custom_call_target="tpu_custom_call" | custom-call | flops 1500000000 | bytes 10000000 | tf_op jit(solution)/shard_map/pallas_call | solution.py:220
  69.3 1.9 %collective-permute-start.8 = (bf16[416,1664]{1,0:T(8,128)(2,1)S(1)}, bf16[416,1664]{1,0:T(8,128)(2,1)S(1)}, u32[]{:S(2)}, u32[]{:S(2)}) collective-permute-start(bf16[416,1664]{1,0:T(8,128)(2,1)S(1)} %get-tuple-element.32), channel_id=1, source_target_pairs={{0,2},{2,0},{1,3},{3,1},{4,6},{6,4},{5,7},{7,5},{8,10},{10,8},{9,1... | collective-permute-start | bytes 4153352 | tf_op jit(solution)/shard_map/ppermute | solution.py:232
  71.2 2.7 %collective-permute-start.7 = (bf16[128,1792]{1,0:T(8,128)(2,1)S(1)}, bf16[128,1792]{1,0:T(8,128)(2,1)S(1)}, u32[]{:S(2)}, u32[]{:S(2)}) collective-permute-start(bf16[128,1792]{1,0:T(8,128)(2,1)S(1)} %get-tuple-element.29), channel_id=1, source_target_pairs={{0,4},{4,0},{8,12},{12,8},{1,5},{5,1},{9,13},{13,9},{2,6},{6,2},{1... | collective-permute-start | bytes 1376264 | tf_op jit(solution)/shard_map/ppermute | solution.py:232
  73.9 0.4 collective-permute-done.8.refs_6_
  74.3 1.0 shard_map.108.refs_6_.refs_3_
  75.3 0.0 copy-start.2
  75.3 0.0 copy-start.3
  75.3 0.0 copy-start.4
  75.3 2.8 %collective-permute-start.9 = (bf16[416,1664]{1,0:T(8,128)(2,1)S(1)}, bf16[416,1664]{1,0:T(8,128)(2,1)S(1)}, u32[]{:S(2)}, u32[]{:S(2)}) collective-permute-start(bf16[416,1664]{1,0:T(8,128)(2,1)S(1)} %shard_map.108.refs_6_.refs_3_), channel_id=1, source_target_pairs={{0,12},{4,8},{8,4},{12,0},{1,13},{5,9},{9,5},{13,1},{2,14},{6,10},... | collective-permute-start | bytes 4153352 | tf_op jit(solution)/shard_map/ppermute | solution.py:232
  78.1 1.0 shard_map.114
  79.1 2.1 %collective-permute-start.10 = (bf16[416,1664]{1,0:T(8,128)(2,1)S(1)}, bf16[416,1664]{1,0:T(8,128)(2,1)S(1)}, u32[]{:S(2)}, u32[]{:S(2)}) collective-permute-start(bf16[416,1664]{1,0:T(8,128)(2,1)S(1)} %shard_map.114), channel_id=1, source_target_pairs={{0,2},{2,0},{1,3},{3,1},{4,6},{6,4},{5,7},{7,5},{8,10},{10,8},{9,1... | collective-permute-start | bytes 4153352 | tf_op jit(solution)/shard_map/ppermute | solution.py:232
  81.2 0.0 copy-done.2
  81.2 0.0 copy-done.3
  81.2 0.0 copy-done.4
  81.3 1.0 shard_map.109.refs_2_.refs_0_
  82.2 3.8 %collective-permute-done.7.refs_1_ = bf16[128,1792]{1,0:T(8,128)(2,1)S(1)} collective-permute-done((bf16[128,1792]{1,0:T(8,128)(2,1)S(1)}, bf16[128,1792]{1,0:T(8,128)(2,1)S(1)}, u32[]{:S(2)}, u32[]{:S(2)}) %collective-permute-start.7) | collective-permute-done | bytes 458784 | tf_op jit(solution)/shard_map/ppermute | solution.py:232
  86.0 0.3 shard_map.111
  86.3 27.4 %all_to_all.10.refs_0_ = bf16[64,14,2,128]{3,2,1,0:T(2,128)(2,1)S(1)} all-to-all(bf16[64,14,2,128]{3,2,1,0:T(2,128)(2,1)S(1)} %shard_map.111), channel_id=1, replica_groups=mesh['zlo'=4,'y'=8,'x'=4,'core'=2,'zhi'=2] {'zlo','y','zhi'}, dimensions={0} | all-to-all | bytes 917504 | tf_op jit(solution)/shard_map/all_to_all | solution.py:344
  113.7 1.2 %shard_map.112 = (bf16[128,1664]{1,0:T(8,128)(2,1)}, f32[2,128]{1,0:T(2,128)}, f32[8,128]{1,0:T(8,128)S(1)}) custom-call(bf16[64,14,2,128]{3,2,1,0:T(2,128)(2,1)S(1)} %all_to_all.10.refs_0_, bf16[3,128,128]{2,1,0:T(8,128)(2,1)S(1)} %get-tuple-element.33.refs_3_.refs_1_, f32[2,128]{1,0:T(2,128)S(1)} %get-tuple-element.34.refs_2_), custom_call_target="tpu_custom_call" | custom-call | flops 300000000 | bytes 1000000 | tf_op jit(solution)/shard_map/pallas_call | solution.py:220
  114.9 0.0 collective-permute-done.9.refs_1_
  114.9 0.3 shard_map.113.refs_0_
  115.2 0.0 collective-permute-done.10.refs_1_
  115.2 1.3 %shard_map.115 = (bf16[208,1664]{1,0:T(8,128)(2,1)}, bf16[208,1664]{1,0:T(8,128)(2,1)}) custom-call(bf16[416,1664]{1,0:T(8,128)(2,1)S(1)} %shard_map.113.refs_0_, bf16[416,1664]{1,0:T(8,128)(2,1)S(1)} %collective-permute-done.10.refs_1_, f32[8,128]{1,0:T(8,128)S(1)} %get-tuple-element.37.refs_2_), custom_call_target="tpu_custom_call" | custom-call | flops 1000000 | bytes 4000000 | tf_op jit(solution)/shard_map/pallas_call | solution.py:220
  (1 shorter events, 0.0 us)
Async XLA Ops:
  0.6 19.4 %copy-start = (bf16[1,208,1664]{2,1,0:T(8,128)(2,1)S(1)}, bf16[1,208,1664]{2,1,0:T(8,128)(2,1)}, u32[]{:S(2)}) copy-start(bf16[1,208,1664]{2,1,0:T(8,128)(2,1)} %param.12) | copy-start | bytes 2076676
  0.6 21.8 %copy-start.1 = (bf16[1,208,1664]{2,1,0:T(8,128)(2,1)S(1)}, bf16[1,208,1664]{2,1,0:T(8,128)(2,1)}, u32[]{:S(2)}) copy-start(bf16[1,208,1664]{2,1,0:T(8,128)(2,1)} %param.13) | copy-start | bytes 2076676
  3.4 43.7 %all-to-all-start = ((bf16[64,13,4,128]{3,2,1,0:T(4,128)(2,1)}), bf16[64,13,4,128]{3,2,1,0:T(4,128)(2,1)S(1)}, u32[]{:S(2)}, u32[]{:S(2)}) async-start(bf16[64,13,4,128]{3,2,1,0:T(4,128)(2,1)} %shard_map.102), calls=%async_computation | async-start | bytes 1703936 | tf_op jit(solution)/shard_map/all_to_all | solution.py:274
  20.0 34.9 %collective-permute-start.2 = (bf16[208,1664]{1,0:T(8,128)(2,1)S(1)}, bf16[208,1664]{1,0:T(8,128)(2,1)S(1)}, u32[]{:S(2)}, u32[]{:S(2)}) collective-permute-start(bf16[208,1664]{1,0:T(8,128)(2,1)S(1)} %bitcast.8), channel_id=1, source_target_pairs={{0,12},{4,8},{8,4},{12,0},{1,13},{5,9},{9,5},{13,1},{2,14},{6,10},... | collective-permute-start | bytes 2076680 | tf_op jit(solution)/shard_map/ppermute | solution.py:232
  22.4 34.4 %collective-permute-start.4 = (bf16[208,1664]{1,0:T(8,128)(2,1)S(1)}, bf16[208,1664]{1,0:T(8,128)(2,1)}, u32[]{:S(2)}, u32[]{:S(2)}) collective-permute-start(bf16[208,1664]{1,0:T(8,128)(2,1)S(1)} %bitcast.13), channel_id=1, source_target_pairs={{0,12},{4,8},{8,4},{12,0},{1,13},{5,9},{9,5},{13,1},{2,14},{6,10},... | collective-permute-start | bytes 2076680 | tf_op jit(solution)/shard_map/ppermute | solution.py:232
  47.8 18.9 %collective-permute-start.6 = (bf16[256,1664]{1,0:T(8,128)(2,1)S(1)}, bf16[256,1664]{1,0:T(8,128)(2,1)S(1)}, u32[]{:S(2)}, u32[]{:S(2)}) collective-permute-start(bf16[256,1664]{1,0:T(8,128)(2,1)S(1)} %shard_map.103.refs_0_.refs_9_), channel_id=1, source_target_pairs={{0,4},{4,0},{8,12},{12,8},{1,5},{5,1},{9,13},{13,9},{2,6},{6,2},{1... | collective-permute-start | bytes 2555912 | tf_op jit(solution)/shard_map/ppermute | solution.py:232
  50.6 8.7 %collective-permute-start = (bf16[208,1664]{1,0:T(8,128)(2,1)S(1)}, bf16[208,1664]{1,0:T(8,128)(2,1)S(1)}, u32[]{:S(2)}, u32[]{:S(2)}) collective-permute-start(bf16[208,1664]{1,0:T(8,128)(2,1)S(1)} %bitcast.9), channel_id=1, source_target_pairs={{0,2},{2,0},{1,3},{3,1},{4,6},{6,4},{5,7},{7,5},{8,10},{10,8},{9,1... | collective-permute-start | bytes 2076680 | tf_op jit(solution)/shard_map/ppermute | solution.py:232
  52.5 6.8 %collective-permute-start.1 = (bf16[208,1664]{1,0:T(8,128)(2,1)S(1)}, bf16[208,1664]{1,0:T(8,128)(2,1)S(1)}, u32[]{:S(2)}, u32[]{:S(2)}) collective-permute-start(bf16[208,1664]{1,0:T(8,128)(2,1)S(1)} %bitcast.14), channel_id=1, source_target_pairs={{0,2},{2,0},{1,3},{3,1},{4,6},{6,4},{5,7},{7,5},{8,10},{10,8},{9,1... | collective-permute-start | bytes 2076680 | tf_op jit(solution)/shard_map/ppermute | solution.py:232
  54.9 5.4 %collective-permute-start.3 = (bf16[208,1664]{1,0:T(8,128)(2,1)S(1)}, bf16[208,1664]{1,0:T(8,128)(2,1)S(1)}, u32[]{:S(2)}, u32[]{:S(2)}) collective-permute-start(bf16[208,1664]{1,0:T(8,128)(2,1)S(1)} %collective-permute-done.2.refs_0_.refs_7_), channel_id=1, source_target_pairs={{0,2},{2,0},{1,3},{3,1},{4,6},{6,4},{5,7},{7,5},{8,10},{10,8},{9,1... | collective-permute-start | bytes 2076680 | tf_op jit(solution)/shard_map/ppermute | solution.py:232
  56.9 4.4 %collective-permute-start.5 = (bf16[208,1664]{1,0:T(8,128)(2,1)}, bf16[208,1664]{1,0:T(8,128)(2,1)S(1)}, u32[]{:S(2)}, u32[]{:S(2)}) collective-permute-start(bf16[208,1664]{1,0:T(8,128)(2,1)} %collective-permute-done.4.refs_2_), channel_id=1, source_target_pairs={{0,2},{2,0},{1,3},{3,1},{4,6},{6,4},{5,7},{7,5},{8,10},{10,8},{9,1... | collective-permute-start | bytes 2076680 | tf_op jit(solution)/shard_map/ppermute | solution.py:232
  69.3 5.0 %collective-permute-start.8 = (bf16[416,1664]{1,0:T(8,128)(2,1)S(1)}, bf16[416,1664]{1,0:T(8,128)(2,1)S(1)}, u32[]{:S(2)}, u32[]{:S(2)}) collective-permute-start(bf16[416,1664]{1,0:T(8,128)(2,1)S(1)} %get-tuple-element.32), channel_id=1, source_target_pairs={{0,2},{2,0},{1,3},{3,1},{4,6},{6,4},{5,7},{7,5},{8,10},{10,8},{9,1... | collective-permute-start | bytes 4153352 | tf_op jit(solution)/shard_map/ppermute | solution.py:232
  71.2 14.8 %collective-permute-start.7 = (bf16[128,1792]{1,0:T(8,128)(2,1)S(1)}, bf16[128,1792]{1,0:T(8,128)(2,1)S(1)}, u32[]{:S(2)}, u32[]{:S(2)}) collective-permute-start(bf16[128,1792]{1,0:T(8,128)(2,1)S(1)} %get-tuple-element.29), channel_id=1, source_target_pairs={{0,4},{4,0},{8,12},{12,8},{1,5},{5,1},{9,13},{13,9},{2,6},{6,2},{1... | collective-permute-start | bytes 1376264 | tf_op jit(solution)/shard_map/ppermute | solution.py:232
  75.3 5.9 %copy-start.2 = (s32[128,2]{0,1:T(2,128)S(1)}, s32[128,2]{0,1:T(2,128)}, u32[]{:S(2)}) copy-start(s32[128,2]{0,1:T(2,128)} %param.10) | copy-start | bytes 3076
  75.3 5.9 %copy-start.3 = (s32[128,2]{0,1:T(2,128)S(1)}, s32[128,2]{0,1:T(2,128)}, u32[]{:S(2)}) copy-start(s32[128,2]{0,1:T(2,128)} %param.11) | copy-start | bytes 3076
  75.3 5.9 %copy-start.4 = (bf16[128,2]{0,1:T(2,128)(2,1)S(1)}, bf16[128,2]{0,1:T(2,128)(2,1)}, u32[]{:S(2)}) copy-start(bf16[128,2]{0,1:T(2,128)(2,1)} %param.9) | copy-start | bytes 1540
  75.3 39.6 %collective-permute-start.9 = (bf16[416,1664]{1,0:T(8,128)(2,1)S(1)}, bf16[416,1664]{1,0:T(8,128)(2,1)S(1)}, u32[]{:S(2)}, u32[]{:S(2)}) collective-permute-start(bf16[416,1664]{1,0:T(8,128)(2,1)S(1)} %shard_map.108.refs_6_.refs_3_), channel_id=1, source_target_pairs={{0,12},{4,8},{8,4},{12,0},{1,13},{5,9},{9,5},{13,1},{2,14},{6,10},... | collective-permute-start | bytes 4153352 | tf_op jit(solution)/shard_map/ppermute | solution.py:232
  79.1 36.1 %collective-permute-start.10 = (bf16[416,1664]{1,0:T(8,128)(2,1)S(1)}, bf16[416,1664]{1,0:T(8,128)(2,1)S(1)}, u32[]{:S(2)}, u32[]{:S(2)}) collective-permute-start(bf16[416,1664]{1,0:T(8,128)(2,1)S(1)} %shard_map.114), channel_id=1, source_target_pairs={{0,2},{2,0},{1,3},{3,1},{4,6},{6,4},{5,7},{7,5},{8,10},{10,8},{9,1... | collective-permute-start | bytes 4153352 | tf_op jit(solution)/shard_map/ppermute | solution.py:232
